TPU v7x, 32 devices: a whole 2x2x4 slice. The times are simulated.
32 devices in a mesh: dp: 8 (over z, x), tensor: 4 (over y, core).
Axes of the slice: x: 2, y: 2, z: 4, core: 2. Of those that a mesh axis runs over, the one named last changes fastest.
Arguments:
- inputs: bfloat16 [8192, 768], P('dp'), may hold values from -6 to 6
- encoded: bfloat16 [32768, 768], P('dp'), may hold values from -6 to 6
- example_counts: int32 [8], P('dp'), may hold values from 4 to 8, as said below
- lengths: int32 [64], P('dp'), may hold values from 57 to 114, as said below
- buckets: int32 [128], replicated, may hold values from 0 to 31, as said below
- gain_self: float32 [768], replicated, may hold values from 0.1 to 1.9
- gain_cross: float32 [768], replicated, may hold values from 0.1 to 1.9
- gain_ffn: float32 [768], replicated, may hold values from 0.1 to 1.9
- bias_table: float32 [32, 12], P(None, 'tensor'), may hold values from -4 to 4
- query_self: bfloat16 [768, 768], P(None, 'tensor'), may hold values from -0.0546875 to 0.0546875
- key_self: bfloat16 [768, 768], P(None, 'tensor'), may hold values from -0.21875 to 0.21875
- value_self: bfloat16 [768, 768], P(None, 'tensor'), may hold values from -0.21875 to 0.21875
- output_self: bfloat16 [768, 768], P(None, 'tensor'), may hold values from -0.625 to 0.625
- query_cross: bfloat16 [768, 768], P(None, 'tensor'), may hold values from -0.0546875 to 0.0546875
- key_cross: bfloat16 [768, 768], P(None, 'tensor'), may hold values from -0.21875 to 0.21875
- value_cross: bfloat16 [768, 768], P(None, 'tensor'), may hold values from -0.21875 to 0.21875
- output_cross: bfloat16 [768, 768], P(None, 'tensor'), may hold values from -0.875 to 0.875
- hidden_in: bfloat16 [768, 3072], P(None, 'tensor'), may hold values from -0.21875 to 0.21875
- hidden_out: bfloat16 [768, 3072], P(None, 'tensor'), may hold values from -0.15625 to 0.15625
- out_grad: bfloat16 [8192, 768], P('dp'), may hold values from -6 to 6
Outputs:
- layer_out: bfloat16 [8192, 768], P('dp', 'tensor')
- input_grad: bfloat16 [8192, 768], P('dp', 'tensor')
- encoded_grad: bfloat16 [32768, 768], P(('dp', 'tensor'))
- grad_gain_self: float32 [768], replicated
- grad_gain_cross: float32 [768], replicated
- grad_gain_ffn: float32 [768], replicated
- grad_bias_table: float32 [32, 12], P(None, 'tensor')
- grad_query_self: float32 [768, 768], P('dp', 'tensor')
- grad_key_self: float32 [768, 768], P('dp', 'tensor')
- grad_value_self: float32 [768, 768], P('dp', 'tensor')
- grad_output_self: float32 [768, 768], P('dp', 'tensor')
- grad_query_cross: float32 [768, 768], P('dp', 'tensor')
- grad_key_cross: float32 [768, 768], P('dp', 'tensor')
- grad_value_cross: float32 [768, 768], P('dp', 'tensor')
- grad_output_cross: float32 [768, 768], P('dp', 'tensor')
- grad_hidden_in: float32 [768, 3072], P('dp', 'tensor')
- grad_hidden_out: float32 [768, 3072], P('dp', 'tensor')
Inputs may be any that keep to these rules, and one draw needn't show every extreme that they name: `example_counts`: every shard of dp has at least 4 live slots, its lowest ones; some shard has all 8. `lengths`: some slot has length 114. buckets[0] = 0 and the buckets never fall with distance; the largest is 31.
All inputs are finite; a program needn't handle non-finite values.
Results may differ from a plain program's by a relative error of at most 0.028.
The roundings to bfloat16 on the way count: a program that leaves them out, or rounds other values in their place, can miss the bound.
Values may be sent and summed in bfloat16 or wider, within the bound.
A program may use at most 192 MiB of HBM per device.

v0:
```python
import jax
import jax.numpy as jnp
from jax import lax
from jax.sharding import PartitionSpec as P

HD = 64
GROUP = 4


norm_epsilon = 1e-06
masked_score = -1e30
highest = lax.Precision.HIGHEST


def dot_plain(left, right):
    return jnp.dot(left, right, preferred_element_type=jnp.float32)


def dot_trans(left, right):
    return lax.dot_general(
        left, right, (((1,), (1,)), ((), ())), preferred_element_type=jnp.float32
    )


def trans_dot(left, right):
    return lax.dot_general(
        left, right, (((0,), (0,)), ((), ())), preferred_element_type=jnp.float32
    )


def rms_forward(row_data, gain):
    inverse = lax.rsqrt(jnp.mean(row_data * row_data, axis=-1, keepdims=True) + norm_epsilon)
    return (inverse, (row_data * inverse * gain).astype(jnp.bfloat16))


def rms_backward(row_data, inverse, gain, grad_normed):
    scaled = gain * grad_normed
    inner = jnp.mean(scaled * row_data, axis=-1, keepdims=True)
    grad_rows = inverse * scaled - row_data * (inverse * inverse * inverse) * inner
    grad_gain = jnp.sum(grad_normed * row_data * inverse, axis=0)
    return (grad_rows, grad_gain)


def attend_forward(query, key_rows, value_rows, score_bias):
    scores = (
        jnp.einsum("gihd,gjhd->ghij", query, key_rows, preferred_element_type=jnp.float32)
        + score_bias
    )
    row_max = jnp.max(scores, axis=-1, keepdims=True)
    exp_terms = jnp.exp(scores - row_max)
    row_total = jnp.sum(exp_terms, axis=-1, keepdims=True)
    soft = (exp_terms / row_total).astype(jnp.bfloat16)
    mixed = jnp.einsum("ghij,gjhd->gihd", soft, value_rows, preferred_element_type=jnp.float32)
    return (mixed.astype(jnp.bfloat16), (row_max + jnp.log(row_total))[..., 0])


def attend_backward(query, key_rows, value_rows, score_bias, log_total, grad_mixed, keep_table):
    scores = (
        jnp.einsum("gihd,gjhd->ghij", query, key_rows, preferred_element_type=jnp.float32)
        + score_bias
    )
    soft = jnp.exp(scores - log_total[..., None])
    grad_soft = jnp.einsum(
        "gihd,gjhd->ghij", grad_mixed, value_rows, preferred_element_type=jnp.float32
    )
    grad_value = jnp.einsum(
        "ghij,gihd->gjhd", soft.astype(jnp.bfloat16), grad_mixed, preferred_element_type=jnp.float32
    ).astype(jnp.bfloat16)
    inner = jnp.sum(soft * grad_soft, axis=-1, keepdims=True)
    grad_scores = (soft * (grad_soft - inner)).astype(jnp.bfloat16)
    grad_query = jnp.einsum(
        "ghij,gjhd->gihd", grad_scores, key_rows, preferred_element_type=jnp.float32
    ).astype(jnp.bfloat16)
    grad_key = jnp.einsum(
        "ghij,gihd->gjhd", grad_scores, query, preferred_element_type=jnp.float32
    ).astype(jnp.bfloat16)
    if keep_table:
        return (grad_query, grad_key, grad_value, jnp.sum(grad_scores.astype(jnp.float32), axis=0))
    return (grad_query, grad_key, grad_value)


def branch_total(term):
    return lax.psum(term, "tensor")


def norm_total(term):
    return lax.psum(term.astype(jnp.bfloat16), "tensor").astype(jnp.float32)


def per_device(
    inputs,
    encoded,
    example_counts,
    lengths,
    buckets,
    gain_self,
    gain_cross,
    gain_ffn,
    bias_table,
    query_self,
    key_self,
    value_self,
    output_self,
    query_cross,
    key_cross,
    value_cross,
    output_cross,
    hidden_in,
    hidden_out,
    out_grad,
):
    model_width = inputs.shape[1]
    seq_len = buckets.shape[0]
    slot_count = lengths.shape[0]
    enc_len = encoded.shape[0] // slot_count
    heads_local = query_self.shape[1] // HD
    block_count = slot_count // GROUP
    positions = jnp.arange(seq_len)
    live = jnp.arange(slot_count) < example_counts[0]
    valid_rows = (
        ((positions[None, :] < lengths[:, None]) & live[:, None]).astype(jnp.float32).reshape(-1, 1)
    )
    row_data = inputs.astype(jnp.float32)
    group_count = lax.axis_size("tensor")

    def forward_sum(term):
        return branch_total(term)

    def backward_sum(term):
        return norm_total(term)

    distance = jnp.maximum(positions[:, None] - positions[None, :], 0)
    dist_table = (distance[:, :, None] == positions[None, None, :]).astype(jnp.float32)
    bucket_table = (buckets[:, None] == jnp.arange(bias_table.shape[0])[None, :]).astype(
        jnp.float32
    )
    per_dist = jnp.dot(bucket_table, bias_table, precision=highest)
    causal = positions[:, None] >= positions[None, :]
    self_bias = jnp.where(
        causal[None],
        jnp.einsum("ijd,dh->hij", dist_table, per_dist, precision=highest),
        masked_score,
    )

    def to_blocks(flat, length):
        return flat.reshape(block_count, GROUP, length, heads_local, HD)

    def run_forward(query, key_rows, value_rows, score_bias, key_len):
        shaped = (
            to_blocks(query, seq_len),
            to_blocks(key_rows, key_len),
            to_blocks(value_rows, key_len),
        )
        mixed, log_total = lax.map(
            lambda packed: attend_forward(packed[0], packed[1], packed[2], score_bias), shaped
        )
        return (mixed.reshape(query.shape), log_total)

    def run_backward(
        query, key_rows, value_rows, score_bias, key_len, log_total, grad_mixed, keep_table
    ):
        shaped = (
            to_blocks(query, seq_len),
            to_blocks(key_rows, key_len),
            to_blocks(value_rows, key_len),
            log_total,
            to_blocks(grad_mixed, seq_len),
        )
        results = lax.map(
            lambda packed: attend_backward(
                packed[0], packed[1], packed[2], score_bias, packed[3], packed[4], keep_table
            ),
            shaped,
        )
        grads = (
            results[0].reshape(query.shape),
            results[1].reshape(key_rows.shape),
            results[2].reshape(value_rows.shape),
        )
        if keep_table:
            return grads + (jnp.sum(results[3], axis=0),)
        return grads

    scale_one, normed_self = rms_forward(row_data, gain_self)
    query = dot_plain(normed_self, query_self).astype(jnp.bfloat16)
    key_rows = dot_plain(normed_self, key_self).astype(jnp.bfloat16)
    value_rows = dot_plain(normed_self, value_self).astype(jnp.bfloat16)
    mixed_self, log_self = run_forward(query, key_rows, value_rows, self_bias, seq_len)
    hidden_one = row_data + forward_sum(dot_trans(mixed_self, output_self))
    scale_two, normed_share_two = rms_forward(hidden_one, gain_cross)
    cross_query = dot_plain(normed_share_two, query_cross).astype(jnp.bfloat16)
    cross_key = dot_plain(encoded, key_cross).astype(jnp.bfloat16)
    cross_value = dot_plain(encoded, value_cross).astype(jnp.bfloat16)
    mixed_cross, log_cross = run_forward(cross_query, cross_key, cross_value, 0.0, enc_len)
    hidden_two = hidden_one + forward_sum(dot_trans(mixed_cross, output_cross))
    scale_three, normed_share_three = rms_forward(hidden_two, gain_ffn)
    pre_act = dot_plain(normed_share_three, hidden_in)
    activ = jax.nn.gelu(pre_act).astype(jnp.bfloat16)
    part_width = model_width // group_count
    column_start = lax.axis_index("tensor") * part_width
    ffn_share = lax.psum_scatter(
        dot_trans(activ, hidden_out).astype(jnp.bfloat16), "tensor", scatter_dimension=1, tiled=True
    ).astype(jnp.float32)
    layer_out = (
        valid_rows * (lax.dynamic_slice_in_dim(hidden_two, column_start, part_width, 1) + ffn_share)
    ).astype(jnp.bfloat16)
    grad_top = out_grad.astype(jnp.float32) * valid_rows
    grad_top_low = grad_top.astype(jnp.bfloat16)
    grad_hidden_out = trans_dot(grad_top_low, activ)
    grad_act = dot_plain(grad_top_low, hidden_out)
    gelu_value, gelu_pull = jax.vjp(jax.nn.gelu, pre_act)
    grad_pre = gelu_pull(grad_act)[0].astype(jnp.bfloat16)
    grad_hidden_in = trans_dot(normed_share_three, grad_pre)
    grad_rows_three, grad_gain_three = rms_backward(
        hidden_two, scale_three, gain_ffn, backward_sum(dot_trans(grad_pre, hidden_in))
    )
    grad_hidden_two = grad_top + grad_rows_three
    grad_two_low = grad_hidden_two.astype(jnp.bfloat16)
    grad_output_cross = trans_dot(grad_two_low, mixed_cross)
    grad_mixed_cross = dot_plain(grad_two_low, output_cross).astype(jnp.bfloat16)
    grad_cq, grad_ck, grad_cv = run_backward(
        cross_query, cross_key, cross_value, 0.0, enc_len, log_cross, grad_mixed_cross, False
    )
    grad_query_cross = trans_dot(normed_share_two, grad_cq)
    grad_key_cross = trans_dot(encoded, grad_ck)
    grad_value_cross = trans_dot(encoded, grad_cv)
    encoded_grad = lax.psum_scatter(
        (dot_trans(grad_ck, key_cross) + dot_trans(grad_cv, value_cross)).astype(jnp.bfloat16),
        "tensor",
        scatter_dimension=0,
        tiled=True,
    )
    grad_rows_two, grad_gain_two = rms_backward(
        hidden_one, scale_two, gain_cross, backward_sum(dot_trans(grad_cq, query_cross))
    )
    grad_hidden_one = grad_hidden_two + grad_rows_two
    grad_one_low = grad_hidden_one.astype(jnp.bfloat16)
    grad_output_self = trans_dot(grad_one_low, mixed_self)
    grad_mixed_self = dot_plain(grad_one_low, output_self).astype(jnp.bfloat16)
    grad_q, grad_k, grad_v, score_sums = run_backward(
        query, key_rows, value_rows, self_bias, seq_len, log_self, grad_mixed_self, True
    )
    dist_sums = jnp.einsum("hij,ijd->dh", score_sums, dist_table, precision=highest)
    table_grad = jnp.dot(bucket_table.T, dist_sums, precision=highest)
    grad_query_self = trans_dot(normed_self, grad_q)
    grad_key_self = trans_dot(normed_self, grad_k)
    grad_value_self = trans_dot(normed_self, grad_v)
    grad_normed_self = backward_sum(
        dot_trans(grad_q, query_self) + dot_trans(grad_k, key_self) + dot_trans(grad_v, value_self)
    )
    grad_rows_one, grad_gain_one = rms_backward(row_data, scale_one, gain_self, grad_normed_self)
    total_grad = grad_hidden_one + grad_rows_one
    input_grad = lax.dynamic_slice_in_dim(total_grad, column_start, part_width, 1).astype(
        jnp.bfloat16
    )
    weight_sums = (
        lax.psum_scatter(grad_query_self, "dp", scatter_dimension=0, tiled=True),
        lax.psum_scatter(grad_key_self, "dp", scatter_dimension=0, tiled=True),
        lax.psum_scatter(grad_value_self, "dp", scatter_dimension=0, tiled=True),
        lax.psum_scatter(grad_output_self, "dp", scatter_dimension=0, tiled=True),
        lax.psum_scatter(grad_query_cross, "dp", scatter_dimension=0, tiled=True),
        lax.psum_scatter(grad_key_cross, "dp", scatter_dimension=0, tiled=True),
        lax.psum_scatter(grad_value_cross, "dp", scatter_dimension=0, tiled=True),
        lax.psum_scatter(grad_output_cross, "dp", scatter_dimension=0, tiled=True),
        lax.psum_scatter(grad_hidden_in, "dp", scatter_dimension=0, tiled=True),
        lax.psum_scatter(grad_hidden_out, "dp", scatter_dimension=0, tiled=True),
    )
    small_sums = lax.psum((grad_gain_one, grad_gain_two, grad_gain_three, table_grad), "dp")
    return (
        layer_out,
        input_grad,
        encoded_grad,
        small_sums[0],
        small_sums[1],
        small_sums[2],
        small_sums[3],
        weight_sums[0],
        weight_sums[1],
        weight_sums[2],
        weight_sums[3],
        weight_sums[4],
        weight_sums[5],
        weight_sums[6],
        weight_sums[7],
        weight_sums[8],
        weight_sums[9],
    )


def solution(mesh):
    placed = (
        P("dp", None),
        P("dp", None),
        P("dp"),
        P("dp"),
        P(),
        P(),
        P(),
        P(),
        P(None, "tensor"),
        P(None, "tensor"),
        P(None, "tensor"),
        P(None, "tensor"),
        P(None, "tensor"),
        P(None, "tensor"),
        P(None, "tensor"),
        P(None, "tensor"),
        P(None, "tensor"),
        P(None, "tensor"),
        P(None, "tensor"),
        P("dp", None),
    )
    return jax.shard_map(
        per_device,
        mesh=mesh,
        in_specs=placed,
        out_specs=(
            P("dp", "tensor"),
            P("dp", "tensor"),
            P(("dp", "tensor"), None),
            P(),
            P(),
            P(),
            P(None, "tensor"),
            P("dp", "tensor"),
            P("dp", "tensor"),
            P("dp", "tensor"),
            P("dp", "tensor"),
            P("dp", "tensor"),
            P("dp", "tensor"),
            P("dp", "tensor"),
            P("dp", "tensor"),
            P("dp", "tensor"),
            P("dp", "tensor"),
        ),
        check_vma=False,
    )
```

profile of v0, /device:TPU:0, one launch (start us, length us, event | category | flops | bytes accessed | tf_op | source)
XLA Modules:
  0.0 1179.0 jit_solution(1674157861249371850)
XLA Ops:
  10.8 5.9 fusion.105
  29.0 5.8 while.54
  48.3 6.2 convolution_convert_fusion.7
  61.5 48.3 %all-reduce.7.cloned.1.call-done = f32[1024,768]{1,0:T(8,128)} async-done(((f32[1024,768]{1,0:T(8,128)}), f32[1024,768]{1,0:T(8,128)}) %all-reduce.7.cloned.1.call-update) | async-done | bytes 3145744 | tf_op jit(solution)/shard_map/psum | solution.py:83
  118.7 8.6 while.55
  135.2 66.3 %all-reduce.9.cloned.1.call-done = f32[1024,768]{1,0:T(8,128)} async-done(((f32[1024,768]{1,0:T(8,128)}), f32[1024,768]{1,0:T(8,128)}) %all-reduce.9.cloned.1.call-update) | async-done | bytes 3145744 | tf_op jit(solution)/shard_map/psum | solution.py:83
  215.2 43.1 %all-reduce.11.cloned.1.call-done = bf16[1024,768]{1,0:T(8,128)(2,1)} async-done(((bf16[1024,768]{1,0:T(8,128)(2,1)}), bf16[1024,768]{1,0:T(8,128)(2,1)}) %all-reduce.11.cloned.1.call-update) | async-done | bytes 1572880 | tf_op jit(solution)/shard_map/psum | solution.py:87
  269.2 18.7 %while.56 = (s32[]{:T(128)}, bf16[2,4,128,3,64]{2,1,0,4,3:T(4,128)(2,1)}, bf16[2,4,512,3,64]{2,1,0,4,3:T(4,128)(2,1)}, bf16[2,4,512,3,64]{2,1,0,4,3:T(4,128)(2,1...) while((s32[]{:T(128)}, ...), condition=%wide.region_18.19_spmd, body=%wide.region_16.18_spmd.sunk | while | flops 511277568 | bytes 67089740 | solution.py:169
  292.3 42.8 %all-reduce.13.cloned.1.call-done = bf16[1024,768]{1,0:T(8,128)(2,1)} async-done(((bf16[1024,768]{1,0:T(8,128)(2,1)}), bf16[1024,768]{1,0:T(8,128)(2,1)}) %all-reduce.13.cloned.1.call-update) | async-done | bytes 1572880 | tf_op jit(solution)/shard_map/psum | solution.py:87
  348.8 11.2 while.57
  379.3 5.6 convolution_bitcast_fusion
  394.1 5.8 convolution_bitcast_fusion.1
  443.9 37.6 %all-reduce = (f32[768]{0:T(1024)}, f32[768]{0:T(1024)}, f32[768]{0:T(1024)}, f32[32,3]{0,1:T(4,128)}) all-reduce(f32[768]{0:T(1024)S(1)} %get-tuple-element.412, f32[768]{0:T(1024)S(1)} %copy-done.82, f32[768]{0:T(1024)S(1)} %copy-done.81, f32[32,3]{0,1:T(4,128)S(1)} %fusion.122), channel_id=1, replica_groups=mesh['dp'=8,'tensor'=4] {'dp'}, use_global_device_ids=true, to_apply=%region_29.30 | all-reduce | flops 2400 | bytes 19200 | tf_op jit(solution)/shard_map/psum | solution.py:268
  485.6 22.8 %reduce-scatter.31.cloned.1.call-done = f32[96,192]{1,0:T(8,128)} async-done(((f32[768,192]{1,0:T(8,128)}), f32[96,192]{1,0:T(8,128)}) %reduce-scatter.31.cloned.1.call-update) | async-done | bytes 73744 | tf_op jit(solution)/shard_map/reduce_scatter | solution.py:264
  508.5 65.4 %reduce-scatter.41.cloned.1.call-done = f32[96,192]{1,0:T(8,128)} async-done(((f32[768,192]{1,0:T(8,128)}), f32[96,192]{1,0:T(8,128)}) %reduce-scatter.41.cloned.1.call-update) | async-done | bytes 73744
  573.9 65.7 %reduce-scatter.29.cloned.1.call-done = f32[96,192]{1,0:T(8,128)} async-done(((f32[768,192]{1,0:T(8,128)}), f32[96,192]{1,0:T(8,128)}) %reduce-scatter.29.cloned.1.call-update) | async-done | bytes 73744 | tf_op jit(solution)/shard_map/reduce_scatter | solution.py:261
  639.5 65.3 %reduce-scatter.39.cloned.1.call-done = f32[96,192]{1,0:T(8,128)} async-done(((f32[768,192]{1,0:T(8,128)}), f32[96,192]{1,0:T(8,128)}) %reduce-scatter.39.cloned.1.call-update) | async-done | bytes 73744
  704.8 65.7 %reduce-scatter.27.cloned.1.call-done = f32[96,192]{1,0:T(8,128)} async-done(((f32[768,192]{1,0:T(8,128)}), f32[96,192]{1,0:T(8,128)}) %reduce-scatter.27.cloned.1.call-update) | async-done | bytes 73744 | tf_op jit(solution)/shard_map/reduce_scatter | solution.py:260
  770.5 65.3 %reduce-scatter.25.cloned.1.call-done = f32[96,192]{1,0:T(8,128)} async-done(((f32[768,192]{1,0:T(8,128)}), f32[96,192]{1,0:T(8,128)}) %reduce-scatter.25.cloned.1.call-update) | async-done | bytes 73744 | tf_op jit(solution)/shard_map/reduce_scatter | solution.py:259
  835.8 65.7 %reduce-scatter.21.cloned.1.call-done = f32[96,192]{1,0:T(8,128)} async-done(((f32[768,192]{1,0:T(8,128)}), f32[96,192]{1,0:T(8,128)}) %reduce-scatter.21.cloned.1.call-update) | async-done | bytes 73744 | tf_op jit(solution)/shard_map/reduce_scatter | solution.py:257
  901.5 65.2 %reduce-scatter.23.cloned.1.call-done = f32[96,192]{1,0:T(8,128)} async-done(((f32[768,192]{1,0:T(8,128)}), f32[96,192]{1,0:T(8,128)}) %reduce-scatter.23.cloned.1.call-update) | async-done | bytes 73744 | tf_op jit(solution)/shard_map/reduce_scatter | solution.py:258
  966.7 72.3 %reduce-scatter.33.cloned.1.call-done = f32[96,768]{1,0:T(8,128)} async-done(((f32[768,768]{1,0:T(8,128)}), f32[96,768]{1,0:T(8,128)}) %reduce-scatter.33.cloned.1.call-update) | async-done | bytes 294928 | tf_op jit(solution)/shard_map/reduce_scatter | solution.py:265
  1039.1 72.4 %reduce-scatter.35.cloned.1.call-done = f32[96,768]{1,0:T(8,128)} async-done(((f32[768,768]{1,0:T(8,128)}), f32[96,768]{1,0:T(8,128)}) %reduce-scatter.35.cloned.1.call-update) | async-done | bytes 294928 | tf_op jit(solution)/shard_map/reduce_scatter | solution.py:266
  1111.4 60.6 %reduce-scatter.19.cloned.1.call-done = bf16[1024,768]{1,0:T(8,128)(2,1)} async-done(((bf16[4096,768]{1,0:T(8,128)(2,1)}), bf16[1024,768]{1,0:T(8,128)(2,1)}) %reduce-scatter.19.cloned.1.call-update) | async-done | bytes 1572880 | tf_op jit(solution)/shard_map/reduce_scatter | solution.py:227
  (411 shorter events, 214.2 us)
Async XLA Ops:
  7.2 199.1 %copy-start = (bf16[768,768]{1,0:T(8,128)(2,1)S(1)}, bf16[768,768]{1,0:T(8,128)(2,1)}, u32[]{:S(2)}) copy-start(bf16[768,768]{1,0:T(8,128)(2,1)} %param.45) | copy-start | bytes 3538948
  7.2 102.6 %all-reduce.7.cloned.1.call-start = ((), (), s32[]{:S(2)}) async-start(), calls=%async_computation.12 | async-start | bytes 6291456 | tf_op jit(solution)/shard_map/psum | solution.py:83
  38.5 162.9 %all-reduce.9.cloned.1.call-start = ((), (), s32[]{:S(2)}) async-start(), calls=%async_computation.13 | async-start | bytes 6291456 | tf_op jit(solution)/shard_map/psum | solution.py:83
  132.7 125.5 %all-reduce.11.cloned.1.call-start = ((), (), s32[]{:S(2)}) async-start(), calls=%async_computation.14 | async-start | bytes 3145728 | tf_op jit(solution)/shard_map/psum | solution.py:87
  215.1 47.4 %copy-start.70 = (f32[1024]{0:T(1024)S(1)}, f32[1024]{0:T(1024)}, u32[]{:S(2)}) copy-start(f32[1024]{0:T(1024)} %convert_bitcast_fusion) | copy-start | bytes 12292
  215.1 47.4 %copy-start.73 = (f32[1024]{0:T(1024)S(1)}, f32[1024]{0:T(1024)}, u32[]{:S(2)}) copy-start(f32[1024]{0:T(1024)} %copy-done.72) | copy-start | bytes 12292
  215.1 47.4 %copy-start.76 = (f32[768]{0:T(1024)S(1)}, f32[768]{0:T(1024)}, u32[]{:S(2)}) copy-start(f32[768]{0:T(1024)} %param.35) | copy-start | bytes 9220
  215.1 47.4 %copy-start.84 = (f32[1024]{0:T(1024)S(1)}, f32[1024]{0:T(1024)}, u32[]{:S(2)}) copy-start(f32[1024]{0:T(1024)} %get-tuple-element.507) | copy-start | bytes 12292
  215.1 120.0 %all-reduce.13.cloned.1.call-start = ((), (), s32[]{:S(2)}) async-start(), calls=%async_computation.15 | async-start | bytes 3145728 | tf_op jit(solution)/shard_map/psum | solution.py:87
  289.1 50.2 %copy-start.26 = (bf16[1024,192]{0,1:T(8,128)(2,1)}, bf16[1024,192]{0,1:T(8,128)(2,1)S(1)}, u32[]{:S(2)}) copy-start(bf16[1024,192]{0,1:T(8,128)(2,1)S(1)} %reshape.265) | copy-start | bytes 1179652
  292.1 144.6 %all-reduce.15.cloned.1.call-start = ((), (), s32[]{:S(2)}) async-start(), calls=%async_computation.16 | async-start | bytes 3145728 | tf_op jit(solution)/shard_map/psum | solution.py:87
  368.0 113.6 %reduce-scatter.37.cloned.1.call-start = ((), (), s32[]{:S(2)}) async-start(), calls=%async_computation.26 | async-start | bytes 1966080
  372.7 135.8 %reduce-scatter.31.cloned.1.call-start = ((), (), s32[]{:S(2)}) async-start(), calls=%async_computation.23 | async-start | bytes 884736 | tf_op jit(solution)/shard_map/reduce_scatter | solution.py:264
  376.4 197.5 %reduce-scatter.41.cloned.1.call-start = ((), (), s32[]{:S(2)}) async-start(), calls=%async_computation.28 | async-start | bytes 884736
  387.2 252.3 %reduce-scatter.29.cloned.1.call-start = ((), (), s32[]{:S(2)}) async-start(), calls=%async_computation.22 | async-start | bytes 884736 | tf_op jit(solution)/shard_map/reduce_scatter | solution.py:261
  391.2 313.6 %reduce-scatter.39.cloned.1.call-start = ((), (), s32[]{:S(2)}) async-start(), calls=%async_computation.27 | async-start | bytes 884736
  402.2 368.3 %reduce-scatter.27.cloned.1.call-start = ((), (), s32[]{:S(2)}) async-start(), calls=%async_computation.21 | async-start | bytes 884736 | tf_op jit(solution)/shard_map/reduce_scatter | solution.py:260
  405.8 430.0 %reduce-scatter.25.cloned.1.call-start = ((), (), s32[]{:S(2)}) async-start(), calls=%async_computation.20 | async-start | bytes 884736 | tf_op jit(solution)/shard_map/reduce_scatter | solution.py:259
  407.4 494.1 %reduce-scatter.21.cloned.1.call-start = ((), (), s32[]{:S(2)}) async-start(), calls=%async_computation.18 | async-start | bytes 884736 | tf_op jit(solution)/shard_map/reduce_scatter | solution.py:257
  409.0 557.7 %reduce-scatter.23.cloned.1.call-start = ((), (), s32[]{:S(2)}) async-start(), calls=%async_computation.19 | async-start | bytes 884736 | tf_op jit(solution)/shard_map/reduce_scatter | solution.py:258
  410.6 628.4 %reduce-scatter.33.cloned.1.call-start = ((), (), s32[]{:S(2)}) async-start(), calls=%async_computation.24 | async-start | bytes 2654208 | tf_op jit(solution)/shard_map/reduce_scatter | solution.py:265
  416.2 695.2 %reduce-scatter.35.cloned.1.call-start = ((), (), s32[]{:S(2)}) async-start(), calls=%async_computation.25 | async-start | bytes 2654208 | tf_op jit(solution)/shard_map/reduce_scatter | solution.py:266
  421.4 750.6 %reduce-scatter.19.cloned.1.call-start = ((), (), s32[]{:S(2)}) async-start(), calls=%async_computation.17 | async-start | bytes 7864320 | tf_op jit(solution)/shard_map/reduce_scatter | solution.py:227
  439.6 732.4 %copy-start.1 = (bf16[768,768]{1,0:T(8,128)(2,1)S(1)}, bf16[768,768]{1,0:T(8,128)(2,1)}, u32[]{:S(2)}) copy-start(bf16[768,768]{1,0:T(8,128)(2,1)} %param.45) | copy-start | bytes 3538948
  (103 other events, 455.4 us)
Sparse Core Ops, SparseCore 0:
  38.6 71.1 all-reduce.6
  132.9 68.5 all-reduce.8
  215.3 42.9 all-reduce.10
  292.2 42.8 all-reduce.12
  368.1 42.8 all-reduce.14
  413.4 28.2 reduce-scatter.36
  445.9 62.5 reduce-scatter.30
  512.3 61.5 reduce-scatter.40
  578.1 61.3 reduce-scatter.28
  643.3 61.5 reduce-scatter.38
  709.1 61.3 reduce-scatter.26
  774.2 61.5 reduce-scatter.24
  840.0 61.4 reduce-scatter.20
  905.2 61.4 reduce-scatter.22
  971.1 67.9 reduce-scatter.32
  1043.4 67.9 reduce-scatter.34
  1114.5 57.4 reduce-scatter.18
where the time goes:
time: 1180 us
  waiting for transfers between devices  887 us (75%)
  matrix products  120 us (10%)
  local copies, waits for them, and re-layouts  75.7 us (6%)
  other arithmetic  40 us (3%)
  blocking collectives  37.6 us (3%)
  between operations  16 us (1%)
    unnamed x20, waiting for transfers between devices  131 us
    psum x2, waiting for transfers between devices, branch_total(): return lax.psum(term, 'tensor')  115 us
    psum x3, waiting for transfers between devices, norm_total(): return lax.psum(term.astype(jnp.bfloat16), 'tensor').astype(jnp.float32)  85.9 us
    reduce_scatter x1, waiting for transfers between devices, per_device(): lax.psum_scatter(grad_hidden_out, 'dp', scatter_dimension=0, tiled=True)  72.4 us
    reduce_scatter x1, waiting for transfers between devices, per_device(): lax.psum_scatter(grad_hidden_in, 'dp', scatter_dimension=0, tiled=True)  72.3 us
    reduce_scatter x1, waiting for transfers between devices, per_device(): lax.psum_scatter(grad_query_self, 'dp', scatter_dimension=0, tiled=True)  65.7 us
    reduce_scatter x1, waiting for transfers between devices, per_device(): lax.psum_scatter(grad_query_cross, 'dp', scatter_dimension=0, tiled=True)  65.7 us
    reduce_scatter x1, waiting for transfers between devices, per_device(): lax.psum_scatter(grad_output_self, 'dp', scatter_dimension=0, tiled=True)  65.7 us
  transfers between devices with their start and end apart: 17, of which 15 were waited for; matrix products, arithmetic and copies ran while one was open for 8% of the time, Pallas kernels for 0%

commit v1 on v0

--- a/solution.py
+++ b/solution.py
@@ -1,6 +1,10 @@
+import functools
+
 import jax
 import jax.numpy as jnp
 from jax import lax
+from jax.experimental import pallas as pl
+from jax.experimental.pallas import tpu as pltpu
 from jax.sharding import PartitionSpec as P
 
 HD = 64
@@ -79,12 +83,185 @@
     return (grad_query, grad_key, grad_value)
 
 
-def branch_total(term):
-    return lax.psum(term, "tensor")
-
-
-def norm_total(term):
-    return lax.psum(term.astype(jnp.bfloat16), "tensor").astype(jnp.float32)
+MESH = pl.DeviceIdType.MESH
+VM = pl.BlockSpec(memory_space=pltpu.VMEM)
+
+
+def tensor_peer(bit):
+    return (lax.axis_index("dp"), lax.axis_index("tensor") ^ bit)
+
+
+def dp_peer(bit):
+    return (lax.axis_index("dp") ^ bit, lax.axis_index("tensor"))
+
+
+def greet(peers):
+    barrier = pltpu.get_barrier_semaphore()
+    for peer in peers:
+        pl.semaphore_signal(barrier, inc=1, device_id=peer, device_id_type=MESH)
+    pl.semaphore_wait(barrier, len(peers))
+
+
+def send(src, dst, sems, index, peer):
+    copy = pltpu.make_async_remote_copy(
+        src_ref=src,
+        dst_ref=dst,
+        send_sem=sems.at[0, index],
+        recv_sem=sems.at[1, index],
+        device_id=peer,
+        device_id_type=MESH,
+    )
+    copy.start()
+    return copy
+
+
+def total_kernel(term, out, near, mine, far, sems):
+    rows = term.shape[0] // 2
+    core = lax.rem(lax.axis_index("tensor"), 2)
+    greet([tensor_peer(1), tensor_peer(2)])
+    own = pl.multiple_of(core * rows, rows)
+    other = pl.multiple_of((1 - core) * rows, rows)
+    first = send(term.at[pl.ds(other, rows)], near, sems, 0, tensor_peer(1))
+    first.wait()
+    mine[...] = (
+        term[pl.ds(own, rows)].astype(jnp.float32) + near[...].astype(jnp.float32)
+    ).astype(jnp.bfloat16)
+    second = send(mine, far, sems, 1, tensor_peer(2))
+    second.wait()
+    out[pl.ds(own, rows)] = (
+        mine[...].astype(jnp.float32) + far[...].astype(jnp.float32)
+    ).astype(jnp.bfloat16)
+    third = send(out.at[pl.ds(own, rows)], out.at[pl.ds(own, rows)], sems, 2, tensor_peer(1))
+    third.wait()
+
+
+def tensor_total(term, ident):
+    rows, width = term.shape
+    half = pltpu.VMEM((rows // 2, width), jnp.bfloat16)
+    return pl.pallas_call(
+        total_kernel,
+        out_shape=jax.ShapeDtypeStruct(term.shape, jnp.bfloat16),
+        in_specs=[VM],
+        out_specs=VM,
+        scratch_shapes=[half, half, half, pltpu.SemaphoreType.DMA((2, 3))],
+        compiler_params=pltpu.CompilerParams(
+            collective_id=ident, has_side_effects=True, vmem_limit_bytes=24 * 2**20
+        ),
+    )(term)
+
+
+def scatter_kernel(term, out, near, mine, far, sems):
+    rows = term.shape[1]
+    me = lax.axis_index("tensor")
+    core = lax.rem(me, 2)
+    greet([tensor_peer(1), tensor_peer(2)])
+    y = me // 2
+    first = send(term.at[(1 - core) + 2 * (1 - y)], near.at[0], sems, 0, tensor_peer(1))
+    second = send(term.at[(1 - core) + 2 * y], near.at[1], sems, 1, tensor_peer(1))
+    first.wait()
+    mine[...] = (
+        term[core + 2 * (1 - y)].astype(jnp.float32) + near[0].astype(jnp.float32)
+    ).astype(jnp.bfloat16)
+    third = send(mine, far, sems, 2, tensor_peer(2))
+    second.wait()
+    third.wait()
+    out[...] = (
+        term[core + 2 * y].astype(jnp.float32)
+        + near[1].astype(jnp.float32)
+        + far[...].astype(jnp.float32)
+    ).astype(jnp.bfloat16)
+
+
+def tensor_scatter(term, ident):
+    rows, width = term.shape
+    quarter = pltpu.VMEM((rows // 4, width), jnp.bfloat16)
+    return pl.pallas_call(
+        scatter_kernel,
+        out_shape=jax.ShapeDtypeStruct((rows // 4, width), jnp.bfloat16),
+        in_specs=[VM],
+        out_specs=VM,
+        scratch_shapes=[
+            pltpu.VMEM((2, rows // 4, width), jnp.bfloat16),
+            quarter,
+            quarter,
+            pltpu.SemaphoreType.DMA((2, 3)),
+        ],
+        compiler_params=pltpu.CompilerParams(
+            collective_id=ident, has_side_effects=True, vmem_limit_bytes=40 * 2**20
+        ),
+    )(term.reshape(4, rows // 4, width))
+
+
+def halving_kernel(chunks, levels, term, out, *rest):
+    lands, holds, sems = rest[:levels], rest[levels:-1], rest[-1]
+    me = lax.axis_index("dp")
+    greet([dp_peer(1 << k) for k in range(levels)])
+
+    def part(ref, chunk, count, bit):
+        return ref.at[chunk, bit, :]
+
+    pending = []
+    for chunk in range(chunks):
+        pending.append(None)
+
+    def start(level, chunk):
+        bit = lax.rem(me // (1 << level), 2)
+        source = term if level == 0 else holds[level - 1]
+        return send(
+            source.at[chunk, 1 - bit],
+            lands[level].at[chunk],
+            sems,
+            level * chunks + chunk,
+            dp_peer(1 << level),
+        )
+
+    def finish(level, chunk, copy):
+        bit = lax.rem(me // (1 << level), 2)
+        source = term if level == 0 else holds[level - 1]
+        copy.wait_recv()
+        total = source[chunk, bit].astype(jnp.float32) + lands[level][chunk].astype(jnp.float32)
+        if level == levels - 1:
+            out[chunk] = total.reshape(out.shape[1:])
+        else:
+            holds[level][chunk] = total.reshape(holds[level].shape[1:]).astype(jnp.bfloat16)
+
+    copies = {}
+    for chunk in range(chunks):
+        copies[0, chunk] = start(0, chunk)
+    for step in range(chunks + levels - 1):
+        for level in range(levels):
+            chunk = step - level
+            if 0 <= chunk < chunks:
+                finish(level, chunk, copies[level, chunk])
+                if level + 1 < levels:
+                    copies[level + 1, chunk] = start(level + 1, chunk)
+    for copy in copies.values():
+        copy.wait_send()
+
+
+def dp_scatter(term, chunks, ident):
+    n, rows, columns = term.shape
+    width = columns // chunks
+    levels = n.bit_length() - 1
+    shape = term.reshape((2,) * levels + (rows, chunks, width))
+    order = (levels + 1,) + tuple(range(levels - 1, -1, -1)) + (levels, levels + 2)
+    pieces = shape.transpose(order)
+    lands, holds = [], []
+    for level in range(levels):
+        left = (2,) * (levels - 1 - level)
+        lands.append(pltpu.VMEM((chunks,) + left + (rows, width), jnp.bfloat16))
+        if level + 1 < levels:
+            holds.append(pltpu.VMEM((chunks,) + left + (rows, width), jnp.bfloat16))
+    return pl.pallas_call(
+        functools.partial(halving_kernel, chunks, levels),
+        out_shape=jax.ShapeDtypeStruct((chunks, rows, width), jnp.float32),
+        in_specs=[VM],
+        out_specs=VM,
+        scratch_shapes=lands + holds + [pltpu.SemaphoreType.DMA((2, levels * chunks))],
+        compiler_params=pltpu.CompilerParams(
+            collective_id=ident, has_side_effects=True, vmem_limit_bytes=48 * 2**20
+        ),
+    )(pieces)
 
 
 def per_device(
@@ -123,11 +300,12 @@
     row_data = inputs.astype(jnp.float32)
     group_count = lax.axis_size("tensor")
 
+    idents = iter(range(1, 20))
+
     def forward_sum(term):
-        return branch_total(term)
-
-    def backward_sum(term):
-        return norm_total(term)
+        return tensor_total(term.astype(jnp.bfloat16), next(idents)).astype(jnp.float32)
+
+    backward_sum = forward_sum
 
     distance = jnp.maximum(positions[:, None] - positions[None, :], 0)
     dist_table = (distance[:, :, None] == positions[None, None, :]).astype(jnp.float32)
@@ -198,9 +376,9 @@
     activ = jax.nn.gelu(pre_act).astype(jnp.bfloat16)
     part_width = model_width // group_count
     column_start = lax.axis_index("tensor") * part_width
-    ffn_share = lax.psum_scatter(
-        dot_trans(activ, hidden_out).astype(jnp.bfloat16), "tensor", scatter_dimension=1, tiled=True
-    ).astype(jnp.float32)
+    ffn_share = lax.dynamic_slice_in_dim(
+        forward_sum(dot_trans(activ, hidden_out)), column_start, part_width, 1
+    )
     layer_out = (
         valid_rows * (lax.dynamic_slice_in_dim(hidden_two, column_start, part_width, 1) + ffn_share)
     ).astype(jnp.bfloat16)
@@ -224,11 +402,9 @@
     grad_query_cross = trans_dot(normed_share_two, grad_cq)
     grad_key_cross = trans_dot(encoded, grad_ck)
     grad_value_cross = trans_dot(encoded, grad_cv)
-    encoded_grad = lax.psum_scatter(
+    encoded_grad = tensor_scatter(
         (dot_trans(grad_ck, key_cross) + dot_trans(grad_cv, value_cross)).astype(jnp.bfloat16),
-        "tensor",
-        scatter_dimension=0,
-        tiled=True,
+        next(idents),
     )
     grad_rows_two, grad_gain_two = rms_backward(
         hidden_one, scale_two, gain_cross, backward_sum(dot_trans(grad_cq, query_cross))
@@ -253,18 +429,36 @@
     input_grad = lax.dynamic_slice_in_dim(total_grad, column_start, part_width, 1).astype(
         jnp.bfloat16
     )
-    weight_sums = (
-        lax.psum_scatter(grad_query_self, "dp", scatter_dimension=0, tiled=True),
-        lax.psum_scatter(grad_key_self, "dp", scatter_dimension=0, tiled=True),
-        lax.psum_scatter(grad_value_self, "dp", scatter_dimension=0, tiled=True),
-        lax.psum_scatter(grad_output_self, "dp", scatter_dimension=0, tiled=True),
-        lax.psum_scatter(grad_query_cross, "dp", scatter_dimension=0, tiled=True),
-        lax.psum_scatter(grad_key_cross, "dp", scatter_dimension=0, tiled=True),
-        lax.psum_scatter(grad_value_cross, "dp", scatter_dimension=0, tiled=True),
-        lax.psum_scatter(grad_output_cross, "dp", scatter_dimension=0, tiled=True),
-        lax.psum_scatter(grad_hidden_in, "dp", scatter_dimension=0, tiled=True),
-        lax.psum_scatter(grad_hidden_out, "dp", scatter_dimension=0, tiled=True),
-    )
+    weight_grads = (
+        grad_query_self,
+        grad_key_self,
+        grad_value_self,
+        grad_output_self,
+        grad_query_cross,
+        grad_key_cross,
+        grad_value_cross,
+        grad_output_cross,
+        grad_hidden_in,
+        grad_hidden_out,
+    )
+    dp_count = lax.axis_size("dp")
+    piece_rows = model_width // dp_count
+    if piece_rows % 16 == 0:
+        merged = jnp.concatenate([grad.astype(jnp.bfloat16) for grad in weight_grads], axis=1)
+        chunks = 4
+        summed = dp_scatter(
+            merged.reshape(dp_count, piece_rows, merged.shape[1]), chunks, next(idents)
+        )
+        summed = summed.transpose(1, 0, 2).reshape(piece_rows, merged.shape[1])
+        weight_sums = []
+        column = 0
+        for grad in weight_grads:
+            weight_sums.append(summed[:, column : column + grad.shape[1]])
+            column += grad.shape[1]
+    else:
+        weight_sums = [
+            lax.psum_scatter(grad, "dp", scatter_dimension=0, tiled=True) for grad in weight_grads
+        ]
     small_sums = lax.psum((grad_gain_one, grad_gain_two, grad_gain_three, table_grad), "dp")
     return (
         layer_out,

time: 1180 us -> 544 us (0.46)
  waiting for transfers between devices: 887 us -> 0 us
  Pallas kernels: 0 us -> 262 us
  local copies, waits for them, and re-layouts: 75.7 us -> 109 us
  matrix products: 120 us -> 97.2 us
  between operations: 16 us -> 4.15 us
    reduce_scatter x9 -> x0, waiting for transfers between devices: 556 us -> none  [the longest x1 72.4 us: per_device(): lax.psum_scatter(grad_hidden_out, 'dp', scatter_dimension=0, tiled=True)]
    pallas_call x0 -> x8, Pallas kernels: none -> 262 us  [the longest x6 148 us: tensor_total(): pl.pallas_call(total_kernel, out_shape=jax.ShapeDtypeStruct(term.shape, j...]
    psum x5 -> x0, waiting for transfers between devices: 200 us -> none  [the longest x2 115 us: branch_total(): return lax.psum(term, 'tensor')]
    unnamed x20 -> x0, waiting for transfers between devices: 131 us -> none
    another operation x8 -> x10, local copies, waits for them, and re-layouts: 5 us -> 40.6 us  [the longest x2 35.6 us: dp_scatter(): shape = term.reshape((2,) * levels + (rows, chunks, width))]
    dot_general x10, matrix products: 27.5 us -> 14.7 us  [dot_trans(): lax.dot_general(left, right, (((1,), (1,)), ((), ())), preferred_element_...]
    dot_general x10, matrix products: 37.4 us -> 25.5 us  [trans_dot(): lax.dot_general(left, right, (((0,), (0,)), ((), ())), preferred_element_...]
  transfers between devices with their start and end apart: 17 -> 0, of which waited for: 15 -> 0; matrix products, arithmetic and copies ran while one was open for 8% -> 0% of each run, Pallas kernels for 0% -> 0%
where the time goes in v1:
time: 544 us; the launch traced here: 539 us
  Pallas kernels  262 us (48%)
  local copies, waits for them, and re-layouts  109 us (20%)
  matrix products  97.2 us (18%)
  blocking collectives  35.3 us (6%)
  other arithmetic  30.4 us (6%)
    pallas_call x6, Pallas kernels, tensor_total(): pl.pallas_call(total_kernel, out_shape=jax.ShapeDtypeStruct(term.shape, j...  148 us
    pallas_call x1, Pallas kernels, dp_scatter(): pl.pallas_call(functools.partial(halving_kernel, chunks, levels), out_sha...  73.6 us
    pallas_call x1, Pallas kernels, tensor_scatter(): pl.pallas_call(scatter_kernel, out_shape=jax.ShapeDtypeStruct((rows // 4,...  41.1 us
    another operation x2, local copies, waits for them, and re-layouts, dp_scatter(): shape = term.reshape((2,) * levels + (rows, chunks, width))  35.6 us
    psum x1, blocking collectives, per_device(): lax.psum((grad_gain_one, grad_gain_two, grad_gain_three, table_grad), 'dp')  35.3 us
    dot_general x10, matrix products, trans_dot(): lax.dot_general(left, right, (((0,), (0,)), ((), ())), preferred_element_...  25.5 us
    dot_general x10, matrix products, dot_plain(): return jnp.dot(left, right, preferred_element_type=jnp.float32)  22.8 us
    unnamed x157, local copies, waits for them, and re-layouts  17.3 us

profile of v1, /device:TPU:0, one launch (start us, length us, event | category | flops | bytes accessed | tf_op | source)
XLA Modules:
  0.0 539.3 jit_solution(4710526724275959234)
XLA Ops:
  11.5 6.0 %fusion.116 = f32[3,128,128]{2,0,1:T(4,128)S(1)} fusion(f32[128,3,1]{0,1,2:T(4,128)S(1)} %convolution_bitcast_fusion, s32[128,128]{1,0:T(8,128)S(1)} %subtract_maximum_fusion, pred[128,128]{1,0:T(8,128)(4,1)S(1)} %iota_compare_fusion.10), kind=kOutput, calls=%fused_computation.191 | convolution fusion | flops 77643776 | bytes 280064 | tf_op jit(solution)/shard_map/ijd,dh->hij/dot_general | solution.py:319
  17.7 3.9 while.54
  23.9 25.5 %shard_map.323 = bf16[1024,768]{1,0:T(8,128)(2,1)S(1)} custom-call(bf16[1024,768]{1,0:T(8,128)(2,1)S(1)} %convolution_convert_fusion.12.term), custom_call_target="tpu_custom_call" | custom-call | tf_op jit(solution)/shard_map/pallas_call | solution.py:141
  57.1 6.1 %convolution_convert_fusion.7 = bf16[4096,192]{0,1:T(8,128)(2,1)} fusion(bf16[4096,768]{1,0:T(8,128)(2,1)} %param.29, bf16[768,192]{0,1:T(8,128)(2,1)} %param.43), kind=kOutput, calls=%fused_computation.107 | convolution fusion | flops 1208745984 | bytes 8159232 | tf_op jit(solution)/shard_map/dot_general | solution.py:20
  63.2 3.8 reshape.266
  70.2 6.1 %convolution_convert_fusion.6 = bf16[4096,192]{0,1:T(8,128)(2,1)} fusion(bf16[4096,768]{1,0:T(8,128)(2,1)} %param.29, bf16[768,192]{0,1:T(8,128)(2,1)S(1)} %copy-done.56), kind=kOutput, calls=%fused_computation.106 | convolution fusion | flops 1208745984 | bytes 8159232 | tf_op jit(solution)/shard_map/dot_general | solution.py:20
  76.3 3.8 reshape.268
  84.7 11.4 %while.55 = (s32[]{:T(128)}, bf16[2,4,128,3,64]{2,1,0,4,3:T(4,128)(2,1)}, f32[2,4,3,128]{3,2,1,0:T(4,128)}, bf16[2,4,512,3,64]{2,4,3,1,0:T(8,128)(2,1)}, bf16[2,...) while((s32[]{:T(128)}, bf16[2,4,128,3,64]{2,1,0,4,3:T(4,128)(2,1)}, ...), condition=%wide.region_9.10_spmd, body=%wide.region_6.9_spmd.sunk | while | flops 206141952 | bytes 18247336 | solution.py:332
  99.9 24.6 %shard_map.324 = bf16[1024,768]{1,0:T(8,128)(2,1)S(1)} custom-call(bf16[1024,768]{1,0:T(8,128)(2,1)S(1)} %convolution_convert_fusion.11.term), custom_call_target="tpu_custom_call" | custom-call | tf_op jit(solution)/shard_map/pallas_call | solution.py:141
  135.1 24.4 %shard_map.326 = bf16[1024,768]{1,0:T(8,128)(2,1)S(1)} custom-call(bf16[1024,768]{1,0:T(8,128)(2,1)S(1)} %convolution_convert_fusion.9.term), custom_call_target="tpu_custom_call" | custom-call | tf_op jit(solution)/shard_map/pallas_call | solution.py:141
  166.6 21.5 %while.56 = (s32[]{:T(128)}, bf16[2,4,128,3,64]{2,1,0,4,3:T(4,128)(2,1)}, bf16[2,4,512,3,64]{2,1,0,4,3:T(4,128)(2,1)}, bf16[2,4,512,3,64]{2,1,0,4,3:T(4,128)(2,1...) while((s32[]{:T(128)}, ...), condition=%wide.region_14.15_spmd, body=%wide.region_12.14_spmd.sunk | while | flops 511277568 | bytes 70235936 | solution.py:347
  191.2 24.4 %shard_map.327 = bf16[1024,768]{1,0:T(8,128)(2,1)S(1)} custom-call(bf16[1024,768]{1,0:T(8,128)(2,1)S(1)} %convolution_convert_fusion.8.term), custom_call_target="tpu_custom_call" | custom-call | tf_op jit(solution)/shard_map/pallas_call | solution.py:141
  225.7 10.5 %while.57 = (s32[]{:T(128)}, bf16[2,4,128,3,64]{2,1,0,4,3:T(4,128)(2,1)}, bf16[2,4,128,3,64]{2,1,0,4,3:T(4,128)(2,1)}, bf16[2,4,128,3,64]{2,1,0,4,3:T(4,128)(2,1...) while((s32[]{:T(128)}, ...), condition=%wide.region_19.20_spmd, body=%wide.region_16.19_spmd.sunk | while | flops 128039424 | bytes 19695924 | solution.py:347
  249.6 4.9 fusion.113
  254.5 3.8 reshape.277
  258.3 5.5 %fusion.115 = bf16[768,3072]{0,1:T(8,128)(2,1)} fusion(bf16[768,3072]{0,1:T(8,128)(2,1)} %fusion.113, bf16[4096,192]{0,1:T(8,128)(2,1)} %reshape.277, bf16[4096,768]{1,0:T(8,128)(2,1)} %param.29), kind=kOutput, calls=%fused_computation.190 | convolution fusion | flops 1208107008 | bytes 8159232 | tf_op jit(solution)/shard_map/dot_general | solution.py:30
  271.8 19.6 %reshape.283 = bf16[2,2,2,96,4,768]{3,2,1,0,5,4:T(2,128)(2,1)} reshape(bf16[768,3072]{0,1:T(8,128)(2,1)} %fusion.104) | data formatting | bytes 9437184 | tf_op jit(solution)/shard_map/reshape;reshape | solution.py:246
  291.3 16.0 %copy.155 = bf16[2,2,2,96,4,768]{5,3,0,1,2,4:T(8,128)(2,1)} copy(bf16[2,2,2,96,4,768]{3,2,1,0,5,4:T(2,128)(2,1)} %reshape.283) | data formatting | bytes 9437184 | tf_op jit(solution)/shard_map/reshape;reshape | solution.py:246
  309.7 73.6 %shard_map.330 = f32[4,96,768]{2,1,0:T(8,128)S(1)} custom-call(bf16[4,2,2,2,96,768]{5,4,3,2,1,0:T(8,128)(2,1)S(1)} %bitcast.298), custom_call_target="tpu_custom_call" | custom-call | tf_op jit(solution)/shard_map/pallas_call | solution.py:255
  387.2 24.4 %shard_map.328 = bf16[1024,768]{1,0:T(8,128)(2,1)S(1)} custom-call(bf16[1024,768]{1,0:T(8,128)(2,1)S(1)} %add_convert_fusion.1.term), custom_call_target="tpu_custom_call" | custom-call | tf_op jit(solution)/shard_map/pallas_call | solution.py:141
  419.5 35.3 %all-reduce = (f32[768]{0:T(1024)}, f32[768]{0:T(1024)}, f32[768]{0:T(1024)}, f32[32,3]{0,1:T(4,128)}) all-reduce(f32[768]{0:T(1024)S(1)} %get-tuple-element.412, f32[768]{0:T(1024)S(1)} %copy-done.79, f32[768]{0:T(1024)S(1)} %copy-done.78, f32[32,3]{0,1:T(4,128)S(1)} %fusion.130), channel_id=1, replica_groups=mesh['dp'=8,'tensor'=4] {'dp'}, use_global_device_ids=true, to_apply=%region_22.23 | all-reduce | flops 2400 | bytes 19200 | tf_op jit(solution)/shard_map/psum | solution.py:462
  460.1 41.1 %shard_map.329 = bf16[1024,768]{1,0:T(8,128)(2,1)S(1)} custom-call(bf16[4,1024,768]{2,1,0:T(8,128)(2,1)S(1)} %bitcast.297), custom_call_target="tpu_custom_call" | custom-call | tf_op jit(solution)/shard_map/pallas_call | solution.py:178
  503.2 24.4 %shard_map.325 = bf16[1024,768]{1,0:T(8,128)(2,1)S(1)} custom-call(bf16[1024,768]{1,0:T(8,128)(2,1)S(1)} %convolution_convert_fusion.10.term), custom_call_target="tpu_custom_call" | custom-call | tf_op jit(solution)/shard_map/pallas_call | solution.py:141
  530.4 4.5 fusion.118
  (365 shorter events, 156.0 us)
Async XLA Ops:
  0.7 124.7 %copy-start = (bf16[768,768]{1,0:T(8,128)(2,1)S(1)}, bf16[768,768]{1,0:T(8,128)(2,1)}, u32[]{:S(2)}) copy-start(bf16[768,768]{1,0:T(8,128)(2,1)} %param.45) | copy-start | bytes 3538948
  17.7 5.5 %copy-start.49 = (bf16[768,192]{0,1:T(8,128)(2,1)S(1)}, bf16[768,192]{0,1:T(8,128)(2,1)}, u32[]{:S(2)}) copy-start(bf16[768,192]{0,1:T(8,128)(2,1)} %param.40) | copy-start | bytes 884740
  23.9 28.7 %copy-start.4 = (bf16[1024,768]{1,0:T(8,128)(2,1)S(1)}, bf16[1024,768]{1,0:T(8,128)(2,1)}, u32[]{:S(2)}) copy-start(bf16[1024,768]{1,0:T(8,128)(2,1)} %param.28) | copy-start | bytes 4718596
  23.9 28.7 %copy-start.68 = (f32[768]{0:T(1024)S(1)}, f32[768]{0:T(1024)}, u32[]{:S(2)}) copy-start(f32[768]{0:T(1024)} %param.34) | copy-start | bytes 9220
  98.1 26.5 %copy-start.5 = (bf16[1024,768]{1,0:T(8,128)(2,1)S(1)}, bf16[1024,768]{1,0:T(8,128)(2,1)}, u32[]{:S(2)}) copy-start(bf16[1024,768]{1,0:T(8,128)(2,1)} %param.28) | copy-start | bytes 4718596
  125.4 35.8 %copy-start.12 = (f32[1024,768]{1,0:T(8,128)}, f32[1024,768]{1,0:T(8,128)S(1)}, u32[]{:S(2)}) copy-start(f32[1024,768]{1,0:T(8,128)S(1)} %get-tuple-element.487) | copy-start | bytes 9437188
  125.4 35.8 %copy-start.72 = (f32[1024]{0:T(1024)}, f32[1024]{0:T(1024)S(1)}, u32[]{:S(2)}) copy-start(f32[1024]{0:T(1024)S(1)} %get-tuple-element.516) | copy-start | bytes 12292
  126.9 5.5 %copy-start.87 = (f32[1024,768]{1,0:T(8,128)}, f32[1024,768]{1,0:T(8,128)S(1)}, u32[]{:S(2)}) copy-start(f32[1024,768]{1,0:T(8,128)S(1)} %fusion.134) | copy-start | bytes 9437188
  129.3 31.8 %copy-start.70 = (f32[1024]{0:T(1024)}, f32[1024]{0:T(1024)S(1)}, u32[]{:S(2)}) copy-start(f32[1024]{0:T(1024)S(1)} %convert_bitcast_fusion) | copy-start | bytes 12292
  188.1 27.4 %copy-start.65 = (f32[1024]{0:T(1024)S(1)}, f32[1024]{0:T(1024)}, u32[]{:S(2)}) copy-start(f32[1024]{0:T(1024)} %copy-done.64) | copy-start | bytes 12292
  188.1 27.4 %copy-start.69 = (f32[768]{0:T(1024)S(1)}, f32[768]{0:T(1024)}, u32[]{:S(2)}) copy-start(f32[768]{0:T(1024)} %param.34) | copy-start | bytes 9220
  189.4 29.7 %copy-start.30 = (bf16[1024,192]{0,1:T(8,128)(2,1)}, bf16[1024,192]{0,1:T(8,128)(2,1)S(1)}, u32[]{:S(2)}) copy-start(bf16[1024,192]{0,1:T(8,128)(2,1)S(1)} %reshape.271) | copy-start | bytes 1179652
  225.7 12.6 %copy-start.22 = (bf16[1024,768]{1,0:T(8,128)(2,1)S(1)}, bf16[1024,768]{1,0:T(8,128)(2,1)}, u32[]{:S(2)}) copy-start(bf16[1024,768]{1,0:T(8,128)(2,1)} %copy-done.21) | copy-start | bytes 4718596
  239.7 5.8 %copy-start.28 = (bf16[1024,192]{0,1:T(8,128)(2,1)}, bf16[1024,192]{0,1:T(8,128)(2,1)S(1)}, u32[]{:S(2)}) copy-start(bf16[1024,192]{0,1:T(8,128)(2,1)S(1)} %reshape.274) | copy-start | bytes 1179652
  258.3 5.5 %copy-start.11 = (f32[1024,768]{1,0:T(8,128)S(1)}, f32[1024,768]{1,0:T(8,128)}, u32[]{:S(2)}) copy-start(f32[1024,768]{1,0:T(8,128)} %copy-done.9) | copy-start | bytes 9437188
  258.3 5.5 %copy-start.27 = (bf16[1024,192]{0,1:T(8,128)(2,1)S(1)}, bf16[1024,192]{0,1:T(8,128)(2,1)}, u32[]{:S(2)}) copy-start(bf16[1024,192]{0,1:T(8,128)(2,1)} %reshape.269) | copy-start | bytes 1179652
  258.3 6.8 %copy-start.91 = (bf16[1024,768]{1,0:T(8,128)(2,1)S(1)}, bf16[1024,768]{1,0:T(8,128)(2,1)}, u32[]{:S(2)}) copy-start(bf16[1024,768]{1,0:T(8,128)(2,1)} %copy-done.90) | copy-start | bytes 4718596
  387.1 24.4 %copy-start.7 = (bf16[1024,768]{1,0:T(8,128)(2,1)S(1)}, bf16[1024,768]{1,0:T(8,128)(2,1)}, u32[]{:S(2)}) copy-start(bf16[1024,768]{1,0:T(8,128)(2,1)} %param.28) | copy-start | bytes 4718596
  387.2 24.4 %copy-start.63 = (f32[1024]{0:T(1024)S(1)}, f32[1024]{0:T(1024)}, u32[]{:S(2)}) copy-start(f32[1024]{0:T(1024)} %copy-done.62) | copy-start | bytes 12292
  387.2 24.4 %copy-start.76 = (f32[768]{0:T(1024)S(1)}, f32[768]{0:T(1024)}, u32[]{:S(2)}) copy-start(f32[768]{0:T(1024)} %param.33) | copy-start | bytes 9220
  414.6 40.2 %copy-start.57 = (bf16[768,192]{0,1:T(8,128)(2,1)S(1)}, bf16[768,192]{0,1:T(8,128)(2,1)}, u32[]{:S(2)}) copy-start(bf16[768,192]{0,1:T(8,128)(2,1)} %param.42) | copy-start | bytes 884740
  460.1 41.1 %copy-start.83 = (bf16[768,768]{1,0:T(8,128)(2,1)S(1)}, bf16[768,768]{1,0:T(8,128)(2,1)}, u32[]{:S(2)}) copy-start(bf16[768,768]{1,0:T(8,128)(2,1)} %param.46) | copy-start | bytes 3538948
  460.1 41.1 %copy-start.89 = (f32[1024,768]{1,0:T(8,128)S(1)}, f32[1024,768]{1,0:T(8,128)}, u32[]{:S(2)}) copy-start(f32[1024,768]{1,0:T(8,128)} %copy-done.87) | copy-start | bytes 9437188
  530.4 8.6 %copy-start.1 = (bf16[768,768]{1,0:T(8,128)(2,1)S(1)}, bf16[768,768]{1,0:T(8,128)(2,1)}, u32[]{:S(2)}) copy-start(bf16[768,768]{1,0:T(8,128)(2,1)} %param.45) | copy-start | bytes 3538948
  (83 other events, 192.0 us)

commit v2 on v0

v2 whole, which is shorter than its diff:
```python
import functools
from types import SimpleNamespace
from typing import NamedTuple

import jax
import jax.numpy as jnp
from jax import lax
from jax.experimental import pallas as pl
from jax.experimental.pallas import tpu as pltpu
from jax.sharding import PartitionSpec as P

HD = 64
CHUNK_SLOTS = 2
GELU_ROWS = 32

norm_epsilon = 1e-06
masked_score = -1e30
highest = lax.Precision.HIGHEST
MESH = pl.DeviceIdType.MESH
VM = pl.BlockSpec(memory_space=pltpu.VMEM)
SM = pl.BlockSpec(memory_space=pltpu.SMEM)
HBM = pl.BlockSpec(memory_space=pl.ANY)
low = jnp.bfloat16
wide = jnp.float32


def dot(left, right):
    return lax.dot_general(left, right, (((1,), (0,)), ((), ())), preferred_element_type=wide)


def dot_t(left, right):
    return lax.dot_general(left, right, (((1,), (1,)), ((), ())), preferred_element_type=wide)


def t_dot(left, right):
    return lax.dot_general(left, right, (((0,), (0,)), ((), ())), preferred_element_type=wide)


def inverse_rms(rows):
    return lax.rsqrt(jnp.mean(rows * rows, axis=-1, keepdims=True) + norm_epsilon)


def norm_back(rows, gain, grad):
    inverse = inverse_rms(rows)
    scaled = gain * grad
    inner = jnp.mean(scaled * rows, axis=-1, keepdims=True)
    grad_rows = inverse * scaled - rows * (inverse * inverse * inverse) * inner
    return grad_rows, jnp.sum(grad * rows * inverse, axis=0, keepdims=True)


def tensor_peer(bit):
    return (lax.axis_index("dp"), lax.axis_index("tensor") ^ bit)


def dp_peer(bit):
    return (lax.axis_index("dp") ^ bit, lax.axis_index("tensor"))


def reversed_bits(value, levels):
    return sum(((value >> k) & 1) << (levels - 1 - k) for k in range(levels))


class Weights(NamedTuple):
    query_self: object
    key_self: object
    value_self: object
    output_self: object
    query_cross: object
    key_cross: object
    value_cross: object
    output_cross: object
    hidden_in: object
    hidden_out: object


def layer_kernel(cfg, names, *refs):
    a = SimpleNamespace(**dict(zip(names, refs, strict=True)))
    seq, enc_len, slots, width = cfg.seq, cfg.enc_len, cfg.slots, cfg.width
    heads, levels, in_kernel = cfg.heads, cfg.levels, cfg.in_kernel
    inner = heads * HD
    if in_kernel:
        a.lands = [getattr(a, "land%d" % i) for i in range(levels)]
        a.holds = [getattr(a, "hold%d" % i) for i in range(levels - 1)]
    chunks = slots // CHUNK_SLOTS
    chunk_rows = CHUNK_SLOTS * seq
    half_rows = chunk_rows // 2
    half_width = width // 2
    quarter_width = width // 4
    me = lax.axis_index("tensor")
    core = lax.rem(me, 2)
    y = me // 2
    dp_me = lax.axis_index("dp")
    c_peer, y_peer = tensor_peer(1), tensor_peer(2)

    def rows_of(k, count):
        return pl.ds(pl.multiple_of(k * count, count), count)

    def load(index, src, dst):
        return pltpu.make_async_copy(src, dst, a.load_sem.at[index])

    load_x, load_g = load(0, a.inputs, a.x), load(1, a.out_grad, a.g3)
    loads = Weights(
        *(
            load(2 + i, getattr(a, name), getattr(a, "w_" + name))
            for i, name in enumerate(Weights._fields)
        )
    )
    load_x.start()
    for copy in loads[:4]:
        copy.start()

    def enc_copy(slot, buffer):
        rows = pl.ds(pl.multiple_of(slot * enc_len, enc_len), enc_len)
        return pltpu.make_async_copy(a.encoded.at[rows], a.enc.at[rows_of(buffer, enc_len)], a.enc_sem.at[buffer])

    enc_copy(0, 0).start()
    for copy in loads[4:]:
        copy.start()
    load_g.start()

    barrier = pltpu.get_barrier_semaphore()
    peers = [c_peer, y_peer] + [dp_peer(1 << k) for k in range(levels)]
    for peer in peers:
        pl.semaphore_signal(barrier, inc=1, device_id=peer, device_id_type=MESH)

    lane = lax.broadcasted_iota(jnp.int32, (1, inner), 1)
    masks = [jnp.where(lane // HD == h, 1.0, 0.0).astype(wide) for h in range(heads)]
    masks_low = [m.astype(low) for m in masks]
    row_i = lax.broadcasted_iota(jnp.int32, (seq, seq), 0)
    col_i = lax.broadcasted_iota(jnp.int32, (seq, seq), 1)
    for h in range(heads):
        line = jnp.broadcast_to(a.bias_line[h : h + 1, :], (seq, seq))
        turned = pltpu.roll(line, 0, 1, stride=1, stride_axis=0)
        a.bias[h * seq : (h + 1) * seq, :] = jnp.where(row_i >= col_i, turned, masked_score)
    a.table[...] = jnp.zeros_like(a.table)
    a.small[...] = jnp.zeros_like(a.small)

    def stack(rows):
        return jnp.concatenate([rows * m for m in masks_low], axis=0)

    def unstack(rows):
        return sum(rows[h * seq : (h + 1) * seq] * masks[h] for h in range(heads))

    def softmax(scores):
        peak = jnp.max(scores, axis=-1, keepdims=True)
        terms = jnp.exp(scores - peak)
        return (terms / jnp.sum(terms, axis=-1, keepdims=True)).astype(low)

    def own_rows(k):
        return pl.ds(pl.multiple_of(k * chunk_rows + core * half_rows, half_rows), half_rows)

    def other_rows(k):
        return pl.ds(pl.multiple_of(k * chunk_rows + (1 - core) * half_rows, half_rows), half_rows)

    def remote(src, dst, sems, index, peer):
        return pltpu.make_async_remote_copy(
            src_ref=src,
            dst_ref=dst,
            send_sem=sems.at[(0,) + index],
            recv_sem=sems.at[(1,) + index],
            device_id=peer,
            device_id_type=MESH,
        )

    def near_copy(p, k):
        return remote(a.part.at[other_rows(k)], a.near.at[k], a.near_sem, (p, k), c_peer)

    def far_copy(p, k):
        return remote(a.mine.at[k], a.far.at[p % 2, k], a.far_sem, (p, k), y_peer)

    def y_send(p, k):
        near_copy(p, k).wait()
        a.mine[k] = (a.part[own_rows(k)].astype(wide) + a.near[k].astype(wide)).astype(low)
        far_copy(p, k).start()

    def total(p, k):
        far_copy(p, k).wait()
        return a.mine[k].astype(wide) + a.far[p % 2, k].astype(wide)

    def share_copy(p, k, buffer):
        return remote(buffer.at[own_rows(k)], buffer.at[own_rows(k)], a.share_sem, (p, k), c_peer)

    def each_chunk(body):
        def step(k, carry):
            body(k)
            return carry

        lax.fori_loop(0, chunks, step, 0)

    def phase(p, finish, buffer, compute):
        def body(k):
            finish(k, total(p - 1, k))
            share_copy(p, k, buffer).start()

            @pl.when(k > 0)
            def _():
                y_send(p, k - 1)

            share_copy(p, k, buffer).wait()
            compute(k)
            near_copy(p, k).start()

        each_chunk(body)
        y_send(p, chunks - 1)

    def project(slot, buffer):
        enc_copy(slot, buffer).wait()

        @pl.when(slot + 1 < slots)
        def _():
            enc_copy(slot + 1, 1 - buffer).start()

        rows = rows_of(slot, enc_len)
        a.k2[rows] = dot(a.enc[rows_of(buffer, enc_len)], a.w_key_cross[...]).astype(low)
        a.v2[rows] = dot(a.enc[rows_of(buffer, enc_len)], a.w_value_cross[...]).astype(low)

    def self_forward(k):
        rows = rows_of(k, chunk_rows)
        x = a.x[rows].astype(wide)
        normed = (x * inverse_rms(x) * a.gain_self[...]).astype(low)
        a.n1[rows] = normed
        query = dot(normed, a.w_query_self[...]).astype(low)
        keys = dot(normed, a.w_key_self[...]).astype(low)
        values = dot(normed, a.w_value_self[...]).astype(low)
        a.q1[rows], a.k1[rows], a.v1[rows] = query, keys, values
        mixed = []
        for s in range(CHUNK_SLOTS):
            part = slice(s * seq, (s + 1) * seq)
            weights = softmax(dot_t(stack(query[part]), keys[part]) + a.bias[...])
            a.soft1[k * CHUNK_SLOTS + s] = weights
            mixed.append(unstack(dot(weights, values[part])).astype(low))
        mixed = jnp.concatenate(mixed, axis=0)
        a.o1[rows] = mixed
        a.part[rows] = dot_t(mixed, a.w_output_self[...]).astype(low)

    load_x.wait()
    for copy in loads[:4]:
        copy.wait()

    def phase_zero(k):
        self_forward(k)

        @pl.when(k == 0)
        def _():
            pl.semaphore_wait(barrier, len(peers))
            loads.key_cross.wait()
            loads.value_cross.wait()

        near_copy(0, k).start()
        project(CHUNK_SLOTS * k, 0)
        y_send(0, k)
        project(CHUNK_SLOTS * k + 1, 1)

    each_chunk(phase_zero)
    loads.query_cross.wait()
    loads.output_cross.wait()

    def finish_one(k, term):
        hidden = a.x[own_rows(k)].astype(wide) + term
        a.h1[k] = hidden
        a.n2[own_rows(k)] = (hidden * inverse_rms(hidden) * a.gain_cross[...]).astype(low)

    def cross_forward(k):
        rows = rows_of(k, chunk_rows)
        query = dot(a.n2[rows], a.w_query_cross[...]).astype(low)
        a.q2[rows] = query
        mixed = []
        for s in range(CHUNK_SLOTS):
            slot = k * CHUNK_SLOTS + s
            enc_rows = rows_of(slot, enc_len)
            weights = softmax(dot_t(stack(query[s * seq : (s + 1) * seq]), a.k2[enc_rows]))
            a.soft2[slot] = weights
            mixed.append(unstack(dot(weights, a.v2[enc_rows])).astype(low))
        mixed = jnp.concatenate(mixed, axis=0)
        a.o2[rows] = mixed
        a.part[rows] = dot_t(mixed, a.w_output_cross[...]).astype(low)

    phase(1, finish_one, a.n2, cross_forward)
    for copy in (loads.hidden_in, loads.hidden_out, load_g):
        copy.wait()

    def limit(slot):
        return jnp.where(slot < a.counts[0], a.lengths[slot], 0)

    def keep_rows(slot, rows):
        pos = lax.broadcasted_iota(jnp.int32, (seq, 1), 0)
        return jnp.where(pos < limit(slot), rows, 0.0)

    def finish_two(k, term):
        hidden = a.h1[k] + term
        a.h2[k] = hidden
        a.n3[own_rows(k)] = (hidden * inverse_rms(hidden) * a.gain_ffn[...]).astype(low)

    def out_near_copy(k):
        return remote(a.out_part.at[k % 2, 1 - core], a.out_near.at[k], a.out_near_sem, (k,), c_peer)

    def out_far_copy(k):
        return remote(a.out_mine.at[k, 1 - y], a.out_far.at[k], a.out_far_sem, (k,), y_peer)

    def out_send(k):
        out_near_copy(k).wait()
        term = a.out_part[k % 2, core].astype(wide) + a.out_near[k].astype(wide)
        a.out_mine[k, 0] = term[:, :half_width].astype(low)
        a.out_mine[k, 1] = term[:, half_width:].astype(low)
        out_far_copy(k).start()

    scale = 0.7978845608028654

    def feed_forward(k):
        rows = rows_of(k, chunk_rows)
        grad = jnp.concatenate(
            [
                keep_rows(k * CHUNK_SLOTS + s, a.g3[rows_of(k * CHUNK_SLOTS + s, seq)].astype(wide))
                for s in range(CHUNK_SLOTS)
            ],
            axis=0,
        ).astype(low)
        a.g3[rows] = grad
        a.pre[...] = dot(a.n3[rows], a.w_hidden_in[...])

        def gelu_rows(i, carry):
            part = rows_of(i, GELU_ROWS)
            pre = a.pre[part]
            square = pre * pre
            bend = jnp.tanh(scale * pre * (1.0 + 0.044715 * square))
            half = 0.5 * (1.0 + bend)
            curve = scale * (1.0 + 3 * 0.044715 * square)
            a.pre[part] = half + 0.5 * pre * (1.0 - bend * bend) * curve
            target = pl.ds(pl.multiple_of(k * chunk_rows + i * GELU_ROWS, GELU_ROWS), GELU_ROWS)
            a.act[target] = (pre * half).astype(low)
            return carry

        lax.fori_loop(0, chunk_rows // GELU_ROWS, gelu_rows, 0)
        out = dot_t(a.act[rows], a.w_hidden_out[...]).astype(low)
        a.out_part[k % 2, 0] = out[:half_rows]
        a.out_part[k % 2, 1] = out[half_rows:]
        out_near_copy(k).start()
        grad_pre = (a.pre[...] * dot(grad, a.w_hidden_out[...])).astype(low)
        a.d_pre[rows] = grad_pre
        a.part[rows] = dot_t(grad_pre, a.w_hidden_in[...]).astype(low)

    def feed_forward_sends(k):
        feed_forward(k)
        out_send(k)

    phase(2, finish_two, a.n3, feed_forward_sends)

    def column_copy(which, k):
        return remote(
            a.col_send.at[which, k], a.columns.at[which, own_rows(k)], a.col_sem, (which, k), c_peer
        )

    def emit_columns(which, k, value):
        left, right = value[:, :quarter_width], value[:, quarter_width:]
        first = core == 0
        a.columns[which, own_rows(k)] = jnp.where(first, left, right).astype(low)
        a.col_send[which, k] = jnp.where(first, right, left).astype(low)
        column_copy(which, k).start()

    def my_half(value):
        return jnp.where(y == 0, value[:, :half_width], value[:, half_width:])

    def finish_out(k):
        out_far_copy(k).wait()
        value = my_half(a.h2[k]) + a.out_mine[k, y].astype(wide) + a.out_far[k].astype(wide)
        emit_columns(0, k, keep_rows(k * CHUNK_SLOTS + core, value))

    def dp_rank(level):
        return (dp_me >> level) & 1

    def dp_copy(block, level):
        buffer = block % 2
        count = 1 << (levels - 1 - level)
        source = a.term if level == 0 else a.holds[level - 1]
        part = pl.ds((1 - dp_rank(level)) * count, count)
        return remote(
            source.at[buffer, part],
            a.lands[level].at[buffer],
            a.dp_sem,
            (block, level),
            dp_peer(1 << level),
        )

    def dp_begin(block):
        if in_kernel:
            if block >= 2:
                credit_wait(block, 0)
            dp_copy(block, 0).start()
        else:
            pltpu.make_async_copy(
                a.term.at[block % 2], a.raw_grads.at[block], a.dp_sem.at[0, block, 0]
            ).start()

    def credit_wait(block, level):
        pl.semaphore_wait(a.credit_sem.at[block % 2, level], 1)

    def dp_advance(block, level):
        if not in_kernel:
            return
        buffer = block % 2
        count = 1 << (levels - 1 - level)
        dp_copy(block, level).wait()
        source = a.term if level == 0 else a.holds[level - 1]
        land = a.lands[level]
        part = pl.ds(dp_rank(level) * count, count)
        value = source[buffer, part].astype(wide) + land[buffer].astype(wide)
        if level == levels - 1:
            emit_grads(block, value[0])
        else:
            a.holds[level][buffer] = value.astype(low)
        if block < 2:
            pl.semaphore_signal(
                a.credit_sem.at[buffer, level],
                inc=1,
                device_id=dp_peer(1 << level),
                device_id_type=MESH,
            )
        if level + 1 < levels:
            if block >= 2:
                credit_wait(block, level + 1)
            dp_copy(block, level + 1).start()

    def dp_finish_raw(block):
        if not in_kernel:
            pltpu.make_async_copy(
                a.term.at[block % 2], a.raw_grads.at[block], a.dp_sem.at[0, block, 0]
            ).wait()

    def emit_grads(block, value):
        if block == 0:
            a.grad_hidden_out[...] = value
        elif block == 1:
            a.grad_hidden_in[...] = value
        else:
            names = Weights._fields[4:8] if block == 2 else Weights._fields[:4]
            for i, name in enumerate(names):
                getattr(a, "grad_" + name)[...] = value[:, i * inner : (i + 1) * inner]

    piece = cfg.piece
    groups = 2
    group_rows = width // groups
    pieces_each = max(group_rows // piece, 1) if in_kernel else 1

    def store_pieces(block, g, rows):
        if in_kernel:
            for i in range(pieces_each):
                for gg in range(groups):
                    index = reversed_bits(gg * pieces_each + i, levels)
                    if gg == g:
                        a.term[block % 2, index] = rows[i * piece : (i + 1) * piece]
        else:
            a.term[block % 2, g * group_rows : (g + 1) * group_rows] = rows

    def plain_grads(block, left, right):
        for g in range(groups):
            columns = slice(g * group_rows, (g + 1) * group_rows)
            store_pieces(block, g, t_dot(left[:, columns], right[...]).astype(low))

    def turned_grads(block):
        for g in range(groups):
            columns = slice(g * group_rows, (g + 1) * group_rows)
            store_pieces(block, g, a.enc[all_turned, columns].T)

    def turned_rows(i):
        return slice(i * inner, (i + 1) * inner)

    all_turned = slice(0, 4 * inner)

    plain_grads(0, a.g3, a.act)
    dp_begin(0)
    plain_grads(1, a.n3, a.d_pre)
    dp_begin(1)

    def add_gain(index, value):
        a.small[index : index + 1, :] += value

    def finish_three(k, term):
        grad_rows, grad_gain = norm_back(a.h2[k], a.gain_ffn[...], term)
        add_gain(2, grad_gain)
        grad = a.g3[own_rows(k)].astype(wide) + grad_rows
        a.dh[k] = grad
        a.dh2[own_rows(k)] = grad.astype(low)
        finish_out(k)

    def score_back(soft, grad_soft):
        weights = soft.astype(wide)
        row_inner = jnp.sum(weights * grad_soft, axis=-1, keepdims=True)
        return (weights * (grad_soft - row_inner)).astype(low)

    def cross_backward(k):
        rows = rows_of(k, chunk_rows)
        grad_mixed = dot(a.dh2[rows], a.w_output_cross[...]).astype(low)
        query = a.q2[rows]
        grads = []
        for s in range(CHUNK_SLOTS):
            slot = k * CHUNK_SLOTS + s
            part = slice(s * seq, (s + 1) * seq)
            enc_rows = rows_of(slot, enc_len)
            tall_grad, tall_query = stack(grad_mixed[part]), stack(query[part])
            soft = a.soft2[slot]
            grad_scores = score_back(soft, dot_t(tall_grad, a.v2[enc_rows]))
            a.dkv[slot, :inner] = t_dot(tall_query, grad_scores).astype(low)
            a.dkv[slot, inner:] = t_dot(tall_grad, soft).astype(low)
            grads.append(unstack(dot(grad_scores, a.k2[enc_rows])).astype(low))
        grads = jnp.concatenate(grads, axis=0)
        a.q2[rows] = grads
        a.part[rows] = dot_t(grads, a.w_query_cross[...]).astype(low)

        @pl.when(k == 2)
        def _():
            dp_advance(0, 0)

    phase(3, finish_three, a.dh2, cross_backward)

    kv_blocks = 2 * inner // half_rows
    for i in range(kv_blocks):
        a.h2[i] = jnp.zeros_like(a.h2[i])

    def enc_slots(j, own):
        which = jnp.where(own == 1, core, 1 - core)
        side = jnp.where(j < 2, 1 - y, y)
        return 4 * side + 2 * which + lax.rem(j, 2)

    def enc_partial(slot, buffer):
        key_grad, value_grad = a.dkv[slot, :inner], a.dkv[slot, inner:]
        for i in range(kv_blocks):
            part = slice(i * half_rows, (i + 1) * half_rows)
            a.h2[i] += dot(a.dkv[slot, part], a.enc[rows_of(buffer, enc_len)])
        return dot_t(key_grad.T, a.w_key_cross[...]) + dot_t(value_grad.T, a.w_value_cross[...])

    def enc_half(j):
        return rows_of(lax.rem(j, 2), enc_len)

    def enc_near_copy(j):
        source = a.n3.at[enc_half(j)]
        target = a.act if j < 2 else a.d_pre
        return remote(source, target.at[enc_half(j)], a.enc_near_sem, (j,), c_peer)

    def enc_far_copy(j):
        return remote(a.g3.at[enc_half(j)], a.enc_far.at[j], a.enc_far_sem, (j,), y_peer)

    enc_copy(enc_slots(0, 0), 0).start()
    for j in range(4):
        enc_copy(enc_slots(j, 0), 0).wait()
        enc_copy(enc_slots(j, 1), 1).start()
        if j >= 2:
            enc_near_copy(j - 2).wait_send()
        a.n3[enc_half(j)] = enc_partial(enc_slots(j, 0), 0).astype(low)
        enc_near_copy(j).start()
        enc_copy(enc_slots(j, 1), 1).wait()
        if j < 3:
            enc_copy(enc_slots(j + 1, 0), 0).start()
        partial = enc_partial(enc_slots(j, 1), 1)
        enc_near_copy(j).wait_recv()
        if j < 2:
            a.g3[enc_half(j)] = (partial + a.act[enc_half(j)].astype(wide)).astype(low)
            enc_far_copy(j).start()
        else:
            a.enc_out[rows_of(j - 2, enc_len)] = (
                partial + a.d_pre[enc_half(j)].astype(wide)
            ).astype(low)
    dp_advance(1, 0)
    dp_advance(0, 1)

    a.enc[turned_rows(0)] = t_dot(a.q2[...], a.n2[...]).astype(low)
    for i in range(kv_blocks):
        a.enc[inner + i * half_rows : inner + (i + 1) * half_rows] = a.h2[i].astype(low)
    a.enc[turned_rows(3)] = t_dot(a.o2[...], a.dh2[...]).astype(low)
    dp_finish_raw(0)
    turned_grads(2)
    dp_begin(2)

    def finish_four(k, term):
        grad_rows, grad_gain = norm_back(a.h1[k], a.gain_cross[...], term)
        add_gain(1, grad_gain)
        grad = a.dh[k] + grad_rows
        a.dh[k] = grad
        a.dh1[own_rows(k)] = grad.astype(low)

    def self_backward(k):
        rows = rows_of(k, chunk_rows)
        grad_mixed = dot(a.dh1[rows], a.w_output_self[...]).astype(low)
        query, keys, values = a.q1[rows], a.k1[rows], a.v1[rows]
        grads = [[], [], []]
        for s in range(CHUNK_SLOTS):
            part = slice(s * seq, (s + 1) * seq)
            tall_grad, tall_query = stack(grad_mixed[part]), stack(query[part])
            soft = a.soft1[k * CHUNK_SLOTS + s]
            grad_scores = score_back(soft, dot_t(tall_grad, values[part]))
            a.table[...] += grad_scores.astype(wide)
            grads[0].append(unstack(dot(grad_scores, keys[part])).astype(low))
            grads[1].append(t_dot(grad_scores, tall_query).astype(low))
            grads[2].append(t_dot(soft, tall_grad).astype(low))
        grads = [jnp.concatenate(g, axis=0) for g in grads]
        a.q1[rows], a.k1[rows], a.v1[rows] = grads
        a.part[rows] = (
            dot_t(grads[0], a.w_query_self[...])
            + dot_t(grads[1], a.w_key_self[...])
            + dot_t(grads[2], a.w_value_self[...])
        ).astype(low)

    phase(4, finish_four, a.dh1, self_backward)
    dp_advance(1, 1)
    dp_advance(0, 2)
    dp_advance(1, 2)
    a.enc[turned_rows(0)] = t_dot(a.q1[...], a.n1[...]).astype(low)
    a.enc[turned_rows(1)] = t_dot(a.k1[...], a.n1[...]).astype(low)
    a.enc[turned_rows(2)] = t_dot(a.v1[...], a.n1[...]).astype(low)
    a.enc[turned_rows(3)] = t_dot(a.o1[...], a.dh1[...]).astype(low)
    dp_finish_raw(1)
    turned_grads(3)
    dp_begin(3)
    dp_advance(2, 0)

    def phase_five(k):
        grad_rows, grad_gain = norm_back(
            a.x[own_rows(k)].astype(wide), a.gain_self[...], total(4, k)
        )
        add_gain(0, grad_gain)
        emit_columns(1, k, my_half(a.dh[k] + grad_rows))

    each_chunk(phase_five)

    mirror = jnp.where(row_i + col_i == seq - 1, 1.0, 0.0).astype(wide)
    for h in range(heads):
        flipped = jnp.dot(
            a.table[h * seq : (h + 1) * seq, :],
            mirror,
            precision=highest,
            preferred_element_type=wide,
        )
        turned = pltpu.roll(flipped, 0, 1, stride=1, stride_axis=0)
        a.small[3:4, h * seq : (h + 1) * seq] = jnp.sum(turned, axis=0, keepdims=True)

    def small_copy(i):
        peer = c_peer if i == 0 else dp_peer(1 << (i - 1))
        return remote(a.small, a.small_land.at[i], a.small_sem, (i,), peer)

    small_copy(0).start()
    dp_advance(2, 1)
    small_copy(0).wait()
    row = lax.broadcasted_iota(jnp.int32, a.small.shape, 0)
    a.small[...] += jnp.where(row < 3, a.small_land[0], 0.0)
    for i in range(1, levels + 1):
        small_copy(i).start()
        if i == 1:
            dp_advance(3, 0)
        if i == 2:
            dp_advance(2, 2)
        small_copy(i).wait()
        a.small[...] += a.small_land[i]
    dp_advance(3, 1)
    dp_advance(3, 2)
    dp_finish_raw(2)
    dp_finish_raw(3)

    for j in range(2):
        enc_far_copy(j).wait()
        a.enc_out[rows_of(j, enc_len)] = (
            a.enc_out[rows_of(j, enc_len)].astype(wide) + a.enc_far[j].astype(wide)
        ).astype(low)
        enc_near_copy(2 + j).wait_send()
    for k in range(chunks):
        column_copy(0, k).wait()
        column_copy(1, k).wait()
    stores = [
        load(0, a.columns.at[0], a.layer_out),
        load(1, a.columns.at[1], a.input_grad),
        load(2, a.enc_out, a.encoded_grad),
    ]
    for store in stores:
        store.start()
    a.small_out[...] = a.small[...]
    for store in stores:
        store.wait()


def per_device(*args):
    (
        inputs,
        encoded,
        example_counts,
        lengths,
        buckets,
        gain_self,
        gain_cross,
        gain_ffn,
        bias_table,
    ) = args[:9]
    weights = args[9:19]
    out_grad = args[19]
    rows, width = inputs.shape
    seq = buckets.shape[0]
    slots = lengths.shape[0]
    enc_rows = encoded.shape[0]
    enc_len = enc_rows // slots
    inner = weights[0].shape[1]
    hidden = weights[8].shape[1]
    heads = inner // HD
    dp_count = lax.axis_size("dp")
    levels = dp_count.bit_length() - 1
    piece = width // dp_count
    in_kernel = piece % 16 == 0
    chunks = slots // CHUNK_SLOTS
    half = CHUNK_SLOTS * seq // 2

    bucket_table = (buckets[:, None] == jnp.arange(bias_table.shape[0])[None, :]).astype(wide)
    per_dist = jnp.dot(bucket_table, bias_table, precision=highest)
    bias_line = jnp.roll(per_dist[::-1], 1, axis=0).T

    ins = dict(
        lengths=(lengths, SM),
        counts=(example_counts, SM),
        gain_self=(gain_self[None], VM),
        gain_cross=(gain_cross[None], VM),
        gain_ffn=(gain_ffn[None], VM),
        bias_line=(bias_line, VM),
        inputs=(inputs, HBM),
        encoded=(encoded, HBM),
        out_grad=(out_grad, HBM),
    )
    for name, weight in zip(Weights._fields, weights, strict=True):
        ins[name] = (weight, HBM)
    shape = jax.ShapeDtypeStruct
    outs = dict(
        layer_out=(shape((rows, width // 4), low), HBM),
        input_grad=(shape((rows, width // 4), low), HBM),
        encoded_grad=(shape((enc_rows // 4, width), low), HBM),
        small_out=(shape((8, width), wide), VM),
    )
    if in_kernel:
        for name, weight in zip(Weights._fields, weights, strict=True):
            outs["grad_" + name] = (shape((piece, weight.shape[1]), wide), VM)
    else:
        outs.update(raw_grads=(shape((4, width, width), low), HBM))
    vmem, dma = pltpu.VMEM, pltpu.SemaphoreType.DMA
    quarter = width // 4
    whole_rows = vmem((rows, width), low)
    hidden_rows = vmem((rows, hidden), low)
    inner_rows = vmem((rows, inner), low)
    own_wide = vmem((chunks, half, width), wide)
    own_low = vmem((chunks, half, width), low)
    scratch = {
        "w_" + name: vmem(weight.shape, low)
        for name, weight in zip(Weights._fields, weights, strict=True)
    }
    scratch.update(
        x=whole_rows,
        g3=whole_rows,
        enc=vmem((2 * enc_len, width), low),
        n1=whole_rows,
        n2=whole_rows,
        n3=whole_rows,
        dh1=whole_rows,
        dh2=whole_rows,
        part=whole_rows,
        act=hidden_rows,
        d_pre=hidden_rows,
        q1=inner_rows,
        k1=inner_rows,
        v1=inner_rows,
        o1=inner_rows,
        q2=inner_rows,
        o2=inner_rows,
        k2=vmem((enc_rows, inner), low),
        v2=vmem((enc_rows, inner), low),
        h1=own_wide,
        h2=own_wide,
        dh=own_wide,
        soft1=vmem((slots, heads * seq, seq), low),
        soft2=vmem((slots, heads * seq, enc_len), low),
        dkv=vmem((slots, 2 * inner, enc_len), low),
        near=own_low,
        mine=own_low,
        far=vmem((2, chunks, half, width), low),
        out_part=vmem((2, 2, half, width), low),
        out_near=own_low,
        out_mine=vmem((chunks, 2, half, width // 2), low),
        out_far=vmem((chunks, half, width // 2), low),
        columns=vmem((2, rows, quarter), low),
        col_send=vmem((2, chunks, half, quarter), low),
        enc_far=vmem((2, enc_len, width), low),
        enc_out=vmem((enc_rows // 4, width), low),
        pre=vmem((CHUNK_SLOTS * seq, hidden), wide),
        bias=vmem((heads * seq, seq), wide),
        table=vmem((heads * seq, seq), wide),
        small=vmem((8, width), wide),
        small_land=vmem((levels + 1, 8, width), wide),
        load_sem=dma((2 + len(weights),)),
        enc_sem=dma((2,)),
        near_sem=dma((2, 5, chunks)),
        far_sem=dma((2, 5, chunks)),
        share_sem=dma((2, 5, chunks)),
        out_near_sem=dma((2, chunks)),
        out_far_sem=dma((2, chunks)),
        col_sem=dma((2, 2, chunks)),
        enc_near_sem=dma((2, 4)),
        enc_far_sem=dma((2, 2)),
        dp_sem=dma((2, 4, levels)),
        small_sem=dma((2, levels + 1)),
        credit_sem=pltpu.SemaphoreType.REGULAR((2, levels)),
    )
    if in_kernel:
        scratch.update(term=vmem((2, dp_count, piece, width), low))
        for level in range(levels):
            count = 1 << (levels - 1 - level)
            scratch["land%d" % level] = vmem((2, count, piece, width), low)
            if level + 1 < levels:
                scratch["hold%d" % level] = vmem((2, count, piece, width), low)
    else:
        scratch.update(term=vmem((2, width, width), low))
    cfg = SimpleNamespace(
        seq=seq,
        enc_len=enc_len,
        slots=slots,
        width=width,
        heads=heads,
        levels=levels,
        in_kernel=in_kernel,
        piece=piece,
    )
    results = pl.pallas_call(
        functools.partial(layer_kernel, cfg, tuple(ins) + tuple(outs) + tuple(scratch)),
        out_shape=tuple(o[0] for o in outs.values()),
        in_specs=[i[1] for i in ins.values()],
        out_specs=tuple(o[1] for o in outs.values()),
        scratch_shapes=list(scratch.values()),
        compiler_params=pltpu.CompilerParams(
            collective_id=1, has_side_effects=True, vmem_limit_bytes=63 * 2**20
        ),
    )(*[i[0] for i in ins.values()])
    out = SimpleNamespace(**dict(zip(outs, results, strict=True)))
    small = out.small_out
    dist_sums = jnp.roll(small[3, : heads * seq].reshape(heads, seq), 1, axis=1)
    table_grad = jnp.dot(dist_sums, bucket_table, precision=highest).T
    if in_kernel:
        grads = [getattr(out, "grad_" + name) for name in Weights._fields]
    else:
        raw = out.raw_grads
        parts = [raw[3][:, i * inner : (i + 1) * inner] for i in range(4)]
        parts += [raw[2][:, i * inner : (i + 1) * inner] for i in range(4)]
        grads = [
            lax.psum_scatter(part.astype(wide), "dp", scatter_dimension=0, tiled=True)
            for part in (*parts, raw[1], raw[0])
        ]
    return (
        out.layer_out,
        out.input_grad,
        out.encoded_grad,
        small[0],
        small[1],
        small[2],
        table_grad,
        *grads,
    )


def solution(mesh):
    columns = P(None, "tensor")
    both = P("dp", "tensor")
    placed = (
        (P("dp", None), P("dp", None), P("dp"), P("dp"), P(), P(), P(), P())
        + (columns,) * 11
        + (P("dp", None),)
    )
    return jax.shard_map(
        per_device,
        mesh=mesh,
        in_specs=placed,
        out_specs=(both, both, P(("dp", "tensor"), None), P(), P(), P(), columns) + (both,) * 10,
        check_vma=False,
    )
```

time: 1180 us -> 198 us (0.17)
  waiting for transfers between devices: 887 us -> 0 us
  Pallas kernels: 0 us -> 166 us
  matrix products: 120 us -> 1.65 us
  local copies, waits for them, and re-layouts: 75.7 us -> 27.5 us
  other arithmetic: 40 us -> 0.72 us
  blocking collectives: 37.6 us -> 0 us
  between operations: 16 us -> 1.51 us
    reduce_scatter x9 -> x0, waiting for transfers between devices: 556 us -> none  [the longest x1 72.4 us: per_device(): lax.psum_scatter(grad_hidden_out, 'dp', scatter_dimension=0, tiled=True)]
    psum x5 -> x0, waiting for transfers between devices: 200 us -> none  [the longest x2 115 us: branch_total(): return lax.psum(term, 'tensor')]
    pallas_call x0 -> x1, Pallas kernels: none -> 166 us  [per_device(): pl.pallas_call(functools.partial(layer_kernel, cfg, tuple(ins) + tuple(ou...]
    unnamed x20 -> x0, waiting for transfers between devices: 131 us -> none
    dot_general x61 -> x1, matrix products: 119 us -> 0.8 us  [per_device(): table_grad = jnp.dot(dist_sums, bucket_table, precision=highest).T]
    psum x1 -> x0, blocking collectives: 37.6 us -> none  [per_device(): lax.psum((grad_gain_one, grad_gain_two, grad_gain_three, table_grad), 'dp')]
    reshape x16 -> x0, local copies, waits for them, and re-layouts: 25 us -> none  [the longest x8 11.9 us: to_blocks(): return flat.reshape(block_count, GROUP, length, heads_local, HD)]
    reduce_sum x13 -> x0, other arithmetic: 21.8 us -> none  [the longest x3 11.3 us: rms_backward(): grad_gain = jnp.sum(grad_normed * row_data * inverse, axis=0)]
  transfers between devices with their start and end apart: 17 -> 0, of which waited for: 15 -> 0; matrix products, arithmetic and copies ran while one was open for 8% -> 0% of each run, Pallas kernels for 0% -> 0%
where the time goes in v2:
time: 198 us; the launch traced here: 197 us
  Pallas kernels  166 us (84%)
  local copies, waits for them, and re-layouts  27.5 us (14%)
    pallas_call x1, Pallas kernels, per_device(): pl.pallas_call(functools.partial(layer_kernel, cfg, tuple(ins) + tuple(ou...  166 us
    unnamed x59, local copies, waits for them, and re-layouts  21.2 us

profile of v2, /device:TPU:0, one launch (start us, length us, event | category | flops | bytes accessed | tf_op | source)
XLA Modules:
  0.0 197.2 jit_solution(392651733429055362)
XLA Ops:
  1.4 0.8 fusion.1
  2.5 0.7 maximum_bitcast_fusion.refs_5_
  3.2 1.3 broadcast_in_dim.11.refs_2_
  4.4 1.3 broadcast_in_dim.12.refs_3_
  5.7 1.3 broadcast_in_dim.13.refs_4_
  7.0 1.9 copy.37.refs_9_
  8.9 1.9 copy.38.refs_10_
  10.8 0.9 copy.39.refs_11_
  11.8 0.9 copy.40.refs_12_
  12.7 0.9 copy.41.refs_13_
  13.6 0.9 copy.42.refs_14_
  14.5 0.9 copy.43.refs_15_
  15.5 0.9 copy.44.refs_16_
  16.4 165.9 %shard_map.323 = (bf16[1024,192]{1,0:T(8,128)(2,1)}, bf16[1024,192]{1,0:T(8,128)(2,1)}, bf16[1024,768]{1,0:T(8,128)(2,1)}, f32[8,768]{1,0:T(8,128)}, f32[96,192]...) custom-call(s32[8]{0:T(128)} %refs_0_.1, ...), custom_call_target="tpu_custom_call" | custom-call | tf_op jit(solution)/shard_map/pallas_call | solution.py:822
  182.3 2.1 %copy.45 = bf16[1024,192]{0,1:T(8,128)(2,1)} copy(bf16[1024,192]{1,0:T(8,128)(2,1)} %get-tuple-element.45) | data formatting | bytes 786432
  184.4 0.7 slice_reduce_fusion.3
  185.1 1.5 slice_reduce_fusion
  186.6 0.8 fusion
  187.4 2.0 %copy.46 = bf16[1024,192]{0,1:T(8,128)(2,1)} copy(bf16[1024,192]{1,0:T(8,128)(2,1)} %get-tuple-element.46) | data formatting | bytes 786432
  189.5 1.1 copy.59
  190.6 0.6 copy.60
  193.2 0.6 copy.64
  195.8 0.7 copy.68
  196.5 0.7 copy.69
  (47 shorter events, 4.2 us)
Async XLA Ops:
  0.7 0.8 copy-start
  0.7 12.0 %copy-start.6 = (bf16[768,192]{0,1:T(8,128)(2,1)S(1)}, bf16[768,192]{0,1:T(8,128)(2,1)}, u32[]{:S(2)}) copy-start(bf16[768,192]{0,1:T(8,128)(2,1)} %param.33) | copy-start | bytes 884740
  0.7 11.1 %copy-start.5 = (bf16[768,192]{0,1:T(8,128)(2,1)S(1)}, bf16[768,192]{0,1:T(8,128)(2,1)}, u32[]{:S(2)}) copy-start(bf16[768,192]{0,1:T(8,128)(2,1)} %param.32) | copy-start | bytes 884740
  0.7 10.1 %copy-start.4 = (bf16[768,192]{0,1:T(8,128)(2,1)S(1)}, bf16[768,192]{0,1:T(8,128)(2,1)}, u32[]{:S(2)}) copy-start(bf16[768,192]{0,1:T(8,128)(2,1)} %param.31) | copy-start | bytes 884740
  7.0 6.6 %copy-start.7 = (bf16[768,192]{0,1:T(8,128)(2,1)S(1)}, bf16[768,192]{0,1:T(8,128)(2,1)}, u32[]{:S(2)}) copy-start(bf16[768,192]{0,1:T(8,128)(2,1)} %param.34) | copy-start | bytes 884740
  8.9 5.6 %copy-start.8 = (bf16[768,192]{0,1:T(8,128)(2,1)S(1)}, bf16[768,192]{0,1:T(8,128)(2,1)}, u32[]{:S(2)}) copy-start(bf16[768,192]{0,1:T(8,128)(2,1)} %param.35) | copy-start | bytes 884740
  10.8 4.6 %copy-start.9 = (bf16[768,192]{0,1:T(8,128)(2,1)S(1)}, bf16[768,192]{0,1:T(8,128)(2,1)}, u32[]{:S(2)}) copy-start(bf16[768,192]{0,1:T(8,128)(2,1)} %param.36) | copy-start | bytes 884740
  16.4 170.3 %copy-start.18 = (s32[128]{0:T(128)S(1)}, s32[128]{0:T(128)}, u32[]{:S(2)}) copy-start(s32[128]{0:T(128)} %param.24) | copy-start | bytes 1540
  182.2 7.2 %copy-start.1 = (bf16[1024,768]{1,0:T(8,128)(2,1)S(1)}, bf16[1024,768]{1,0:T(8,128)(2,1)}, u32[]{:S(2)}) copy-start(bf16[1024,768]{1,0:T(8,128)(2,1)} %get-tuple-element.84) | copy-start | bytes 4718596
  189.4 1.2 copy-start.17
  189.4 1.9 copy-start.16
  189.4 2.5 %copy-start.15 = (f32[96,192]{1,0:T(8,128)S(1)}, f32[96,192]{1,0:T(8,128)}, u32[]{:S(2)}) copy-start(f32[96,192]{1,0:T(8,128)} %get-tuple-element.91) | copy-start | bytes 221188
  189.4 3.1 %copy-start.14 = (f32[96,192]{1,0:T(8,128)S(1)}, f32[96,192]{1,0:T(8,128)}, u32[]{:S(2)}) copy-start(f32[96,192]{1,0:T(8,128)} %get-tuple-element.92) | copy-start | bytes 221188
  189.4 3.8 %copy-start.13 = (f32[96,192]{1,0:T(8,128)S(1)}, f32[96,192]{1,0:T(8,128)}, u32[]{:S(2)}) copy-start(f32[96,192]{1,0:T(8,128)} %get-tuple-element.93) | copy-start | bytes 221188
  189.4 4.4 %copy-start.12 = (f32[96,192]{1,0:T(8,128)S(1)}, f32[96,192]{1,0:T(8,128)}, u32[]{:S(2)}) copy-start(f32[96,192]{1,0:T(8,128)} %get-tuple-element.94) | copy-start | bytes 221188
  189.4 5.0 %copy-start.11 = (f32[96,192]{1,0:T(8,128)S(1)}, f32[96,192]{1,0:T(8,128)}, u32[]{:S(2)}) copy-start(f32[96,192]{1,0:T(8,128)} %get-tuple-element.95) | copy-start | bytes 221188
  189.5 5.7 %copy-start.10 = (f32[96,192]{1,0:T(8,128)S(1)}, f32[96,192]{1,0:T(8,128)}, u32[]{:S(2)}) copy-start(f32[96,192]{1,0:T(8,128)} %get-tuple-element.96) | copy-start | bytes 221188
  190.6 5.2 %copy-start.3 = (f32[96,768]{1,0:T(8,128)S(1)}, f32[96,768]{1,0:T(8,128)}, u32[]{:S(2)}) copy-start(f32[96,768]{1,0:T(8,128)} %get-tuple-element.97) | copy-start | bytes 884740
  190.6 5.9 %copy-start.2 = (f32[96,768]{1,0:T(8,128)S(1)}, f32[96,768]{1,0:T(8,128)}, u32[]{:S(2)}) copy-start(f32[96,768]{1,0:T(8,128)} %get-tuple-element.98) | copy-start | bytes 884740

commit v3 on v2

--- a/solution.py
+++ b/solution.py
@@ -34,6 +34,10 @@
 
 def t_dot(left, right):
     return lax.dot_general(left, right, (((0,), (0,)), ((), ())), preferred_element_type=wide)
+
+
+def exact_dot(left, right):
+    return jnp.dot(left, right, precision=highest, preferred_element_type=wide)
 
 
 def inverse_rms(rows):
@@ -123,13 +127,22 @@
     for peer in peers:
         pl.semaphore_signal(barrier, inc=1, device_id=peer, device_id_type=MESH)
 
+    gain_self, gain_cross, gain_ffn = (
+        ref[...].reshape(1, width) for ref in (a.gain_self, a.gain_cross, a.gain_ffn)
+    )
+
     lane = lax.broadcasted_iota(jnp.int32, (1, inner), 1)
     masks = [jnp.where(lane // HD == h, 1.0, 0.0).astype(wide) for h in range(heads)]
     masks_low = [m.astype(low) for m in masks]
     row_i = lax.broadcasted_iota(jnp.int32, (seq, seq), 0)
     col_i = lax.broadcasted_iota(jnp.int32, (seq, seq), 1)
+    bucket = lax.broadcasted_iota(jnp.int32, (a.table_in.shape[1], seq), 0)
+    chosen = jnp.where(a.buckets[...] == bucket, 1.0, 0.0).astype(wide)
+    per_dist = exact_dot(a.table_in[...], chosen)
+    backward = jnp.where((row_i + col_i) % seq == 0, 1.0, 0.0).astype(wide)
+    lines = exact_dot(per_dist, backward)
     for h in range(heads):
-        line = jnp.broadcast_to(a.bias_line[h : h + 1, :], (seq, seq))
+        line = jnp.broadcast_to(lines[h : h + 1, :], (seq, seq))
         turned = pltpu.roll(line, 0, 1, stride=1, stride_axis=0)
         a.bias[h * seq : (h + 1) * seq, :] = jnp.where(row_i >= col_i, turned, masked_score)
     a.table[...] = jnp.zeros_like(a.table)
@@ -211,17 +224,17 @@
             enc_copy(slot + 1, 1 - buffer).start()
 
         rows = rows_of(slot, enc_len)
-        a.k2[rows] = dot(a.enc[rows_of(buffer, enc_len)], a.w_key_cross[...]).astype(low)
-        a.v2[rows] = dot(a.enc[rows_of(buffer, enc_len)], a.w_value_cross[...]).astype(low)
+        a.k2[rows] = dot_t(a.enc[rows_of(buffer, enc_len)], a.w_key_cross[...]).astype(low)
+        a.v2[rows] = dot_t(a.enc[rows_of(buffer, enc_len)], a.w_value_cross[...]).astype(low)
 
     def self_forward(k):
         rows = rows_of(k, chunk_rows)
         x = a.x[rows].astype(wide)
-        normed = (x * inverse_rms(x) * a.gain_self[...]).astype(low)
+        normed = (x * inverse_rms(x) * gain_self).astype(low)
         a.n1[rows] = normed
-        query = dot(normed, a.w_query_self[...]).astype(low)
-        keys = dot(normed, a.w_key_self[...]).astype(low)
-        values = dot(normed, a.w_value_self[...]).astype(low)
+        query = dot_t(normed, a.w_query_self[...]).astype(low)
+        keys = dot_t(normed, a.w_key_self[...]).astype(low)
+        values = dot_t(normed, a.w_value_self[...]).astype(low)
         a.q1[rows], a.k1[rows], a.v1[rows] = query, keys, values
         mixed = []
         for s in range(CHUNK_SLOTS):
@@ -231,7 +244,7 @@
             mixed.append(unstack(dot(weights, values[part])).astype(low))
         mixed = jnp.concatenate(mixed, axis=0)
         a.o1[rows] = mixed
-        a.part[rows] = dot_t(mixed, a.w_output_self[...]).astype(low)
+        a.part[rows] = dot(mixed, a.w_output_self[...]).astype(low)
 
     load_x.wait()
     for copy in loads[:4]:
@@ -258,11 +271,11 @@
     def finish_one(k, term):
         hidden = a.x[own_rows(k)].astype(wide) + term
         a.h1[k] = hidden
-        a.n2[own_rows(k)] = (hidden * inverse_rms(hidden) * a.gain_cross[...]).astype(low)
+        a.n2[own_rows(k)] = (hidden * inverse_rms(hidden) * gain_cross).astype(low)
 
     def cross_forward(k):
         rows = rows_of(k, chunk_rows)
-        query = dot(a.n2[rows], a.w_query_cross[...]).astype(low)
+        query = dot_t(a.n2[rows], a.w_query_cross[...]).astype(low)
         a.q2[rows] = query
         mixed = []
         for s in range(CHUNK_SLOTS):
@@ -273,7 +286,7 @@
             mixed.append(unstack(dot(weights, a.v2[enc_rows])).astype(low))
         mixed = jnp.concatenate(mixed, axis=0)
         a.o2[rows] = mixed
-        a.part[rows] = dot_t(mixed, a.w_output_cross[...]).astype(low)
+        a.part[rows] = dot(mixed, a.w_output_cross[...]).astype(low)
 
     phase(1, finish_one, a.n2, cross_forward)
     for copy in (loads.hidden_in, loads.hidden_out, load_g):
@@ -289,7 +302,7 @@
     def finish_two(k, term):
         hidden = a.h1[k] + term
         a.h2[k] = hidden
-        a.n3[own_rows(k)] = (hidden * inverse_rms(hidden) * a.gain_ffn[...]).astype(low)
+        a.n3[own_rows(k)] = (hidden * inverse_rms(hidden) * gain_ffn).astype(low)
 
     def out_near_copy(k):
         return remote(a.out_part.at[k % 2, 1 - core], a.out_near.at[k], a.out_near_sem, (k,), c_peer)
@@ -347,13 +360,18 @@
 
     def column_copy(which, k):
         return remote(
-            a.col_send.at[which, k], a.columns.at[which, own_rows(k)], a.col_sem, (which, k), c_peer
+            a.col_send.at[which, k],
+            a.columns.at[which, :, own_rows(k)],
+            a.col_sem,
+            (which, k),
+            c_peer,
         )
 
     def emit_columns(which, k, value):
-        left, right = value[:, :quarter_width], value[:, quarter_width:]
+        value = value.T
+        left, right = value[:quarter_width], value[quarter_width:]
         first = core == 0
-        a.columns[which, own_rows(k)] = jnp.where(first, left, right).astype(low)
+        a.columns[which, :, own_rows(k)] = jnp.where(first, left, right).astype(low)
         a.col_send[which, k] = jnp.where(first, right, left).astype(low)
         column_copy(which, k).start()
 
@@ -475,7 +493,7 @@
         a.small[index : index + 1, :] += value
 
     def finish_three(k, term):
-        grad_rows, grad_gain = norm_back(a.h2[k], a.gain_ffn[...], term)
+        grad_rows, grad_gain = norm_back(a.h2[k], gain_ffn, term)
         add_gain(2, grad_gain)
         grad = a.g3[own_rows(k)].astype(wide) + grad_rows
         a.dh[k] = grad
@@ -489,7 +507,7 @@
 
     def cross_backward(k):
         rows = rows_of(k, chunk_rows)
-        grad_mixed = dot(a.dh2[rows], a.w_output_cross[...]).astype(low)
+        grad_mixed = dot_t(a.dh2[rows], a.w_output_cross[...]).astype(low)
         query = a.q2[rows]
         grads = []
         for s in range(CHUNK_SLOTS):
@@ -504,7 +522,7 @@
             grads.append(unstack(dot(grad_scores, a.k2[enc_rows])).astype(low))
         grads = jnp.concatenate(grads, axis=0)
         a.q2[rows] = grads
-        a.part[rows] = dot_t(grads, a.w_query_cross[...]).astype(low)
+        a.part[rows] = dot(grads, a.w_query_cross[...]).astype(low)
 
         @pl.when(k == 2)
         def _():
@@ -526,7 +544,7 @@
         for i in range(kv_blocks):
             part = slice(i * half_rows, (i + 1) * half_rows)
             a.h2[i] += dot(a.dkv[slot, part], a.enc[rows_of(buffer, enc_len)])
-        return dot_t(key_grad.T, a.w_key_cross[...]) + dot_t(value_grad.T, a.w_value_cross[...])
+        return t_dot(key_grad, a.w_key_cross[...]) + t_dot(value_grad, a.w_value_cross[...])
 
     def enc_half(j):
         return rows_of(lax.rem(j, 2), enc_len)
@@ -571,7 +589,7 @@
     dp_begin(2)
 
     def finish_four(k, term):
-        grad_rows, grad_gain = norm_back(a.h1[k], a.gain_cross[...], term)
+        grad_rows, grad_gain = norm_back(a.h1[k], gain_cross, term)
         add_gain(1, grad_gain)
         grad = a.dh[k] + grad_rows
         a.dh[k] = grad
@@ -579,7 +597,7 @@
 
     def self_backward(k):
         rows = rows_of(k, chunk_rows)
-        grad_mixed = dot(a.dh1[rows], a.w_output_self[...]).astype(low)
+        grad_mixed = dot_t(a.dh1[rows], a.w_output_self[...]).astype(low)
         query, keys, values = a.q1[rows], a.k1[rows], a.v1[rows]
         grads = [[], [], []]
         for s in range(CHUNK_SLOTS):
@@ -594,9 +612,9 @@
         grads = [jnp.concatenate(g, axis=0) for g in grads]
         a.q1[rows], a.k1[rows], a.v1[rows] = grads
         a.part[rows] = (
-            dot_t(grads[0], a.w_query_self[...])
-            + dot_t(grads[1], a.w_key_self[...])
-            + dot_t(grads[2], a.w_value_self[...])
+            dot(grads[0], a.w_query_self[...])
+            + dot(grads[1], a.w_key_self[...])
+            + dot(grads[2], a.w_value_self[...])
         ).astype(low)
 
     phase(4, finish_four, a.dh1, self_backward)
@@ -614,7 +632,7 @@
 
     def phase_five(k):
         grad_rows, grad_gain = norm_back(
-            a.x[own_rows(k)].astype(wide), a.gain_self[...], total(4, k)
+            a.x[own_rows(k)].astype(wide), gain_self, total(4, k)
         )
         add_gain(0, grad_gain)
         emit_columns(1, k, my_half(a.dh[k] + grad_rows))
@@ -623,12 +641,7 @@
 
     mirror = jnp.where(row_i + col_i == seq - 1, 1.0, 0.0).astype(wide)
     for h in range(heads):
-        flipped = jnp.dot(
-            a.table[h * seq : (h + 1) * seq, :],
-            mirror,
-            precision=highest,
-            preferred_element_type=wide,
-        )
+        flipped = exact_dot(a.table[h * seq : (h + 1) * seq, :], mirror)
         turned = pltpu.roll(flipped, 0, 1, stride=1, stride_axis=0)
         a.small[3:4, h * seq : (h + 1) * seq] = jnp.sum(turned, axis=0, keepdims=True)
 
@@ -673,6 +686,34 @@
     a.small_out[...] = a.small[...]
     for store in stores:
         store.wait()
+
+
+def finish_kernel(count, heads, seq, *refs):
+    small, buckets = refs[count], refs[count + 1]
+    targets, held, sems = refs[count + 2 : 2 * count + 6], refs[2 * count + 6 : -1], refs[-1]
+    copies = [pltpu.make_async_copy(refs[i], held[i], sems.at[i]) for i in range(count)]
+    for copy in copies:
+        copy.start()
+    for i in range(count):
+        copies[i].wait()
+        copies[i] = pltpu.make_async_copy(held[i], targets[i], sems.at[i])
+        copies[i].start()
+    for i in range(3):
+        targets[count + i][...] = small[i, :]
+    sums = jnp.concatenate([small[3:4, h * seq : (h + 1) * seq] for h in range(heads)], axis=0)
+    by_lane = pltpu.roll(jnp.broadcast_to(buckets[...], (8, seq)), seq - 1, 1)[:1]
+    kinds = targets[count + 3].shape[1]
+    bucket = lax.broadcasted_iota(jnp.int32, (kinds, seq), 0)
+    chosen = jnp.where(by_lane == bucket, 1.0, 0.0).astype(wide)
+    targets[count + 3][...] = lax.dot_general(
+        sums,
+        chosen,
+        (((1,), (1,)), ((), ())),
+        precision=highest,
+        preferred_element_type=wide,
+    )
+    for copy in copies:
+        copy.wait()
 
 
 def per_device(*args):
@@ -704,27 +745,26 @@
     chunks = slots // CHUNK_SLOTS
     half = CHUNK_SLOTS * seq // 2
 
-    bucket_table = (buckets[:, None] == jnp.arange(bias_table.shape[0])[None, :]).astype(wide)
-    per_dist = jnp.dot(bucket_table, bias_table, precision=highest)
-    bias_line = jnp.roll(per_dist[::-1], 1, axis=0).T
-
     ins = dict(
         lengths=(lengths, SM),
         counts=(example_counts, SM),
-        gain_self=(gain_self[None], VM),
-        gain_cross=(gain_cross[None], VM),
-        gain_ffn=(gain_ffn[None], VM),
-        bias_line=(bias_line, VM),
+        gain_self=(gain_self, VM),
+        gain_cross=(gain_cross, VM),
+        gain_ffn=(gain_ffn, VM),
+        table_in=(bias_table.T, VM),
+        buckets=(buckets[None], VM),
         inputs=(inputs, HBM),
         encoded=(encoded, HBM),
         out_grad=(out_grad, HBM),
     )
     for name, weight in zip(Weights._fields, weights, strict=True):
         ins[name] = (weight, HBM)
+    for name in Weights._fields[:8]:
+        ins[name] = (ins[name][0].T, HBM)
     shape = jax.ShapeDtypeStruct
     outs = dict(
-        layer_out=(shape((rows, width // 4), low), HBM),
-        input_grad=(shape((rows, width // 4), low), HBM),
+        layer_out=(shape((width // 4, rows), low), HBM),
+        input_grad=(shape((width // 4, rows), low), HBM),
         encoded_grad=(shape((enc_rows // 4, width), low), HBM),
         small_out=(shape((8, width), wide), VM),
     )
@@ -741,8 +781,7 @@
     own_wide = vmem((chunks, half, width), wide)
     own_low = vmem((chunks, half, width), low)
     scratch = {
-        "w_" + name: vmem(weight.shape, low)
-        for name, weight in zip(Weights._fields, weights, strict=True)
+        "w_" + name: vmem(ins[name][0].shape, low) for name in Weights._fields
     }
     scratch.update(
         x=whole_rows,
@@ -777,8 +816,8 @@
         out_near=own_low,
         out_mine=vmem((chunks, 2, half, width // 2), low),
         out_far=vmem((chunks, half, width // 2), low),
-        columns=vmem((2, rows, quarter), low),
-        col_send=vmem((2, chunks, half, quarter), low),
+        columns=vmem((2, quarter, rows), low),
+        col_send=vmem((2, chunks, quarter, half), low),
         enc_far=vmem((2, enc_len, width), low),
         enc_out=vmem((enc_rows // 4, width), low),
         pre=vmem((CHUNK_SLOTS * seq, hidden), wide),
@@ -829,30 +868,35 @@
             collective_id=1, has_side_effects=True, vmem_limit_bytes=63 * 2**20
         ),
     )(*[i[0] for i in ins.values()])
-    out = SimpleNamespace(**dict(zip(outs, results, strict=True)))
-    small = out.small_out
-    dist_sums = jnp.roll(small[3, : heads * seq].reshape(heads, seq), 1, axis=1)
-    table_grad = jnp.dot(dist_sums, bucket_table, precision=highest).T
+    moved = [i for i, name in enumerate(outs) if name not in ("small_out", "raw_grads")]
+    buckets_row = buckets[None]
+    kinds = bias_table.shape[0]
+    finals = pl.pallas_call(
+        functools.partial(finish_kernel, len(moved), heads, seq),
+        out_shape=(
+            *(shape(results[i].shape, results[i].dtype) for i in moved),
+            *(shape((width,), wide) for _ in range(3)),
+            shape((heads, kinds), wide),
+        ),
+        in_specs=[HBM] * len(moved) + [VM, VM],
+        out_specs=(HBM,) * len(moved) + (VM,) * 4,
+        scratch_shapes=[
+            *(vmem(results[i].shape, results[i].dtype) for i in moved),
+            dma((len(moved),)),
+        ],
+    )(*[results[i] for i in moved], results[3], buckets_row)
     if in_kernel:
-        grads = [getattr(out, "grad_" + name) for name in Weights._fields]
+        grads = finals[3 : len(moved)]
     else:
-        raw = out.raw_grads
+        raw = results[4]
         parts = [raw[3][:, i * inner : (i + 1) * inner] for i in range(4)]
         parts += [raw[2][:, i * inner : (i + 1) * inner] for i in range(4)]
         grads = [
             lax.psum_scatter(part.astype(wide), "dp", scatter_dimension=0, tiled=True)
             for part in (*parts, raw[1], raw[0])
         ]
-    return (
-        out.layer_out,
-        out.input_grad,
-        out.encoded_grad,
-        small[0],
-        small[1],
-        small[2],
-        table_grad,
-        *grads,
-    )
+    gains = finals[len(moved) : len(moved) + 3]
+    return (finals[0].T, finals[1].T, finals[2], *gains, finals[-1].T, *grads)
 
 
 def solution(mesh):

time: 198 us -> 172 us (0.87)
  local copies, waits for them, and re-layouts: 27.5 us -> 0 us
  Pallas kernels: 166 us -> 170 us
    unnamed x59 -> x0, local copies, waits for them, and re-layouts: 21.2 us -> none
    pallas_call x0 -> x1, Pallas kernels: none -> 4.74 us  [per_device(): pl.pallas_call(functools.partial(finish_kernel, len(moved), heads, seq),...]
    broadcast_in_dim x3 -> x0, local copies, waits for them, and re-layouts: 3.8 us -> none  [the longest x1 1.27 us: per_device(): gain_self[None]]
    slice x5 -> x0, local copies, waits for them, and re-layouts: 2.44 us -> none  [the longest x1 1.48 us: per_device(): small[2]]
where the time goes in v3:
time: 172 us
  Pallas kernels  170 us (99%)
    pallas_call x1, Pallas kernels, per_device(): pl.pallas_call(functools.partial(layer_kernel, cfg, tuple(ins) + tuple(ou...  166 us
    pallas_call x1, Pallas kernels, per_device(): pl.pallas_call(functools.partial(finish_kernel, len(moved), heads, seq),...  4.74 us

profile of v3, /device:TPU:0, one launch (start us, length us, event | category | flops | bytes accessed | tf_op | source)
XLA Modules:
  0.0 171.9 jit_solution(2227435804309585883)
XLA Ops:
  1.3 165.6 %shard_map.323 = (bf16[192,1024]{1,0:T(8,128)(2,1)}, bf16[192,1024]{1,0:T(8,128)(2,1)}, bf16[1024,768]{1,0:T(8,128)(2,1)}, f32[8,768]{1,0:T(8,128)}, f32[96,192]...) custom-call(s32[8]{0:T(128)} %refs_0_.1, ...), custom_call_target="tpu_custom_call" | custom-call | tf_op jit(solution)/shard_map/pallas_call | solution.py:861
  167.0 4.7 %shard_map.324 = (bf16[192,1024]{1,0:T(8,128)(2,1)}, bf16[192,1024]{1,0:T(8,128)(2,1)}, bf16[1024,768]{1,0:T(8,128)(2,1)}, f32[96,192]{1,0:T(8,128)}, f32[96,192...) custom-call(bf16[192,1024]{1,0:T(8,128)(2,1)} %get-tuple-element.48., ...), custom_call_target="tpu_custom_call" | custom-call | tf_op jit(solution)/shard_map/pallas_call | solution.py:874

commit v4 on v3

--- a/solution.py
+++ b/solution.py
@@ -60,8 +60,8 @@
     return (lax.axis_index("dp") ^ bit, lax.axis_index("tensor"))
 
 
-def reversed_bits(value, levels):
-    return sum(((value >> k) & 1) << (levels - 1 - k) for k in range(levels))
+def piece_index(rank, order):
+    return sum(((rank >> bit) & 1) << (len(order) - 1 - k) for k, bit in enumerate(order))
 
 
 class Weights(NamedTuple):
@@ -102,25 +102,31 @@
     def load(index, src, dst):
         return pltpu.make_async_copy(src, dst, a.load_sem.at[index])
 
-    load_x, load_g = load(0, a.inputs, a.x), load(1, a.out_grad, a.g3)
+    inner_rows = slice(0, inner), slice(inner, 2 * inner)
+    first_rows, later_rows = pl.ds(0, chunk_rows), pl.ds(chunk_rows, slots * seq - chunk_rows)
+    load_x = load(0, a.inputs.at[first_rows], a.x.at[first_rows])
+    load_more = load(2 + len(Weights._fields), a.inputs.at[later_rows], a.x.at[later_rows])
+    load_g = load(1, a.out_grad, a.g3)
+    spots = {name: getattr(a, "w_" + name) for name in Weights._fields if hasattr(a, "w_" + name)}
+    spots.update(key_cross=a.w_kv.at[inner_rows[0]], value_cross=a.w_kv.at[inner_rows[1]])
     loads = Weights(
-        *(
-            load(2 + i, getattr(a, name), getattr(a, "w_" + name))
-            for i, name in enumerate(Weights._fields)
-        )
+        *(load(2 + i, getattr(a, name), spots[name]) for i, name in enumerate(Weights._fields))
     )
     load_x.start()
-    for copy in loads[:4]:
+    for copy in loads[:3]:
         copy.start()
+    loads.key_cross.start()
+    loads.value_cross.start()
+    loads.output_self.start()
+    load_more.start()
 
     def enc_copy(slot, buffer):
         rows = pl.ds(pl.multiple_of(slot * enc_len, enc_len), enc_len)
         return pltpu.make_async_copy(a.encoded.at[rows], a.enc.at[rows_of(buffer, enc_len)], a.enc_sem.at[buffer])
 
     enc_copy(0, 0).start()
-    for copy in loads[4:]:
+    for copy in (loads.query_cross, loads.output_cross, loads.hidden_in, loads.hidden_out, load_g):
         copy.start()
-    load_g.start()
 
     barrier = pltpu.get_barrier_semaphore()
     peers = [c_peer, y_peer] + [dp_peer(1 << k) for k in range(levels)]
@@ -175,6 +181,9 @@
             device_id_type=MESH,
         )
 
+    def add_gain(index, value):
+        a.small[index : index + 1, :] += value
+
     def near_copy(p, k):
         return remote(a.part.at[other_rows(k)], a.near.at[k], a.near_sem, (p, k), c_peer)
 
@@ -186,6 +195,33 @@
         a.mine[k] = (a.part[own_rows(k)].astype(wide) + a.near[k].astype(wide)).astype(low)
         far_copy(p, k).start()
 
+    def last_copies(k):
+        return (
+            remote(
+                a.mine.at[k, :, pl.ds(0, half_width)],
+                a.far.at[0, k, :, pl.ds(0, half_width)],
+                a.far_sem,
+                (4, k),
+                y_peer,
+            ),
+            remote(a.inner_send.at[k], a.inner_far.at[k], a.inner_sem, (k,), y_peer),
+        )
+
+    def y_send_last(k):
+        near_copy(4, k).wait()
+        term = a.part[own_rows(k)].astype(wide) + a.near[k].astype(wide)
+        a.h1[k] = term
+        rows = a.x[own_rows(k)].astype(wide)
+        product = term * rows
+        row_inner = jnp.sum(product * gain_self, axis=-1, keepdims=True)
+        add_gain(0, jnp.sum(product * inverse_rms(rows), axis=0, keepdims=True))
+        a.inner_send[k] = jnp.broadcast_to(row_inner, (half_rows, half_rows)).T[:8]
+        a.mine[k, :, :half_width] = jnp.where(
+            y == 0, term[:, half_width:], term[:, :half_width]
+        ).astype(low)
+        for copy in last_copies(k):
+            copy.start()
+
     def total(p, k):
         far_copy(p, k).wait()
         return a.mine[k].astype(wide) + a.far[p % 2, k].astype(wide)
@@ -200,21 +236,25 @@
 
         lax.fori_loop(0, chunks, step, 0)
 
-    def phase(p, finish, buffer, compute):
+    def phase(p, finish, buffer, compute, extra=None, send=None):
+        send = send or functools.partial(y_send, p)
+
         def body(k):
             finish(k, total(p - 1, k))
             share_copy(p, k, buffer).start()
 
             @pl.when(k > 0)
             def _():
-                y_send(p, k - 1)
+                send(k - 1)
 
             share_copy(p, k, buffer).wait()
             compute(k)
             near_copy(p, k).start()
+            if extra is not None:
+                extra(k)
 
         each_chunk(body)
-        y_send(p, chunks - 1)
+        send(chunks - 1)
 
     def project(slot, buffer):
         enc_copy(slot, buffer).wait()
@@ -224,8 +264,8 @@
             enc_copy(slot + 1, 1 - buffer).start()
 
         rows = rows_of(slot, enc_len)
-        a.k2[rows] = dot_t(a.enc[rows_of(buffer, enc_len)], a.w_key_cross[...]).astype(low)
-        a.v2[rows] = dot_t(a.enc[rows_of(buffer, enc_len)], a.w_value_cross[...]).astype(low)
+        a.k2[rows] = dot_t(a.enc[rows_of(buffer, enc_len)], a.w_kv[:inner]).astype(low)
+        a.v2[rows] = dot_t(a.enc[rows_of(buffer, enc_len)], a.w_kv[inner : 2 * inner]).astype(low)
 
     def self_forward(k):
         rows = rows_of(k, chunk_rows)
@@ -246,27 +286,53 @@
         a.o1[rows] = mixed
         a.part[rows] = dot(mixed, a.w_output_self[...]).astype(low)
 
+    def peer_weights():
+        own, theirs = pl.ds(0, 2 * inner), pl.ds(2 * inner, 2 * inner)
+        return remote(a.w_kv.at[own], a.w_kv.at[theirs], a.kv_sem, (0,), y_peer)
+
+    loads.key_cross.wait()
+    loads.value_cross.wait()
+    pl.semaphore_wait(barrier, len(peers))
+    peer_weights().start()
     load_x.wait()
     for copy in loads[:4]:
         copy.wait()
 
     def phase_zero(k):
+        @pl.when(k == 1)
+        def _():
+            load_more.wait()
+
         self_forward(k)
-
-        @pl.when(k == 0)
-        def _():
-            pl.semaphore_wait(barrier, len(peers))
-            loads.key_cross.wait()
-            loads.value_cross.wait()
-
         near_copy(0, k).start()
+        y_send(0, k)
         project(CHUNK_SLOTS * k, 0)
-        y_send(0, k)
         project(CHUNK_SLOTS * k + 1, 1)
 
     each_chunk(phase_zero)
     loads.query_cross.wait()
     loads.output_cross.wait()
+    peer_weights().wait()
+
+    chip_slots = slots // 2
+
+    def chip_slot(k):
+        return chip_slots * y + k
+
+    enc_copy(chip_slot(0), 0).start()
+
+    def project_peer(k):
+        buffer = lax.rem(k, 2)
+        enc_copy(chip_slot(k), buffer).wait()
+
+        @pl.when(k + 1 < chip_slots)
+        def _():
+            enc_copy(chip_slot(k + 1), 1 - buffer).start()
+
+        rows = rows_of(k, enc_len)
+        encoded = a.enc[rows_of(buffer, enc_len)]
+        a.k2_peer[rows] = dot_t(encoded, a.w_kv[2 * inner : 3 * inner]).astype(low)
+        a.v2_peer[rows] = dot_t(encoded, a.w_kv[3 * inner :]).astype(low)
 
     def finish_one(k, term):
         hidden = a.x[own_rows(k)].astype(wide) + term
@@ -288,7 +354,7 @@
         a.o2[rows] = mixed
         a.part[rows] = dot(mixed, a.w_output_cross[...]).astype(low)
 
-    phase(1, finish_one, a.n2, cross_forward)
+    phase(1, finish_one, a.n2, cross_forward, project_peer)
     for copy in (loads.hidden_in, loads.hidden_out, load_g):
         copy.wait()
 
@@ -308,14 +374,19 @@
         return remote(a.out_part.at[k % 2, 1 - core], a.out_near.at[k], a.out_near_sem, (k,), c_peer)
 
     def out_far_copy(k):
-        return remote(a.out_mine.at[k, 1 - y], a.out_far.at[k], a.out_far_sem, (k,), y_peer)
-
-    def out_send(k):
+        return remote(a.out_mine.at[k], a.out_far.at[k], a.out_far_sem, (k,), y_peer)
+
+    def my_half(value):
+        return jnp.where(y == 0, value[:, :half_width], value[:, half_width:])
+
+    def other_half(value):
+        return jnp.where(y == 0, value[:, half_width:], value[:, :half_width])
+
+    def out_gather(k):
         out_near_copy(k).wait()
         term = a.out_part[k % 2, core].astype(wide) + a.out_near[k].astype(wide)
-        a.out_mine[k, 0] = term[:, :half_width].astype(low)
-        a.out_mine[k, 1] = term[:, half_width:].astype(low)
-        out_far_copy(k).start()
+        a.out_mine[k] = other_half(term).astype(low)
+        a.out_keep[k] = my_half(term) + my_half(a.h2[k])
 
     scale = 0.7978845608028654
 
@@ -352,11 +423,7 @@
         a.d_pre[rows] = grad_pre
         a.part[rows] = dot_t(grad_pre, a.w_hidden_in[...]).astype(low)
 
-    def feed_forward_sends(k):
-        feed_forward(k)
-        out_send(k)
-
-    phase(2, finish_two, a.n3, feed_forward_sends)
+    phase(2, finish_two, a.n3, feed_forward, out_gather)
 
     def column_copy(which, k):
         return remote(
@@ -375,83 +442,86 @@
         a.col_send[which, k] = jnp.where(first, right, left).astype(low)
         column_copy(which, k).start()
 
-    def my_half(value):
-        return jnp.where(y == 0, value[:, :half_width], value[:, half_width:])
-
     def finish_out(k):
         out_far_copy(k).wait()
-        value = my_half(a.h2[k]) + a.out_mine[k, y].astype(wide) + a.out_far[k].astype(wide)
+        value = a.out_keep[k] + a.out_far[k].astype(wide)
         emit_columns(0, k, keep_rows(k * CHUNK_SLOTS + core, value))
 
-    def dp_rank(level):
-        return (dp_me >> level) & 1
-
-    def dp_copy(block, level):
+    orders = (tuple(range(levels)), (1, 0) + tuple(range(2, levels)))
+
+    def dp_rank(half, level):
+        return (dp_me >> orders[half][level]) & 1
+
+    def dp_copy(block, half, level):
         buffer = block % 2
         count = 1 << (levels - 1 - level)
         source = a.term if level == 0 else a.holds[level - 1]
-        part = pl.ds((1 - dp_rank(level)) * count, count)
+        part = pl.ds((1 - dp_rank(half, level)) * count, count)
         return remote(
-            source.at[buffer, part],
-            a.lands[level].at[buffer],
+            source.at[buffer, half, part],
+            a.lands[level].at[buffer, half],
             a.dp_sem,
-            (block, level),
-            dp_peer(1 << level),
+            (block, half, level),
+            dp_peer(1 << orders[half][level]),
         )
+
+    def raw_copy(block):
+        return pltpu.make_async_copy(
+            a.term.at[block % 2], a.raw_grads.at[block], a.dp_sem.at[0, block, 0, 0]
+        )
+
+    def credit_wait(block, half, level):
+        pl.semaphore_wait(a.credit_sem.at[block % 2, half, level], 1)
 
     def dp_begin(block):
         if in_kernel:
-            if block >= 2:
-                credit_wait(block, 0)
-            dp_copy(block, 0).start()
+            for half in range(2):
+                if block >= 2:
+                    credit_wait(block, half, 0)
+                dp_copy(block, half, 0).start()
         else:
-            pltpu.make_async_copy(
-                a.term.at[block % 2], a.raw_grads.at[block], a.dp_sem.at[0, block, 0]
-            ).start()
-
-    def credit_wait(block, level):
-        pl.semaphore_wait(a.credit_sem.at[block % 2, level], 1)
+            raw_copy(block).start()
 
     def dp_advance(block, level):
         if not in_kernel:
             return
         buffer = block % 2
         count = 1 << (levels - 1 - level)
-        dp_copy(block, level).wait()
-        source = a.term if level == 0 else a.holds[level - 1]
-        land = a.lands[level]
-        part = pl.ds(dp_rank(level) * count, count)
-        value = source[buffer, part].astype(wide) + land[buffer].astype(wide)
-        if level == levels - 1:
-            emit_grads(block, value[0])
-        else:
-            a.holds[level][buffer] = value.astype(low)
-        if block < 2:
-            pl.semaphore_signal(
-                a.credit_sem.at[buffer, level],
-                inc=1,
-                device_id=dp_peer(1 << level),
-                device_id_type=MESH,
-            )
-        if level + 1 < levels:
-            if block >= 2:
-                credit_wait(block, level + 1)
-            dp_copy(block, level + 1).start()
+        for half in range(2):
+            dp_copy(block, half, level).wait()
+            source = a.term if level == 0 else a.holds[level - 1]
+            part = pl.ds(dp_rank(half, level) * count, count)
+            value = source[buffer, half, part].astype(wide)
+            value += a.lands[level][buffer, half].astype(wide)
+            if level == levels - 1:
+                emit_grads(block, half, value[0])
+            else:
+                a.holds[level][buffer, half] = value.astype(low)
+            if block < 2:
+                pl.semaphore_signal(
+                    a.credit_sem.at[buffer, half, level],
+                    inc=1,
+                    device_id=dp_peer(1 << orders[half][level]),
+                    device_id_type=MESH,
+                )
+            if level + 1 < levels:
+                if block >= 2:
+                    credit_wait(block, half, level + 1)
+                dp_copy(block, half, level + 1).start()
 
     def dp_finish_raw(block):
         if not in_kernel:
-            pltpu.make_async_copy(
-                a.term.at[block % 2], a.raw_grads.at[block], a.dp_sem.at[0, block, 0]
-            ).wait()
-
-    def emit_grads(block, value):
+            raw_copy(block).wait()
+
+    def emit_grads(block, half, value):
+        columns = slice(half * half_width, (half + 1) * half_width)
         if block == 0:
-            a.grad_hidden_out[...] = value
+            a.grad_hidden_out[:, columns] = value
         elif block == 1:
-            a.grad_hidden_in[...] = value
+            a.grad_hidden_in[:, columns] = value
         else:
-            names = Weights._fields[4:8] if block == 2 else Weights._fields[:4]
-            for i, name in enumerate(names):
+            start = (4 if block == 2 else 0) + 2 * half
+            for i, name in enumerate(Weights._fields[start : start + 2]):
                 getattr(a, "grad_" + name)[...] = value[:, i * inner : (i + 1) * inner]
 
     piece = cfg.piece
@@ -463,9 +533,14 @@
         if in_kernel:
             for i in range(pieces_each):
                 for gg in range(groups):
-                    index = reversed_bits(gg * pieces_each + i, levels)
-                    if gg == g:
-                        a.term[block % 2, index] = rows[i * piece : (i + 1) * piece]
+                    if gg != g:
+                        continue
+                    for half in range(2):
+                        index = piece_index(gg * pieces_each + i, orders[half])
+                        a.term[block % 2, half, index] = rows[
+                            i * piece : (i + 1) * piece,
+                            half * half_width : (half + 1) * half_width,
+                        ]
         else:
             a.term[block % 2, g * group_rows : (g + 1) * group_rows] = rows
 
@@ -488,9 +563,6 @@
     dp_begin(0)
     plain_grads(1, a.n3, a.d_pre)
     dp_begin(1)
-
-    def add_gain(index, value):
-        a.small[index : index + 1, :] += value
 
     def finish_three(k, term):
         grad_rows, grad_gain = norm_back(a.h2[k], gain_ffn, term)
@@ -498,7 +570,6 @@
         grad = a.g3[own_rows(k)].astype(wide) + grad_rows
         a.dh[k] = grad
         a.dh2[own_rows(k)] = grad.astype(low)
-        finish_out(k)
 
     def score_back(soft, grad_soft):
         weights = soft.astype(wide)
@@ -508,6 +579,7 @@
     def cross_backward(k):
         rows = rows_of(k, chunk_rows)
         grad_mixed = dot_t(a.dh2[rows], a.w_output_cross[...]).astype(low)
+        a.do2[rows] = grad_mixed
         query = a.q2[rows]
         grads = []
         for s in range(CHUNK_SLOTS):
@@ -521,69 +593,58 @@
             a.dkv[slot, inner:] = t_dot(tall_grad, soft).astype(low)
             grads.append(unstack(dot(grad_scores, a.k2[enc_rows])).astype(low))
         grads = jnp.concatenate(grads, axis=0)
-        a.q2[rows] = grads
+        a.d_pre[rows, :inner] = grads
         a.part[rows] = dot(grads, a.w_query_cross[...]).astype(low)
 
         @pl.when(k == 2)
         def _():
             dp_advance(0, 0)
 
+        @pl.when(k == 3)
+        def _():
+            dp_advance(0, 1)
+
     phase(3, finish_three, a.dh2, cross_backward)
+
+    def peer_rows(index, source, target):
+        rows = rows_of(1 - y, chip_slots * seq)
+        return remote(source.at[rows], target, a.peer_sem, (index,), y_peer)
+
+    peer_copies = peer_rows(0, a.q2, a.q2_peer), peer_rows(1, a.do2, a.do2_peer)
+    for copy in peer_copies:
+        copy.start()
+    enc_copy(0, 0).start()
+    dp_advance(1, 0)
+    dp_advance(0, 2)
 
     kv_blocks = 2 * inner // half_rows
     for i in range(kv_blocks):
         a.h2[i] = jnp.zeros_like(a.h2[i])
 
-    def enc_slots(j, own):
-        which = jnp.where(own == 1, core, 1 - core)
-        side = jnp.where(j < 2, 1 - y, y)
-        return 4 * side + 2 * which + lax.rem(j, 2)
-
-    def enc_partial(slot, buffer):
-        key_grad, value_grad = a.dkv[slot, :inner], a.dkv[slot, inner:]
+    def add_kv(slot, buffer):
+        value = dot(a.dkv[slot], a.enc[rows_of(buffer, enc_len)])
         for i in range(kv_blocks):
-            part = slice(i * half_rows, (i + 1) * half_rows)
-            a.h2[i] += dot(a.dkv[slot, part], a.enc[rows_of(buffer, enc_len)])
-        return t_dot(key_grad, a.w_key_cross[...]) + t_dot(value_grad, a.w_value_cross[...])
-
-    def enc_half(j):
-        return rows_of(lax.rem(j, 2), enc_len)
-
-    def enc_near_copy(j):
-        source = a.n3.at[enc_half(j)]
-        target = a.act if j < 2 else a.d_pre
-        return remote(source, target.at[enc_half(j)], a.enc_near_sem, (j,), c_peer)
-
-    def enc_far_copy(j):
-        return remote(a.g3.at[enc_half(j)], a.enc_far.at[j], a.enc_far_sem, (j,), y_peer)
-
-    enc_copy(enc_slots(0, 0), 0).start()
-    for j in range(4):
-        enc_copy(enc_slots(j, 0), 0).wait()
-        enc_copy(enc_slots(j, 1), 1).start()
-        if j >= 2:
-            enc_near_copy(j - 2).wait_send()
-        a.n3[enc_half(j)] = enc_partial(enc_slots(j, 0), 0).astype(low)
-        enc_near_copy(j).start()
-        enc_copy(enc_slots(j, 1), 1).wait()
-        if j < 3:
-            enc_copy(enc_slots(j + 1, 0), 0).start()
-        partial = enc_partial(enc_slots(j, 1), 1)
-        enc_near_copy(j).wait_recv()
-        if j < 2:
-            a.g3[enc_half(j)] = (partial + a.act[enc_half(j)].astype(wide)).astype(low)
-            enc_far_copy(j).start()
-        else:
-            a.enc_out[rows_of(j - 2, enc_len)] = (
-                partial + a.d_pre[enc_half(j)].astype(wide)
-            ).astype(low)
-    dp_advance(1, 0)
-    dp_advance(0, 1)
-
-    a.enc[turned_rows(0)] = t_dot(a.q2[...], a.n2[...]).astype(low)
+            a.h2[i] += value[i * half_rows : (i + 1) * half_rows]
+
+    def kv_pair(j, carry):
+        enc_copy(2 * j, 0).wait()
+        enc_copy(2 * j + 1, 1).start()
+        add_kv(2 * j, 0)
+        enc_copy(2 * j + 1, 1).wait()
+
+        @pl.when(2 * j + 2 < slots)
+        def _():
+            enc_copy(2 * j + 2, 0).start()
+
+        add_kv(2 * j + 1, 1)
+        return carry
+
+    lax.fori_loop(0, slots // 2, kv_pair, 0)
+    a.enc[turned_rows(0)] = t_dot(a.d_pre[:, :inner], a.n2[...]).astype(low)
     for i in range(kv_blocks):
         a.enc[inner + i * half_rows : inner + (i + 1) * half_rows] = a.h2[i].astype(low)
     a.enc[turned_rows(3)] = t_dot(a.o2[...], a.dh2[...]).astype(low)
+    dp_advance(1, 1)
     dp_finish_raw(0)
     turned_grads(2)
     dp_begin(2)
@@ -617,10 +678,17 @@
             + dot(grads[2], a.w_value_self[...])
         ).astype(low)
 
-    phase(4, finish_four, a.dh1, self_backward)
-    dp_advance(1, 1)
-    dp_advance(0, 2)
-    dp_advance(1, 2)
+        @pl.when(k == 1)
+        def _():
+            dp_advance(1, 2)
+
+        @pl.when(k == 3)
+        def _():
+            dp_advance(2, 0)
+
+    phase(4, finish_four, a.dh1, self_backward, send=y_send_last)
+    for k in range(chunks):
+        out_far_copy(k).start()
     a.enc[turned_rows(0)] = t_dot(a.q1[...], a.n1[...]).astype(low)
     a.enc[turned_rows(1)] = t_dot(a.k1[...], a.n1[...]).astype(low)
     a.enc[turned_rows(2)] = t_dot(a.v1[...], a.n1[...]).astype(low)
@@ -628,16 +696,7 @@
     dp_finish_raw(1)
     turned_grads(3)
     dp_begin(3)
-    dp_advance(2, 0)
-
-    def phase_five(k):
-        grad_rows, grad_gain = norm_back(
-            a.x[own_rows(k)].astype(wide), gain_self, total(4, k)
-        )
-        add_gain(0, grad_gain)
-        emit_columns(1, k, my_half(a.dh[k] + grad_rows))
-
-    each_chunk(phase_five)
+    dp_advance(2, 1)
 
     mirror = jnp.where(row_i + col_i == seq - 1, 1.0, 0.0).astype(wide)
     for h in range(heads):
@@ -646,45 +705,93 @@
         a.small[3:4, h * seq : (h + 1) * seq] = jnp.sum(turned, axis=0, keepdims=True)
 
     def small_copy(i):
-        peer = c_peer if i == 0 else dp_peer(1 << (i - 1))
+        peer = (c_peer, y_peer)[i] if i < 2 else dp_peer(1 << (i - 2))
         return remote(a.small, a.small_land.at[i], a.small_sem, (i,), peer)
 
+    row = lax.broadcasted_iota(jnp.int32, a.small.shape, 0)
+
+    def small_step(i):
+        small_copy(i).wait()
+        summed = (row < 3, row < 1)[i] if i < 2 else row < 8
+        a.small[...] += jnp.where(summed, a.small_land[i], 0.0)
+        if i < levels + 1:
+            small_copy(i + 1).start()
+
     small_copy(0).start()
-    dp_advance(2, 1)
-    small_copy(0).wait()
-    row = lax.broadcasted_iota(jnp.int32, a.small.shape, 0)
-    a.small[...] += jnp.where(row < 3, a.small_land[0], 0.0)
-    for i in range(1, levels + 1):
-        small_copy(i).start()
-        if i == 1:
-            dp_advance(3, 0)
-        if i == 2:
-            dp_advance(2, 2)
-        small_copy(i).wait()
-        a.small[...] += a.small_land[i]
+    for copy in peer_copies:
+        copy.wait()
+
+    def enc_partial(k):
+        rows = rows_of(k, seq)
+        enc_rows = rows_of(k, enc_len)
+        tall_query, tall_grad = stack(a.q2_peer[rows]), stack(a.do2_peer[rows])
+        soft = softmax(dot_t(tall_query, a.k2_peer[enc_rows]))
+        grad_scores = score_back(soft, dot_t(tall_grad, a.v2_peer[enc_rows]))
+        peer_grads = jnp.concatenate(
+            [t_dot(tall_query, grad_scores).astype(low), t_dot(tall_grad, soft).astype(low)], axis=0
+        )
+        own = t_dot(a.dkv[chip_slot(k)], a.w_kv[: 2 * inner])
+        return own + t_dot(peer_grads, a.w_kv[2 * inner :])
+
+    enc_each = chip_slots // 2
+
+    def enc_near_copy(j):
+        rows = rows_of(j, enc_len)
+        return remote(a.n3.at[rows], a.act.at[rows], a.enc_near_sem, (j,), c_peer)
+
+    def enc_give(j, carry):
+        a.n3[rows_of(j, enc_len)] = enc_partial((1 - core) * enc_each + j).astype(low)
+        enc_near_copy(j).start()
+        return carry
+
+    def enc_keep(j, carry):
+        partial = enc_partial(core * enc_each + j)
+        enc_near_copy(j).wait()
+        rows = rows_of(j, enc_len)
+        a.enc_out[rows] = (partial + a.act[rows].astype(wide)).astype(low)
+        return carry
+
+    small_step(0)
+    lax.fori_loop(0, enc_each, enc_give, 0)
+    small_step(1)
+    dp_advance(2, 2)
+    dp_advance(3, 0)
+    lax.fori_loop(0, enc_each, enc_keep, 0)
+    store_enc = load(2, a.enc_out, a.encoded_grad)
+    store_enc.start()
+    small_step(2)
     dp_advance(3, 1)
+
+    def phase_five(k):
+        for copy in last_copies(k):
+            copy.wait()
+        rows = my_half(a.x[own_rows(k)]).astype(wide)
+        inverse = inverse_rms(a.x[own_rows(k)].astype(wide))
+        sums = (a.inner_send[k] + a.inner_far[k])[:1]
+        row_inner = jnp.broadcast_to(sums, (half_rows, half_rows)).T[:, :1] * (1.0 / width)
+        term = my_half(a.h1[k]) + a.far[0, k, :, :half_width].astype(wide)
+        grad_rows = inverse * my_half(gain_self) * term
+        grad_rows -= rows * (inverse * inverse * inverse) * row_inner
+        emit_columns(1, k, my_half(a.dh[k]) + grad_rows)
+
+    each_chunk(phase_five)
+    each_chunk(finish_out)
+    for i in range(3, levels + 2):
+        small_step(i)
     dp_advance(3, 2)
     dp_finish_raw(2)
     dp_finish_raw(3)
-
-    for j in range(2):
-        enc_far_copy(j).wait()
-        a.enc_out[rows_of(j, enc_len)] = (
-            a.enc_out[rows_of(j, enc_len)].astype(wide) + a.enc_far[j].astype(wide)
-        ).astype(low)
-        enc_near_copy(2 + j).wait_send()
     for k in range(chunks):
         column_copy(0, k).wait()
         column_copy(1, k).wait()
     stores = [
         load(0, a.columns.at[0], a.layer_out),
         load(1, a.columns.at[1], a.input_grad),
-        load(2, a.enc_out, a.encoded_grad),
     ]
     for store in stores:
         store.start()
     a.small_out[...] = a.small[...]
-    for store in stores:
+    for store in (*stores, store_enc):
         store.wait()
 
 
@@ -781,7 +888,9 @@
     own_wide = vmem((chunks, half, width), wide)
     own_low = vmem((chunks, half, width), low)
     scratch = {
-        "w_" + name: vmem(ins[name][0].shape, low) for name in Weights._fields
+        "w_" + name: vmem(ins[name][0].shape, low)
+        for name in Weights._fields
+        if name not in Weights._fields[5:7]
     }
     scratch.update(
         x=whole_rows,
@@ -814,18 +923,26 @@
         far=vmem((2, chunks, half, width), low),
         out_part=vmem((2, 2, half, width), low),
         out_near=own_low,
-        out_mine=vmem((chunks, 2, half, width // 2), low),
+        out_mine=vmem((chunks, half, width // 2), low),
+        out_keep=vmem((chunks, half, width // 2), wide),
         out_far=vmem((chunks, half, width // 2), low),
         columns=vmem((2, quarter, rows), low),
         col_send=vmem((2, chunks, quarter, half), low),
-        enc_far=vmem((2, enc_len, width), low),
+        w_kv=vmem((4 * inner, width), low),
+        k2_peer=vmem((enc_rows // 2, inner), low),
+        v2_peer=vmem((enc_rows // 2, inner), low),
+        q2_peer=vmem((rows // 2, inner), low),
+        do2_peer=vmem((rows // 2, inner), low),
+        do2=inner_rows,
+        inner_send=vmem((chunks, 8, half), wide),
+        inner_far=vmem((chunks, 8, half), wide),
         enc_out=vmem((enc_rows // 4, width), low),
         pre=vmem((CHUNK_SLOTS * seq, hidden), wide),
         bias=vmem((heads * seq, seq), wide),
         table=vmem((heads * seq, seq), wide),
         small=vmem((8, width), wide),
-        small_land=vmem((levels + 1, 8, width), wide),
-        load_sem=dma((2 + len(weights),)),
+        small_land=vmem((levels + 2, 8, width), wide),
+        load_sem=dma((3 + len(weights),)),
         enc_sem=dma((2,)),
         near_sem=dma((2, 5, chunks)),
         far_sem=dma((2, 5, chunks)),
@@ -833,19 +950,21 @@
         out_near_sem=dma((2, chunks)),
         out_far_sem=dma((2, chunks)),
         col_sem=dma((2, 2, chunks)),
-        enc_near_sem=dma((2, 4)),
-        enc_far_sem=dma((2, 2)),
-        dp_sem=dma((2, 4, levels)),
-        small_sem=dma((2, levels + 1)),
-        credit_sem=pltpu.SemaphoreType.REGULAR((2, levels)),
+        enc_near_sem=dma((2, 2)),
+        peer_sem=dma((2, 2)),
+        kv_sem=dma((2, 1)),
+        inner_sem=dma((2, chunks)),
+        dp_sem=dma((2, 4, 2, levels)),
+        small_sem=dma((2, levels + 2)),
+        credit_sem=pltpu.SemaphoreType.REGULAR((2, 2, levels)),
     )
     if in_kernel:
-        scratch.update(term=vmem((2, dp_count, piece, width), low))
+        scratch.update(term=vmem((2, 2, dp_count, piece, width // 2), low))
         for level in range(levels):
             count = 1 << (levels - 1 - level)
-            scratch["land%d" % level] = vmem((2, count, piece, width), low)
+            scratch["land%d" % level] = vmem((2, 2, count, piece, width // 2), low)
             if level + 1 < levels:
-                scratch["hold%d" % level] = vmem((2, count, piece, width), low)
+                scratch["hold%d" % level] = vmem((2, 2, count, piece, width // 2), low)
     else:
         scratch.update(term=vmem((2, width, width), low))
     cfg = SimpleNamespace(
@@ -865,7 +984,7 @@
         out_specs=tuple(o[1] for o in outs.values()),
         scratch_shapes=list(scratch.values()),
         compiler_params=pltpu.CompilerParams(
-            collective_id=1, has_side_effects=True, vmem_limit_bytes=63 * 2**20
+            collective_id=1, has_side_effects=True, vmem_limit_bytes=65000 * 2**10
         ),
     )(*[i[0] for i in ins.values()])
     moved = [i for i, name in enumerate(outs) if name not in ("small_out", "raw_grads")]

time: 172 us -> 152 us (0.88)
  Pallas kernels: 170 us -> 149 us
    pallas_call x1, Pallas kernels: 166 us -> 145 us  [per_device(): pl.pallas_call(functools.partial(layer_kernel, cfg, tuple(ins) + tuple(ou...]
where the time goes in v4:
time: 152 us; the launch traced here: 151 us
  Pallas kernels  149 us (98%)
    pallas_call x1, Pallas kernels, per_device(): pl.pallas_call(functools.partial(layer_kernel, cfg, tuple(ins) + tuple(ou...  145 us
    pallas_call x1, Pallas kernels, per_device(): pl.pallas_call(functools.partial(finish_kernel, len(moved), heads, seq),...  4.74 us

profile of v4, /device:TPU:0, one launch (start us, length us, event | category | flops | bytes accessed | tf_op | source)
XLA Modules:
  0.0 151.0 jit_solution(14514922548660103405)
XLA Ops:
  1.3 144.8 %shard_map.323 = (bf16[192,1024]{1,0:T(8,128)(2,1)}, bf16[192,1024]{1,0:T(8,128)(2,1)}, bf16[1024,768]{1,0:T(8,128)(2,1)}, f32[8,768]{1,0:T(8,128)}, f32[96,192]...) custom-call(s32[8]{0:T(128)} %refs_0_.1, ...), custom_call_target="tpu_custom_call" | custom-call | tf_op jit(solution)/shard_map/pallas_call | solution.py:980
  146.1 4.7 %shard_map.324 = (bf16[192,1024]{1,0:T(8,128)(2,1)}, bf16[192,1024]{1,0:T(8,128)(2,1)}, bf16[1024,768]{1,0:T(8,128)(2,1)}, f32[96,192]{1,0:T(8,128)}, f32[96,192...) custom-call(bf16[192,1024]{1,0:T(8,128)(2,1)} %get-tuple-element.48., ...), custom_call_target="tpu_custom_call" | custom-call | tf_op jit(solution)/shard_map/pallas_call | solution.py:993

commit v5 on v4

--- a/solution.py
+++ b/solution.py
@@ -112,26 +112,45 @@
     loads = Weights(
         *(load(2 + i, getattr(a, name), spots[name]) for i, name in enumerate(Weights._fields))
     )
-    load_x.start()
-    for copy in loads[:3]:
-        copy.start()
     loads.key_cross.start()
     loads.value_cross.start()
-    loads.output_self.start()
+    load_x.start()
+    for copy in loads[:4]:
+        copy.start()
     load_more.start()
-
-    def enc_copy(slot, buffer):
-        rows = pl.ds(pl.multiple_of(slot * enc_len, enc_len), enc_len)
-        return pltpu.make_async_copy(a.encoded.at[rows], a.enc.at[rows_of(buffer, enc_len)], a.enc_sem.at[buffer])
-
-    enc_copy(0, 0).start()
-    for copy in (loads.query_cross, loads.output_cross, loads.hidden_in, loads.hidden_out, load_g):
-        copy.start()
 
     barrier = pltpu.get_barrier_semaphore()
     peers = [c_peer, y_peer] + [dp_peer(1 << k) for k in range(levels)]
     for peer in peers:
         pl.semaphore_signal(barrier, inc=1, device_id=peer, device_id_type=MESH)
+
+    def remote(src, dst, sems, index, peer):
+        return pltpu.make_async_remote_copy(
+            src_ref=src,
+            dst_ref=dst,
+            send_sem=sems.at[(0,) + index],
+            recv_sem=sems.at[(1,) + index],
+            device_id=peer,
+            device_id_type=MESH,
+        )
+
+    def peer_weights():
+        own, theirs = pl.ds(0, 2 * inner), pl.ds(2 * inner, 2 * inner)
+        return remote(a.w_kv.at[own], a.w_kv.at[theirs], a.kv_sem, (0,), y_peer)
+
+    def enc_copy(slot, buffer):
+        rows = pl.ds(pl.multiple_of(slot * enc_len, enc_len), enc_len)
+        target = a.enc.at[rows_of(buffer, enc_len)]
+        return pltpu.make_async_copy(a.encoded.at[rows], target, a.enc_sem.at[buffer])
+
+    enc_copy(0, 0).start()
+    for copy in (loads.query_cross, loads.output_cross, loads.hidden_in, loads.hidden_out, load_g):
+        copy.start()
+
+    loads.key_cross.wait()
+    loads.value_cross.wait()
+    pl.semaphore_wait(barrier, len(peers))
+    peer_weights().start()
 
     gain_self, gain_cross, gain_ffn = (
         ref[...].reshape(1, width) for ref in (a.gain_self, a.gain_cross, a.gain_ffn)
@@ -170,16 +189,6 @@
 
     def other_rows(k):
         return pl.ds(pl.multiple_of(k * chunk_rows + (1 - core) * half_rows, half_rows), half_rows)
-
-    def remote(src, dst, sems, index, peer):
-        return pltpu.make_async_remote_copy(
-            src_ref=src,
-            dst_ref=dst,
-            send_sem=sems.at[(0,) + index],
-            recv_sem=sems.at[(1,) + index],
-            device_id=peer,
-            device_id_type=MESH,
-        )
 
     def add_gain(index, value):
         a.small[index : index + 1, :] += value
@@ -286,14 +295,6 @@
         a.o1[rows] = mixed
         a.part[rows] = dot(mixed, a.w_output_self[...]).astype(low)
 
-    def peer_weights():
-        own, theirs = pl.ds(0, 2 * inner), pl.ds(2 * inner, 2 * inner)
-        return remote(a.w_kv.at[own], a.w_kv.at[theirs], a.kv_sem, (0,), y_peer)
-
-    loads.key_cross.wait()
-    loads.value_cross.wait()
-    pl.semaphore_wait(barrier, len(peers))
-    peer_weights().start()
     load_x.wait()
     for copy in loads[:4]:
         copy.wait()
@@ -473,21 +474,21 @@
     def credit_wait(block, half, level):
         pl.semaphore_wait(a.credit_sem.at[block % 2, half, level], 1)
 
-    def dp_begin(block):
+    def dp_begin(block, halves=(0, 1)):
         if in_kernel:
-            for half in range(2):
+            for half in halves:
                 if block >= 2:
                     credit_wait(block, half, 0)
                 dp_copy(block, half, 0).start()
-        else:
+        elif 1 in halves:
             raw_copy(block).start()
 
-    def dp_advance(block, level):
+    def dp_advance(block, level, halves=(0, 1)):
         if not in_kernel:
             return
         buffer = block % 2
         count = 1 << (levels - 1 - level)
-        for half in range(2):
+        for half in halves:
             dp_copy(block, half, level).wait()
             source = a.term if level == 0 else a.holds[level - 1]
             part = pl.ds(dp_rank(half, level) * count, count)
@@ -509,6 +510,12 @@
                     credit_wait(block, half, level + 1)
                 dp_copy(block, half, level + 1).start()
 
+    def at_chunk(k, step, *moves):
+        @pl.when(k == step)
+        def _():
+            for move in moves:
+                dp_advance(*move)
+
     def dp_finish_raw(block):
         if not in_kernel:
             raw_copy(block).wait()
@@ -549,15 +556,18 @@
             columns = slice(g * group_rows, (g + 1) * group_rows)
             store_pieces(block, g, t_dot(left[:, columns], right[...]).astype(low))
 
-    def turned_grads(block):
-        for g in range(groups):
-            columns = slice(g * group_rows, (g + 1) * group_rows)
-            store_pieces(block, g, a.enc[all_turned, columns].T)
+    def turned_grads(block, half):
+        value = a.enc[half * 2 * inner : (half + 1) * 2 * inner].T
+        columns = slice(half * half_width, (half + 1) * half_width)
+        if in_kernel:
+            for i in range(width // piece):
+                index = piece_index(i, orders[half])
+                a.term[block % 2, half, index] = value[i * piece : (i + 1) * piece]
+        else:
+            a.term[block % 2, :, columns] = value
 
     def turned_rows(i):
         return slice(i * inner, (i + 1) * inner)
-
-    all_turned = slice(0, 4 * inner)
 
     plain_grads(0, a.g3, a.act)
     dp_begin(0)
@@ -579,7 +589,8 @@
     def cross_backward(k):
         rows = rows_of(k, chunk_rows)
         grad_mixed = dot_t(a.dh2[rows], a.w_output_cross[...]).astype(low)
-        a.do2[rows] = grad_mixed
+        a.pair[rows, inner:] = grad_mixed
+        a.pair[rows, :inner] = a.q2[rows]
         query = a.q2[rows]
         grads = []
         for s in range(CHUNK_SLOTS):
@@ -596,57 +607,51 @@
         a.d_pre[rows, :inner] = grads
         a.part[rows] = dot(grads, a.w_query_cross[...]).astype(low)
 
-        @pl.when(k == 2)
-        def _():
-            dp_advance(0, 0)
-
-        @pl.when(k == 3)
-        def _():
-            dp_advance(0, 1)
-
-    phase(3, finish_three, a.dh2, cross_backward)
-
-    def peer_rows(index, source, target):
-        rows = rows_of(1 - y, chip_slots * seq)
-        return remote(source.at[rows], target, a.peer_sem, (index,), y_peer)
-
-    peer_copies = peer_rows(0, a.q2, a.q2_peer), peer_rows(1, a.do2, a.do2_peer)
-    for copy in peer_copies:
-        copy.start()
-    enc_copy(0, 0).start()
-    dp_advance(1, 0)
-    dp_advance(0, 2)
-
     kv_blocks = 2 * inner // half_rows
-    for i in range(kv_blocks):
-        a.h2[i] = jnp.zeros_like(a.h2[i])
+    a.pre[...] = jnp.zeros_like(a.pre)
+
+    def kv_part(i):
+        if i == kv_blocks - 1:
+            return a.h2.at[0]
+        return a.pre.at[slice(i * half_rows, (i + 1) * half_rows)]
 
     def add_kv(slot, buffer):
         value = dot(a.dkv[slot], a.enc[rows_of(buffer, enc_len)])
         for i in range(kv_blocks):
-            a.h2[i] += value[i * half_rows : (i + 1) * half_rows]
-
-    def kv_pair(j, carry):
-        enc_copy(2 * j, 0).wait()
-        enc_copy(2 * j + 1, 1).start()
-        add_kv(2 * j, 0)
-        enc_copy(2 * j + 1, 1).wait()
-
-        @pl.when(2 * j + 2 < slots)
+            kv_part(i)[...] += value[i * half_rows : (i + 1) * half_rows]
+
+    def kv_chunk(k):
+        @pl.when(k == 0)
         def _():
-            enc_copy(2 * j + 2, 0).start()
-
-        add_kv(2 * j + 1, 1)
-        return carry
-
-    lax.fori_loop(0, slots // 2, kv_pair, 0)
+            a.h2[0] = jnp.zeros_like(a.h2[0])
+
+        for i in range(2):
+            enc_copy(2 * k + i, i).wait()
+            add_kv(2 * k + i, i)
+
+            @pl.when(k + 1 < chunks)
+            def _():
+                enc_copy(2 * k + 2 + i, i).start()
+
+        at_chunk(k, 2, (0, 0))
+        at_chunk(k, 3, (1, 0))
+
+    enc_copy(0, 0).start()
+    enc_copy(1, 1).start()
+    phase(3, finish_three, a.dh2, cross_backward, kv_chunk)
+
+    peer_copy = remote(
+        a.pair.at[rows_of(1 - y, chip_slots * seq)], a.pair_peer, a.peer_sem, (0,), y_peer
+    )
+    peer_copy.start()
     a.enc[turned_rows(0)] = t_dot(a.d_pre[:, :inner], a.n2[...]).astype(low)
     for i in range(kv_blocks):
-        a.enc[inner + i * half_rows : inner + (i + 1) * half_rows] = a.h2[i].astype(low)
+        a.enc[inner + i * half_rows : inner + (i + 1) * half_rows] = kv_part(i)[...].astype(low)
     a.enc[turned_rows(3)] = t_dot(a.o2[...], a.dh2[...]).astype(low)
-    dp_advance(1, 1)
     dp_finish_raw(0)
-    turned_grads(2)
+    for half in range(2):
+        turned_grads(2, half)
+    dp_advance(0, 1)
     dp_begin(2)
 
     def finish_four(k, term):
@@ -678,53 +683,53 @@
             + dot(grads[2], a.w_value_self[...])
         ).astype(low)
 
-        @pl.when(k == 1)
-        def _():
-            dp_advance(1, 2)
-
-        @pl.when(k == 3)
-        def _():
-            dp_advance(2, 0)
-
-    phase(4, finish_four, a.dh1, self_backward, send=y_send_last)
+    def self_moves(k):
+        at_chunk(k, 1, (1, 1))
+        at_chunk(k, 2, (0, 2))
+        at_chunk(k, 3, (2, 0))
+
+    phase(4, finish_four, a.dh1, self_backward, self_moves, y_send_last)
     for k in range(chunks):
         out_far_copy(k).start()
-    a.enc[turned_rows(0)] = t_dot(a.q1[...], a.n1[...]).astype(low)
-    a.enc[turned_rows(1)] = t_dot(a.k1[...], a.n1[...]).astype(low)
-    a.enc[turned_rows(2)] = t_dot(a.v1[...], a.n1[...]).astype(low)
-    a.enc[turned_rows(3)] = t_dot(a.o1[...], a.dh1[...]).astype(low)
-    dp_finish_raw(1)
-    turned_grads(3)
-    dp_begin(3)
-    dp_advance(2, 1)
-
     mirror = jnp.where(row_i + col_i == seq - 1, 1.0, 0.0).astype(wide)
     for h in range(heads):
         flipped = exact_dot(a.table[h * seq : (h + 1) * seq, :], mirror)
         turned = pltpu.roll(flipped, 0, 1, stride=1, stride_axis=0)
         a.small[3:4, h * seq : (h + 1) * seq] = jnp.sum(turned, axis=0, keepdims=True)
 
+    hops = [dp_peer(1 << k) for k in range(levels)] + [c_peer, y_peer]
+    row = lax.broadcasted_iota(jnp.int32, a.small.shape, 0)
+
     def small_copy(i):
-        peer = (c_peer, y_peer)[i] if i < 2 else dp_peer(1 << (i - 2))
-        return remote(a.small, a.small_land.at[i], a.small_sem, (i,), peer)
-
-    row = lax.broadcasted_iota(jnp.int32, a.small.shape, 0)
+        return remote(a.small, a.small_land.at[i], a.small_sem, (i,), hops[i])
 
     def small_step(i):
         small_copy(i).wait()
-        summed = (row < 3, row < 1)[i] if i < 2 else row < 8
+        summed = row < (8 if i < levels else 3 if i == levels else 1)
         a.small[...] += jnp.where(summed, a.small_land[i], 0.0)
         if i < levels + 1:
             small_copy(i + 1).start()
 
     small_copy(0).start()
-    for copy in peer_copies:
-        copy.wait()
+    a.enc[turned_rows(0)] = t_dot(a.q1[...], a.n1[...]).astype(low)
+    a.enc[turned_rows(1)] = t_dot(a.k1[...], a.n1[...]).astype(low)
+    dp_finish_raw(1)
+    turned_grads(3, 0)
+    dp_begin(3, (0,))
+    a.enc[turned_rows(2)] = t_dot(a.v1[...], a.n1[...]).astype(low)
+    a.enc[turned_rows(3)] = t_dot(a.o1[...], a.dh1[...]).astype(low)
+    turned_grads(3, 1)
+    dp_begin(3, (1,))
+    small_step(0)
+    dp_advance(2, 1)
+    dp_advance(1, 2)
+    peer_copy.wait()
 
     def enc_partial(k):
         rows = rows_of(k, seq)
         enc_rows = rows_of(k, enc_len)
-        tall_query, tall_grad = stack(a.q2_peer[rows]), stack(a.do2_peer[rows])
+        pair = a.pair_peer[rows]
+        tall_query, tall_grad = stack(pair[:, :inner]), stack(pair[:, inner:])
         soft = softmax(dot_t(tall_query, a.k2_peer[enc_rows]))
         grad_scores = score_back(soft, dot_t(tall_grad, a.v2_peer[enc_rows]))
         peer_grads = jnp.concatenate(
@@ -745,22 +750,24 @@
         return carry
 
     def enc_keep(j, carry):
+        @pl.when(j == 1)
+        def _():
+            dp_advance(3, 0, (0,))
+
         partial = enc_partial(core * enc_each + j)
         enc_near_copy(j).wait()
         rows = rows_of(j, enc_len)
         a.enc_out[rows] = (partial + a.act[rows].astype(wide)).astype(low)
         return carry
 
-    small_step(0)
     lax.fori_loop(0, enc_each, enc_give, 0)
     small_step(1)
-    dp_advance(2, 2)
-    dp_advance(3, 0)
     lax.fori_loop(0, enc_each, enc_keep, 0)
+    for i in range(2, levels):
+        small_step(i)
+    dp_advance(3, 0, (1,))
     store_enc = load(2, a.enc_out, a.encoded_grad)
     store_enc.start()
-    small_step(2)
-    dp_advance(3, 1)
 
     def phase_five(k):
         for copy in last_copies(k):
@@ -775,10 +782,12 @@
         emit_columns(1, k, my_half(a.dh[k]) + grad_rows)
 
     each_chunk(phase_five)
+    dp_advance(2, 2)
+    dp_advance(3, 1)
+    small_step(levels)
     each_chunk(finish_out)
-    for i in range(3, levels + 2):
-        small_step(i)
     dp_advance(3, 2)
+    small_step(levels + 1)
     dp_finish_raw(2)
     dp_finish_raw(3)
     for k in range(chunks):
@@ -931,9 +940,8 @@
         w_kv=vmem((4 * inner, width), low),
         k2_peer=vmem((enc_rows // 2, inner), low),
         v2_peer=vmem((enc_rows // 2, inner), low),
-        q2_peer=vmem((rows // 2, inner), low),
-        do2_peer=vmem((rows // 2, inner), low),
-        do2=inner_rows,
+        pair=vmem((rows, 2 * inner), low),
+        pair_peer=vmem((rows // 2, 2 * inner), low),
         inner_send=vmem((chunks, 8, half), wide),
         inner_far=vmem((chunks, 8, half), wide),
         enc_out=vmem((enc_rows // 4, width), low),
@@ -951,7 +959,7 @@
         out_far_sem=dma((2, chunks)),
         col_sem=dma((2, 2, chunks)),
         enc_near_sem=dma((2, 2)),
-        peer_sem=dma((2, 2)),
+        peer_sem=dma((2, 1)),
         kv_sem=dma((2, 1)),
         inner_sem=dma((2, chunks)),
         dp_sem=dma((2, 4, 2, levels)),

time: 152 us -> 137 us (0.901)
  Pallas kernels: 149 us -> 135 us
    pallas_call x1, Pallas kernels: 145 us -> 131 us  [per_device(): pl.pallas_call(functools.partial(layer_kernel, cfg, tuple(ins) + tuple(ou...]
where the time goes in v5:
time: 137 us
  Pallas kernels  135 us (99%)
  between operations  1.48 us (1%)
    pallas_call x1, Pallas kernels, per_device(): pl.pallas_call(functools.partial(layer_kernel, cfg, tuple(ins) + tuple(ou...  131 us
    pallas_call x1, Pallas kernels, per_device(): pl.pallas_call(functools.partial(finish_kernel, len(moved), heads, seq),...  4.74 us

profile of v5, /device:TPU:0, one launch (start us, length us, event | category | flops | bytes accessed | tf_op | source)
XLA Modules:
  0.0 136.8 jit_solution(8376322049983036163)
XLA Ops:
  1.3 130.6 %shard_map.323 = (bf16[192,1024]{1,0:T(8,128)(2,1)}, bf16[192,1024]{1,0:T(8,128)(2,1)}, bf16[1024,768]{1,0:T(8,128)(2,1)}, f32[8,768]{1,0:T(8,128)}, f32[96,192]...) custom-call(s32[8]{0:T(128)} %refs_0_.1, ...), custom_call_target="tpu_custom_call" | custom-call | tf_op jit(solution)/shard_map/pallas_call | solution.py:988
  131.9 4.7 %shard_map.324 = (bf16[192,1024]{1,0:T(8,128)(2,1)}, bf16[192,1024]{1,0:T(8,128)(2,1)}, bf16[1024,768]{1,0:T(8,128)(2,1)}, f32[96,192]{1,0:T(8,128)}, f32[96,192...) custom-call(bf16[192,1024]{1,0:T(8,128)(2,1)} %get-tuple-element.48., ...), custom_call_target="tpu_custom_call" | custom-call | tf_op jit(solution)/shard_map/pallas_call | solution.py:1001

commit v6 on v5

--- a/solution.py
+++ b/solution.py
@@ -12,6 +12,9 @@
 HD = 64
 CHUNK_SLOTS = 2
 GELU_ROWS = 32
+MAIN_ROWS = 112
+TAIL_ROWS = 2
+TILE = (16, 128)
 
 norm_epsilon = 1e-06
 masked_score = -1e30
@@ -196,23 +199,58 @@
     def near_copy(p, k):
         return remote(a.part.at[other_rows(k)], a.near.at[k], a.near_sem, (p, k), c_peer)
 
-    def far_copy(p, k):
-        return remote(a.mine.at[k], a.far.at[p % 2, k], a.far_sem, (p, k), y_peer)
+    main_rows = pl.ds(0, MAIN_ROWS)
+
+    def pack_tail(rows):
+        tail = rows[MAIN_ROWS : MAIN_ROWS + TAIL_ROWS]
+        lanes = TILE[1]
+        parts = [
+            tail[r : r + 1, c * lanes : (c + 1) * lanes]
+            for r in range(TAIL_ROWS)
+            for c in range(rows.shape[1] // lanes)
+        ]
+        parts.append(jnp.zeros((TILE[0] - len(parts), lanes), wide))
+        return jnp.concatenate(parts, axis=0).astype(low)
+
+    def unpack_rows(main, tile, columns):
+        tile = tile.astype(wide)
+        each = columns // TILE[1]
+        rest = half_rows - MAIN_ROWS
+        spot = lax.broadcasted_iota(jnp.int32, (rest, columns), 0)
+        block = jnp.zeros((rest, columns), wide)
+        for r in range(TAIL_ROWS):
+            line = jnp.concatenate(
+                [tile[r * each + c : r * each + c + 1] for c in range(each)], axis=1
+            )
+            block = jnp.where(spot == r, jnp.broadcast_to(line, (rest, columns)), block)
+        return jnp.concatenate([main.astype(wide), block], axis=0)
+
+    def far_copies(p, k):
+        return (
+            remote(
+                a.mine.at[k, main_rows], a.far.at[p % 2, k, main_rows], a.far_sem, (p, k), y_peer
+            ),
+            remote(a.tail_send.at[k], a.tail_far.at[p % 2, k], a.tail_sem, (p, k), y_peer),
+        )
 
     def y_send(p, k):
         near_copy(p, k).wait()
-        a.mine[k] = (a.part[own_rows(k)].astype(wide) + a.near[k].astype(wide)).astype(low)
-        far_copy(p, k).start()
+        term = a.part[own_rows(k)].astype(wide) + a.near[k].astype(wide)
+        a.mine[k] = term.astype(low)
+        a.tail_send[k] = pack_tail(term)
+        for copy in far_copies(p, k):
+            copy.start()
 
     def last_copies(k):
         return (
             remote(
-                a.mine.at[k, :, pl.ds(0, half_width)],
-                a.far.at[0, k, :, pl.ds(0, half_width)],
+                a.mine.at[k, main_rows, pl.ds(0, half_width)],
+                a.far.at[0, k, main_rows, pl.ds(0, half_width)],
                 a.far_sem,
                 (4, k),
                 y_peer,
             ),
+            remote(a.tail_send.at[k], a.tail_far.at[0, k], a.tail_sem, (4, k), y_peer),
             remote(a.inner_send.at[k], a.inner_far.at[k], a.inner_sem, (k,), y_peer),
         )
 
@@ -225,15 +263,17 @@
         row_inner = jnp.sum(product * gain_self, axis=-1, keepdims=True)
         add_gain(0, jnp.sum(product * inverse_rms(rows), axis=0, keepdims=True))
         a.inner_send[k] = jnp.broadcast_to(row_inner, (half_rows, half_rows)).T[:8]
-        a.mine[k, :, :half_width] = jnp.where(
-            y == 0, term[:, half_width:], term[:, :half_width]
-        ).astype(low)
+        away = jnp.where(y == 0, term[:, half_width:], term[:, :half_width])
+        a.mine[k, :, :half_width] = away.astype(low)
+        a.tail_send[k] = pack_tail(away)
         for copy in last_copies(k):
             copy.start()
 
     def total(p, k):
-        far_copy(p, k).wait()
-        return a.mine[k].astype(wide) + a.far[p % 2, k].astype(wide)
+        for copy in far_copies(p, k):
+            copy.wait()
+        far = unpack_rows(a.far[p % 2, k, :MAIN_ROWS], a.tail_far[p % 2, k], width)
+        return a.mine[k].astype(wide) + far
 
     def share_copy(p, k, buffer):
         return remote(buffer.at[own_rows(k)], buffer.at[own_rows(k)], a.share_sem, (p, k), c_peer)
@@ -248,20 +288,28 @@
     def phase(p, finish, buffer, compute, extra=None, send=None):
         send = send or functools.partial(y_send, p)
 
-        def body(k):
+        def begin(k):
             finish(k, total(p - 1, k))
             share_copy(p, k, buffer).start()
+
+        def body(k):
+            share_copy(p, k, buffer).wait()
+
+            @pl.when(k + 1 < chunks)
+            def _():
+                begin(k + 1)
+
+            compute(k)
+            near_copy(p, k).start()
 
             @pl.when(k > 0)
             def _():
                 send(k - 1)
 
-            share_copy(p, k, buffer).wait()
-            compute(k)
-            near_copy(p, k).start()
             if extra is not None:
                 extra(k)
 
+        begin(0)
         each_chunk(body)
         send(chunks - 1)
 
@@ -374,8 +422,17 @@
     def out_near_copy(k):
         return remote(a.out_part.at[k % 2, 1 - core], a.out_near.at[k], a.out_near_sem, (k,), c_peer)
 
-    def out_far_copy(k):
-        return remote(a.out_mine.at[k], a.out_far.at[k], a.out_far_sem, (k,), y_peer)
+    def out_far_copies(k):
+        return (
+            remote(
+                a.out_mine.at[k, main_rows],
+                a.out_far.at[k, main_rows],
+                a.out_far_sem,
+                (0, k),
+                y_peer,
+            ),
+            remote(a.out_tail_send.at[k], a.out_tail_far.at[k], a.out_far_sem, (1, k), y_peer),
+        )
 
     def my_half(value):
         return jnp.where(y == 0, value[:, :half_width], value[:, half_width:])
@@ -386,7 +443,9 @@
     def out_gather(k):
         out_near_copy(k).wait()
         term = a.out_part[k % 2, core].astype(wide) + a.out_near[k].astype(wide)
-        a.out_mine[k] = other_half(term).astype(low)
+        away = other_half(term)
+        a.out_mine[k] = away.astype(low)
+        a.out_tail_send[k] = pack_tail(away)
         a.out_keep[k] = my_half(term) + my_half(a.h2[k])
 
     scale = 0.7978845608028654
@@ -444,8 +503,10 @@
         column_copy(which, k).start()
 
     def finish_out(k):
-        out_far_copy(k).wait()
-        value = a.out_keep[k] + a.out_far[k].astype(wide)
+        for copy in out_far_copies(k):
+            copy.wait()
+        far = unpack_rows(a.out_far[k, :MAIN_ROWS], a.out_tail_far[k], half_width)
+        value = a.out_keep[k] + far
         emit_columns(0, k, keep_rows(k * CHUNK_SLOTS + core, value))
 
     orders = (tuple(range(levels)), (1, 0) + tuple(range(2, levels)))
@@ -581,14 +642,17 @@
         a.dh[k] = grad
         a.dh2[own_rows(k)] = grad.astype(low)
 
-    def score_back(soft, grad_soft):
-        weights = soft.astype(wide)
-        row_inner = jnp.sum(weights * grad_soft, axis=-1, keepdims=True)
-        return (weights * (grad_soft - row_inner)).astype(low)
+    def inner_by_head(grad_mixed, mixed):
+        product = grad_mixed.astype(wide) * mixed.astype(wide)
+        return [jnp.sum(product * m, axis=-1, keepdims=True) for m in masks]
+
+    def score_back(soft, grad_soft, row_inner):
+        return (soft.astype(wide) * (grad_soft - row_inner)).astype(low)
 
     def cross_backward(k):
         rows = rows_of(k, chunk_rows)
         grad_mixed = dot_t(a.dh2[rows], a.w_output_cross[...]).astype(low)
+        inners = inner_by_head(grad_mixed, a.o2[rows])
         a.pair[rows, inner:] = grad_mixed
         a.pair[rows, :inner] = a.q2[rows]
         query = a.q2[rows]
@@ -599,7 +663,8 @@
             enc_rows = rows_of(slot, enc_len)
             tall_grad, tall_query = stack(grad_mixed[part]), stack(query[part])
             soft = a.soft2[slot]
-            grad_scores = score_back(soft, dot_t(tall_grad, a.v2[enc_rows]))
+            row_inner = jnp.concatenate([column[part] for column in inners], axis=0)
+            grad_scores = score_back(soft, dot_t(tall_grad, a.v2[enc_rows]), row_inner)
             a.dkv[slot, :inner] = t_dot(tall_query, grad_scores).astype(low)
             a.dkv[slot, inner:] = t_dot(tall_grad, soft).astype(low)
             grads.append(unstack(dot(grad_scores, a.k2[enc_rows])).astype(low))
@@ -664,13 +729,15 @@
     def self_backward(k):
         rows = rows_of(k, chunk_rows)
         grad_mixed = dot_t(a.dh1[rows], a.w_output_self[...]).astype(low)
+        inners = inner_by_head(grad_mixed, a.o1[rows])
         query, keys, values = a.q1[rows], a.k1[rows], a.v1[rows]
         grads = [[], [], []]
         for s in range(CHUNK_SLOTS):
             part = slice(s * seq, (s + 1) * seq)
             tall_grad, tall_query = stack(grad_mixed[part]), stack(query[part])
             soft = a.soft1[k * CHUNK_SLOTS + s]
-            grad_scores = score_back(soft, dot_t(tall_grad, values[part]))
+            row_inner = jnp.concatenate([column[part] for column in inners], axis=0)
+            grad_scores = score_back(soft, dot_t(tall_grad, values[part]), row_inner)
             a.table[...] += grad_scores.astype(wide)
             grads[0].append(unstack(dot(grad_scores, keys[part])).astype(low))
             grads[1].append(t_dot(grad_scores, tall_query).astype(low))
@@ -690,7 +757,8 @@
 
     phase(4, finish_four, a.dh1, self_backward, self_moves, y_send_last)
     for k in range(chunks):
-        out_far_copy(k).start()
+        for copy in out_far_copies(k):
+            copy.start()
     mirror = jnp.where(row_i + col_i == seq - 1, 1.0, 0.0).astype(wide)
     for h in range(heads):
         flipped = exact_dot(a.table[h * seq : (h + 1) * seq, :], mirror)
@@ -731,7 +799,9 @@
         pair = a.pair_peer[rows]
         tall_query, tall_grad = stack(pair[:, :inner]), stack(pair[:, inner:])
         soft = softmax(dot_t(tall_query, a.k2_peer[enc_rows]))
-        grad_scores = score_back(soft, dot_t(tall_grad, a.v2_peer[enc_rows]))
+        grad_soft = dot_t(tall_grad, a.v2_peer[enc_rows])
+        row_inner = jnp.sum(soft.astype(wide) * grad_soft, axis=-1, keepdims=True)
+        grad_scores = score_back(soft, grad_soft, row_inner)
         peer_grads = jnp.concatenate(
             [t_dot(tall_query, grad_scores).astype(low), t_dot(tall_grad, soft).astype(low)], axis=0
         )
@@ -745,15 +815,13 @@
         return remote(a.n3.at[rows], a.act.at[rows], a.enc_near_sem, (j,), c_peer)
 
     def enc_give(j, carry):
+        at_chunk(j, 1, (3, 0, (0,)))
         a.n3[rows_of(j, enc_len)] = enc_partial((1 - core) * enc_each + j).astype(low)
         enc_near_copy(j).start()
         return carry
 
     def enc_keep(j, carry):
-        @pl.when(j == 1)
-        def _():
-            dp_advance(3, 0, (0,))
-
+        at_chunk(j, 1, (3, 1, (0,)))
         partial = enc_partial(core * enc_each + j)
         enc_near_copy(j).wait()
         rows = rows_of(j, enc_len)
@@ -761,11 +829,12 @@
         return carry
 
     lax.fori_loop(0, enc_each, enc_give, 0)
+    dp_advance(3, 0, (1,))
     small_step(1)
     lax.fori_loop(0, enc_each, enc_keep, 0)
+    dp_advance(3, 1, (1,))
     for i in range(2, levels):
         small_step(i)
-    dp_advance(3, 0, (1,))
     store_enc = load(2, a.enc_out, a.encoded_grad)
     store_enc.start()
 
@@ -776,14 +845,14 @@
         inverse = inverse_rms(a.x[own_rows(k)].astype(wide))
         sums = (a.inner_send[k] + a.inner_far[k])[:1]
         row_inner = jnp.broadcast_to(sums, (half_rows, half_rows)).T[:, :1] * (1.0 / width)
-        term = my_half(a.h1[k]) + a.far[0, k, :, :half_width].astype(wide)
+        far = unpack_rows(a.far[0, k, :MAIN_ROWS, :half_width], a.tail_far[0, k], half_width)
+        term = my_half(a.h1[k]) + far
         grad_rows = inverse * my_half(gain_self) * term
         grad_rows -= rows * (inverse * inverse * inverse) * row_inner
         emit_columns(1, k, my_half(a.dh[k]) + grad_rows)
 
     each_chunk(phase_five)
     dp_advance(2, 2)
-    dp_advance(3, 1)
     small_step(levels)
     each_chunk(finish_out)
     dp_advance(3, 2)
@@ -942,6 +1011,10 @@
         v2_peer=vmem((enc_rows // 2, inner), low),
         pair=vmem((rows, 2 * inner), low),
         pair_peer=vmem((rows // 2, 2 * inner), low),
+        tail_send=vmem((chunks, *TILE), low),
+        tail_far=vmem((2, chunks, *TILE), low),
+        out_tail_send=vmem((chunks, *TILE), low),
+        out_tail_far=vmem((chunks, *TILE), low),
         inner_send=vmem((chunks, 8, half), wide),
         inner_far=vmem((chunks, 8, half), wide),
         enc_out=vmem((enc_rows // 4, width), low),
@@ -956,7 +1029,8 @@
         far_sem=dma((2, 5, chunks)),
         share_sem=dma((2, 5, chunks)),
         out_near_sem=dma((2, chunks)),
-        out_far_sem=dma((2, chunks)),
+        out_far_sem=dma((2, 2, chunks)),
+        tail_sem=dma((2, 5, chunks)),
         col_sem=dma((2, 2, chunks)),
         enc_near_sem=dma((2, 2)),
         peer_sem=dma((2, 1)),

time: 137 us -> 129 us (0.942)
  Pallas kernels: 135 us -> 128 us
    pallas_call x1, Pallas kernels: 131 us -> 123 us  [per_device(): pl.pallas_call(functools.partial(layer_kernel, cfg, tuple(ins) + tuple(ou...]
where the time goes in v6:
time: 129 us
  Pallas kernels  128 us (99%)
  between operations  1.48 us (1%)
    pallas_call x1, Pallas kernels, per_device(): pl.pallas_call(functools.partial(layer_kernel, cfg, tuple(ins) + tuple(ou...  123 us
    pallas_call x1, Pallas kernels, per_device(): pl.pallas_call(functools.partial(finish_kernel, len(moved), heads, seq),...  4.74 us

profile of v6, /device:TPU:0, one launch (start us, length us, event | category | flops | bytes accessed | tf_op | source)
XLA Modules:
  0.0 129.0 jit_solution(563754899890754548)
XLA Ops:
  1.3 122.8 %shard_map.323 = (bf16[192,1024]{1,0:T(8,128)(2,1)}, bf16[192,1024]{1,0:T(8,128)(2,1)}, bf16[1024,768]{1,0:T(8,128)(2,1)}, f32[8,768]{1,0:T(8,128)}, f32[96,192]...) custom-call(s32[8]{0:T(128)} %refs_0_.1, ...), custom_call_target="tpu_custom_call" | custom-call | tf_op jit(solution)/shard_map/pallas_call | solution.py:1062
  124.1 4.7 %shard_map.324 = (bf16[192,1024]{1,0:T(8,128)(2,1)}, bf16[192,1024]{1,0:T(8,128)(2,1)}, bf16[1024,768]{1,0:T(8,128)(2,1)}, f32[96,192]{1,0:T(8,128)}, f32[96,192...) custom-call(bf16[192,1024]{1,0:T(8,128)(2,1)} %get-tuple-element.48., ...), custom_call_target="tpu_custom_call" | custom-call | tf_op jit(solution)/shard_map/pallas_call | solution.py:1075

commit v7 on v6

--- a/solution.py
+++ b/solution.py
@@ -333,12 +333,13 @@
         keys = dot_t(normed, a.w_key_self[...]).astype(low)
         values = dot_t(normed, a.w_value_self[...]).astype(low)
         a.q1[rows], a.k1[rows], a.v1[rows] = query, keys, values
+        parts = [slice(s * seq, (s + 1) * seq) for s in range(CHUNK_SLOTS)]
+        scores = [dot_t(stack(query[part]), keys[part]) + a.bias[...] for part in parts]
+        weights = [softmax(score) for score in scores]
         mixed = []
-        for s in range(CHUNK_SLOTS):
-            part = slice(s * seq, (s + 1) * seq)
-            weights = softmax(dot_t(stack(query[part]), keys[part]) + a.bias[...])
-            a.soft1[k * CHUNK_SLOTS + s] = weights
-            mixed.append(unstack(dot(weights, values[part])).astype(low))
+        for s, part in enumerate(parts):
+            a.soft1[k * CHUNK_SLOTS + s] = weights[s]
+            mixed.append(unstack(dot(weights[s], values[part])).astype(low))
         mixed = jnp.concatenate(mixed, axis=0)
         a.o1[rows] = mixed
         a.part[rows] = dot(mixed, a.w_output_self[...]).astype(low)
@@ -392,13 +393,17 @@
         rows = rows_of(k, chunk_rows)
         query = dot_t(a.n2[rows], a.w_query_cross[...]).astype(low)
         a.q2[rows] = query
+        slots_here = [k * CHUNK_SLOTS + s for s in range(CHUNK_SLOTS)]
+        enc_parts = [rows_of(slot, enc_len) for slot in slots_here]
+        scores = [
+            dot_t(stack(query[s * seq : (s + 1) * seq]), a.k2[enc_rows])
+            for s, enc_rows in enumerate(enc_parts)
+        ]
+        weights = [softmax(score) for score in scores]
         mixed = []
-        for s in range(CHUNK_SLOTS):
-            slot = k * CHUNK_SLOTS + s
-            enc_rows = rows_of(slot, enc_len)
-            weights = softmax(dot_t(stack(query[s * seq : (s + 1) * seq]), a.k2[enc_rows]))
-            a.soft2[slot] = weights
-            mixed.append(unstack(dot(weights, a.v2[enc_rows])).astype(low))
+        for s, slot in enumerate(slots_here):
+            a.soft2[slot] = weights[s]
+            mixed.append(unstack(dot(weights[s], a.v2[enc_parts[s]])).astype(low))
         mixed = jnp.concatenate(mixed, axis=0)
         a.o2[rows] = mixed
         a.part[rows] = dot(mixed, a.w_output_cross[...]).astype(low)
@@ -581,16 +586,25 @@
         if not in_kernel:
             raw_copy(block).wait()
 
+    def grad_store(index):
+        if index < 8:
+            source, target = a.held.at[index], getattr(a, "grad_" + Weights._fields[index])
+        else:
+            block, half = divmod(index - 8, 2)
+            source = a.held_wide.at[block, half]
+            target = (a.grad_hidden_out, a.grad_hidden_in)[block]
+            target = target.at[:, pl.ds(half * half_width, half_width)]
+        return pltpu.make_async_copy(source, target, a.grad_sem.at[index])
+
     def emit_grads(block, half, value):
-        columns = slice(half * half_width, (half + 1) * half_width)
-        if block == 0:
-            a.grad_hidden_out[:, columns] = value
-        elif block == 1:
-            a.grad_hidden_in[:, columns] = value
+        if block < 2:
+            a.held_wide[block, half] = value
+            grad_store(8 + 2 * block + half).start()
         else:
             start = (4 if block == 2 else 0) + 2 * half
-            for i, name in enumerate(Weights._fields[start : start + 2]):
-                getattr(a, "grad_" + name)[...] = value[:, i * inner : (i + 1) * inner]
+            for i in range(2):
+                a.held[start + i] = value[:, i * inner : (i + 1) * inner]
+                grad_store(start + i).start()
 
     piece = cfg.piece
     groups = 2
@@ -656,18 +670,27 @@
         a.pair[rows, inner:] = grad_mixed
         a.pair[rows, :inner] = a.q2[rows]
         query = a.q2[rows]
-        grads = []
-        for s in range(CHUNK_SLOTS):
-            slot = k * CHUNK_SLOTS + s
-            part = slice(s * seq, (s + 1) * seq)
-            enc_rows = rows_of(slot, enc_len)
-            tall_grad, tall_query = stack(grad_mixed[part]), stack(query[part])
-            soft = a.soft2[slot]
-            row_inner = jnp.concatenate([column[part] for column in inners], axis=0)
-            grad_scores = score_back(soft, dot_t(tall_grad, a.v2[enc_rows]), row_inner)
-            a.dkv[slot, :inner] = t_dot(tall_query, grad_scores).astype(low)
-            a.dkv[slot, inner:] = t_dot(tall_grad, soft).astype(low)
-            grads.append(unstack(dot(grad_scores, a.k2[enc_rows])).astype(low))
+        parts = [slice(s * seq, (s + 1) * seq) for s in range(CHUNK_SLOTS)]
+        slots_here = [k * CHUNK_SLOTS + s for s in range(CHUNK_SLOTS)]
+        enc_parts = [rows_of(slot, enc_len) for slot in slots_here]
+        tall_grads = [stack(grad_mixed[part]) for part in parts]
+        tall_queries = [stack(query[part]) for part in parts]
+        grad_softs = [dot_t(tall_grads[s], a.v2[enc_parts[s]]) for s in range(CHUNK_SLOTS)]
+        softs = [a.soft2[slot] for slot in slots_here]
+        grad_scores = [
+            score_back(
+                softs[s],
+                grad_softs[s],
+                jnp.concatenate([column[part] for column in inners], axis=0),
+            )
+            for s, part in enumerate(parts)
+        ]
+        grads = [
+            unstack(dot(grad_scores[s], a.k2[enc_parts[s]])).astype(low) for s in range(CHUNK_SLOTS)
+        ]
+        for s, slot in enumerate(slots_here):
+            a.dkv[slot, :inner] = t_dot(tall_queries[s], grad_scores[s]).astype(low)
+            a.dkv[slot, inner:] = t_dot(tall_grads[s], softs[s]).astype(low)
         grads = jnp.concatenate(grads, axis=0)
         a.d_pre[rows, :inner] = grads
         a.part[rows] = dot(grads, a.w_query_cross[...]).astype(low)
@@ -731,17 +754,25 @@
         grad_mixed = dot_t(a.dh1[rows], a.w_output_self[...]).astype(low)
         inners = inner_by_head(grad_mixed, a.o1[rows])
         query, keys, values = a.q1[rows], a.k1[rows], a.v1[rows]
-        grads = [[], [], []]
-        for s in range(CHUNK_SLOTS):
-            part = slice(s * seq, (s + 1) * seq)
-            tall_grad, tall_query = stack(grad_mixed[part]), stack(query[part])
-            soft = a.soft1[k * CHUNK_SLOTS + s]
-            row_inner = jnp.concatenate([column[part] for column in inners], axis=0)
-            grad_scores = score_back(soft, dot_t(tall_grad, values[part]), row_inner)
-            a.table[...] += grad_scores.astype(wide)
-            grads[0].append(unstack(dot(grad_scores, keys[part])).astype(low))
-            grads[1].append(t_dot(grad_scores, tall_query).astype(low))
-            grads[2].append(t_dot(soft, tall_grad).astype(low))
+        parts = [slice(s * seq, (s + 1) * seq) for s in range(CHUNK_SLOTS)]
+        tall_grads = [stack(grad_mixed[part]) for part in parts]
+        tall_queries = [stack(query[part]) for part in parts]
+        softs = [a.soft1[k * CHUNK_SLOTS + s] for s in range(CHUNK_SLOTS)]
+        grad_softs = [dot_t(tall_grads[s], values[part]) for s, part in enumerate(parts)]
+        grad_scores = [
+            score_back(
+                softs[s],
+                grad_softs[s],
+                jnp.concatenate([column[part] for column in inners], axis=0),
+            )
+            for s, part in enumerate(parts)
+        ]
+        a.table[...] += sum(g.astype(wide) for g in grad_scores)
+        grads = [
+            [unstack(dot(grad_scores[s], keys[part])).astype(low) for s, part in enumerate(parts)],
+            [t_dot(g, q).astype(low) for g, q in zip(grad_scores, tall_queries, strict=True)],
+            [t_dot(w, g).astype(low) for w, g in zip(softs, tall_grads, strict=True)],
+        ]
         grads = [jnp.concatenate(g, axis=0) for g in grads]
         a.q1[rows], a.k1[rows], a.v1[rows] = grads
         a.part[rows] = (
@@ -790,7 +821,6 @@
     dp_begin(3, (1,))
     small_step(0)
     dp_advance(2, 1)
-    dp_advance(1, 2)
     peer_copy.wait()
 
     def enc_partial(k):
@@ -815,7 +845,7 @@
         return remote(a.n3.at[rows], a.act.at[rows], a.enc_near_sem, (j,), c_peer)
 
     def enc_give(j, carry):
-        at_chunk(j, 1, (3, 0, (0,)))
+        at_chunk(j, 1, (1, 2), (3, 0, (0,)))
         a.n3[rows_of(j, enc_len)] = enc_partial((1 - core) * enc_each + j).astype(low)
         enc_near_copy(j).start()
         return carry
@@ -825,7 +855,7 @@
         partial = enc_partial(core * enc_each + j)
         enc_near_copy(j).wait()
         rows = rows_of(j, enc_len)
-        a.enc_out[rows] = (partial + a.act[rows].astype(wide)).astype(low)
+        a.d_pre[rows] = (partial + a.act[rows].astype(wide)).astype(low)
         return carry
 
     lax.fori_loop(0, enc_each, enc_give, 0)
@@ -835,7 +865,7 @@
     dp_advance(3, 1, (1,))
     for i in range(2, levels):
         small_step(i)
-    store_enc = load(2, a.enc_out, a.encoded_grad)
+    store_enc = load(2, a.d_pre, a.encoded_grad)
     store_enc.start()
 
     def phase_five(k):
@@ -855,10 +885,6 @@
     dp_advance(2, 2)
     small_step(levels)
     each_chunk(finish_out)
-    dp_advance(3, 2)
-    small_step(levels + 1)
-    dp_finish_raw(2)
-    dp_finish_raw(3)
     for k in range(chunks):
         column_copy(0, k).wait()
         column_copy(1, k).wait()
@@ -868,21 +894,36 @@
     ]
     for store in stores:
         store.start()
+    dp_advance(3, 2)
+    small_step(levels + 1)
+    dp_finish_raw(2)
+    dp_finish_raw(3)
     a.small_out[...] = a.small[...]
     for store in (*stores, store_enc):
         store.wait()
+    if in_kernel:
+        for index in range(12):
+            grad_store(index).wait()
 
 
 def finish_kernel(count, heads, seq, *refs):
     small, buckets = refs[count], refs[count + 1]
     targets, held, sems = refs[count + 2 : 2 * count + 6], refs[2 * count + 6 : -1], refs[-1]
-    copies = [pltpu.make_async_copy(refs[i], held[i], sems.at[i]) for i in range(count)]
+    parts = []
+    for i in range(count):
+        cuts = 1
+        rows = refs[i].shape[0] // cuts
+        parts += [(i, pl.ds(c * rows, rows)) for c in range(cuts)]
+    copies = [
+        pltpu.make_async_copy(refs[i].at[rows], held[i].at[rows], sems.at[n])
+        for n, (i, rows) in enumerate(parts)
+    ]
     for copy in copies:
         copy.start()
-    for i in range(count):
-        copies[i].wait()
-        copies[i] = pltpu.make_async_copy(held[i], targets[i], sems.at[i])
-        copies[i].start()
+    for n, (i, rows) in enumerate(parts):
+        copies[n].wait()
+        copies[n] = pltpu.make_async_copy(held[i].at[rows], targets[i].at[rows], sems.at[n])
+        copies[n].start()
     for i in range(3):
         targets[count + i][...] = small[i, :]
     sums = jnp.concatenate([small[3:4, h * seq : (h + 1) * seq] for h in range(heads)], axis=0)
@@ -955,7 +996,7 @@
     )
     if in_kernel:
         for name, weight in zip(Weights._fields, weights, strict=True):
-            outs["grad_" + name] = (shape((piece, weight.shape[1]), wide), VM)
+            outs["grad_" + name] = (shape((piece, weight.shape[1]), wide), HBM)
     else:
         outs.update(raw_grads=(shape((4, width, width), low), HBM))
     vmem, dma = pltpu.VMEM, pltpu.SemaphoreType.DMA
@@ -1017,7 +1058,6 @@
         out_tail_far=vmem((chunks, *TILE), low),
         inner_send=vmem((chunks, 8, half), wide),
         inner_far=vmem((chunks, 8, half), wide),
-        enc_out=vmem((enc_rows // 4, width), low),
         pre=vmem((CHUNK_SLOTS * seq, hidden), wide),
         bias=vmem((heads * seq, seq), wide),
         table=vmem((heads * seq, seq), wide),
@@ -1041,7 +1081,12 @@
         credit_sem=pltpu.SemaphoreType.REGULAR((2, 2, levels)),
     )
     if in_kernel:
-        scratch.update(term=vmem((2, 2, dp_count, piece, width // 2), low))
+        scratch.update(
+            term=vmem((2, 2, dp_count, piece, width // 2), low),
+            held=vmem((8, piece, inner), wide),
+            held_wide=vmem((2, 2, piece, width // 2), wide),
+            grad_sem=dma((12,)),
+        )
         for level in range(levels):
             count = 1 << (levels - 1 - level)
             scratch["land%d" % level] = vmem((2, 2, count, piece, width // 2), low)
@@ -1083,7 +1128,7 @@
         out_specs=(HBM,) * len(moved) + (VM,) * 4,
         scratch_shapes=[
             *(vmem(results[i].shape, results[i].dtype) for i in moved),
-            dma((len(moved),)),
+            dma((4 * len(moved),)),
         ],
     )(*[results[i] for i in moved], results[3], buckets_row)
     if in_kernel:

time: 129 us -> 129 us (level)
  no operation moved by 1% of the time
where the time goes in v7:
time: 129 us
  Pallas kernels  127 us (98%)
  between operations  1.48 us (1%)
    pallas_call x1, Pallas kernels, per_device(): pl.pallas_call(functools.partial(layer_kernel, cfg, tuple(ins) + tuple(ou...  122 us
    pallas_call x1, Pallas kernels, per_device(): pl.pallas_call(functools.partial(finish_kernel, len(moved), heads, seq),...  5.09 us

profile of v7, /device:TPU:0, one launch (start us, length us, event | category | flops | bytes accessed | tf_op | source)
XLA Modules:
  0.0 128.5 jit_solution(12241065391540146032)
XLA Ops:
  1.3 122.0 %shard_map.323 = (bf16[192,1024]{1,0:T(8,128)(2,1)}, bf16[192,1024]{1,0:T(8,128)(2,1)}, bf16[1024,768]{1,0:T(8,128)(2,1)}, f32[8,768]{1,0:T(8,128)}, f32[96,192]...) custom-call(s32[8]{0:T(128)} %refs_0_.1, ...), custom_call_target="tpu_custom_call" | custom-call | tf_op jit(solution)/shard_map/pallas_call | solution.py:1107
  123.3 5.1 %shard_map.324 = (bf16[192,1024]{1,0:T(8,128)(2,1)}, bf16[192,1024]{1,0:T(8,128)(2,1)}, bf16[1024,768]{1,0:T(8,128)(2,1)}, f32[96,192]{1,0:T(8,128)}, f32[96,192...) custom-call(bf16[192,1024]{1,0:T(8,128)(2,1)} %get-tuple-element.48., ...), custom_call_target="tpu_custom_call" | custom-call | tf_op jit(solution)/shard_map/pallas_call | solution.py:1120

commit v8 on v7

--- a/solution.py
+++ b/solution.py
@@ -851,6 +851,7 @@
         return carry
 
     def enc_keep(j, carry):
+        at_chunk(j, 0, (3, 0, (1,)))
         at_chunk(j, 1, (3, 1, (0,)))
         partial = enc_partial(core * enc_each + j)
         enc_near_copy(j).wait()
@@ -859,7 +860,6 @@
         return carry
 
     lax.fori_loop(0, enc_each, enc_give, 0)
-    dp_advance(3, 0, (1,))
     small_step(1)
     lax.fori_loop(0, enc_each, enc_keep, 0)
     dp_advance(3, 1, (1,))

time: 129 us -> 129 us (level)
  no operation moved by 1% of the time
where the time goes in v8:
time: 129 us
  Pallas kernels  127 us (98%)
  between operations  1.48 us (1%)
    pallas_call x1, Pallas kernels, per_device(): pl.pallas_call(functools.partial(layer_kernel, cfg, tuple(ins) + tuple(ou...  122 us
    pallas_call x1, Pallas kernels, per_device(): pl.pallas_call(functools.partial(finish_kernel, len(moved), heads, seq),...  5.09 us

profile of v8, /device:TPU:0, one launch (start us, length us, event | category | flops | bytes accessed | tf_op | source)
XLA Modules:
  0.0 128.5 jit_solution(3993142291824759750)
XLA Ops:
  1.3 122.0 %shard_map.323 = (bf16[192,1024]{1,0:T(8,128)(2,1)}, bf16[192,1024]{1,0:T(8,128)(2,1)}, bf16[1024,768]{1,0:T(8,128)(2,1)}, f32[8,768]{1,0:T(8,128)}, f32[96,192]...) custom-call(s32[8]{0:T(128)} %refs_0_.1, ...), custom_call_target="tpu_custom_call" | custom-call | tf_op jit(solution)/shard_map/pallas_call | solution.py:1107
  123.3 5.1 %shard_map.324 = (bf16[192,1024]{1,0:T(8,128)(2,1)}, bf16[192,1024]{1,0:T(8,128)(2,1)}, bf16[1024,768]{1,0:T(8,128)(2,1)}, f32[96,192]{1,0:T(8,128)}, f32[96,192...) custom-call(bf16[192,1024]{1,0:T(8,128)(2,1)} %get-tuple-element.48., ...), custom_call_target="tpu_custom_call" | custom-call | tf_op jit(solution)/shard_map/pallas_call | solution.py:1120
